TPU v7x, 256 devices: a whole 4x4x8 slice. The times are simulated.
256 devices in a mesh: dp: 64 (over y, z, core), tensor: 4 (over x).
Axes of the slice: x: 4, y: 4, z: 8, core: 2. Of those that a mesh axis runs over, the one named last changes fastest.
Arguments:
- tokens: bfloat16 [16384, 4096], P('dp', 'tensor'), may hold values from -6 to 6
- x_weight: bfloat16 [4096, 8192], P('dp', 'tensor'), may hold values from -0.09375 to 0.09375
- bc_weight: bfloat16 [4096, 512], P('dp', 'tensor'), may hold values from -0.0234375 to 0.0234375
- step_weight: bfloat16 [4096, 128], P('dp', 'tensor'), may hold values from -0.09375 to 0.09375
- step_bias: float32 [128], P('tensor'), may hold values from -2 to 1
- decay_log: float32 [128], P('tensor'), may hold values from -6 to -1.5
- skip_gain: float32 [128], P('tensor'), may hold values from 0.5 to 1.5
- queries: bfloat16 [16384, 4096], P('dp', 'tensor'), may hold values from -12 to 12
- new_keyvals: bfloat16 [16384, 1024], P('dp', 'tensor'), may hold values from -6 to 6
- page_pool: bfloat16 [6144, 128, 1024], P('dp', None, 'tensor'), may hold values from -6 to 6
- page_table: int32 [128, 48], P('dp'), may hold values from 0 to 6143, as said below
- prefix_pages: int32 [128], P('dp'), may hold values from 16 to 32
- new_counts: int32 [128], P('dp'), may hold values from 64 to 128
Outputs:
- mamba_out: bfloat16 [16384, 8192], P('dp', 'tensor')
- attention_out: bfloat16 [16384, 4096], P('dp', 'tensor')
Inputs may be any that keep to these rules, and one draw needn't show every extreme that they name: `page_table`: row g lists sequence g's 16 state pages, then its 32 key-value page slots; every pool page is named exactly once; page id // 96 is its pool owner; the rows of one owner's 2 sequences name at most 2 pages of any one pool owner, of which at most 1 are state pages and at most 1 key-value pages.
All inputs are finite; a program needn't handle non-finite values.
Results may differ from a plain program's by a relative error of at most 0.0061.
Values may be sent and summed in bfloat16 or wider, within the bound.
No kernel may reach another device: no remote copies, remote signals or barrier semaphores. Data moves between devices by JAX's collectives and lax.ppermute only.
A program may use at most 192 MiB of HBM per device.

v0:
```python
import math

import jax
import jax.numpy as jnp
from jax import lax
from jax.sharding import PartitionSpec as P

HP = 64
NST = 256
HD = 128
PAGE = 128
SP = 16


def pages_to_state(state_pages, heads):
    blocks = state_pages.shape[2] // (2 * HD)
    shaped = state_pages.reshape(SP, PAGE, blocks, 2 * HD).transpose(2, 0, 1, 3)
    return shaped.reshape(heads, HP, NST).astype(jnp.float32)


def scan_block(inner, b_values, c_values, step, rate, skip_gain, state, live):
    length = inner.shape[0]
    heads = step.shape[1]
    values = inner.reshape(length, heads, HP)
    decay_sum = jnp.cumsum(-step * rate[None, :], axis=0)
    order = jnp.arange(length)
    causal = order[:, None] >= order[None, :]
    gaps = jnp.where(causal[:, :, None], decay_sum[:, None, :] - decay_sum[None, :, :], -jnp.inf)
    intersection = jnp.dot(c_values, b_values.T, preferred_element_type=jnp.float32)
    mixing = jnp.exp(gaps) * intersection[:, :, None] * step[None, :, :]
    values_wide = values.astype(jnp.float32)
    local = jnp.einsum("jih,ihp->jhp", mixing, values_wide, precision=lax.Precision.HIGHEST)
    carried = jnp.einsum(
        "hpn,jn->jhp", state, c_values.astype(jnp.float32), precision=lax.Precision.HIGHEST
    )
    carried = carried * jnp.exp(decay_sum)[:, :, None]
    output = (local + carried + skip_gain[None, :, None] * values_wide) * live[:, None, None]
    return output.reshape(length, heads * HP).astype(jnp.bfloat16)


def attend(queries, fresh, kv_pages, prefix, live):
    length = queries.shape[0]
    kv_heads = fresh.shape[1] // (2 * HD)
    cached = kv_pages.reshape(-1, kv_heads, 2 * HD)
    combined = jnp.concatenate([cached, fresh.reshape(length, kv_heads, 2 * HD)], axis=0)
    keys = combined[:, :, :HD]
    values = combined[:, :, HD:]
    grouped = queries.reshape(length, kv_heads, -1, HD)
    scores = jnp.einsum("jgrd,kgd->grjk", grouped, keys, preferred_element_type=jnp.float32)
    scores = scores * (1.0 / math.sqrt(HD))
    cached_len = cached.shape[0]
    order = jnp.arange(length)
    slots = jnp.arange(cached_len) // PAGE
    seen = jnp.broadcast_to((slots < prefix)[None, :], (length, cached_len))
    allowed = jnp.concatenate([seen, order[None, :] <= order[:, None]], axis=1)
    scores = jnp.where(allowed[None, None], scores, -jnp.inf)
    top = jnp.max(scores, axis=-1, keepdims=True)
    weights = jnp.exp(scores - top)
    weights = (weights / jnp.sum(weights, axis=-1, keepdims=True)).astype(jnp.bfloat16)
    mixed = jnp.einsum("grjk,kgd->jgrd", weights, values, preferred_element_type=jnp.float32)
    mixed = mixed * live[:, None, None, None]
    return mixed.reshape(length, -1).astype(jnp.bfloat16)


def pair_ranks(sources):
    count = sources.shape[-1]
    place = jnp.arange(count)
    earlier = place[None, :] < place[:, None]
    same = (sources[..., :, None] == sources[..., None, :]) & earlier
    return jnp.sum(same.astype(jnp.int32), axis=-1)


def send_pages(page_pool, requests, position, capacity):
    owners = requests.shape[0]
    pool_size = page_pool.shape[0]
    sources = requests // pool_size
    ranks = pair_ranks(sources)
    targets = jnp.arange(owners)[:, None] * capacity + ranks
    targets = jnp.where(sources == position, targets, owners * capacity)
    picks = jnp.zeros((owners * capacity + 1,), jnp.int32)
    picks = picks.at[targets.reshape(-1)].set((requests % pool_size).reshape(-1))
    outgoing = page_pool[picks[: owners * capacity]]
    return outgoing.reshape(owners, capacity, page_pool.shape[1], page_pool.shape[2])


def take_pages(incoming, own_requests, pool_size, capacity):
    own_sources = own_requests // pool_size
    own_ranks = pair_ranks(own_sources)
    flat_incoming = incoming.reshape(-1, incoming.shape[2], incoming.shape[3])
    return flat_incoming[own_sources * capacity + own_ranks]


def run_mamba(inner, b_values, c_values, step_all, rate, skip_gain, state_pages, new_counts):
    seq_dev = state_pages.shape[0]
    length = inner.shape[0] // seq_dev
    heads = step_all.shape[1]
    order = jnp.arange(length)
    outputs = []
    for member in range(seq_dev):
        lower = member * length
        upper = lower + length
        live = (order < new_counts[member]).astype(jnp.float32)
        step = step_all[lower:upper] * live[:, None]
        state = pages_to_state(state_pages[member], heads)
        outputs.append(
            scan_block(
                inner[lower:upper],
                b_values[lower:upper],
                c_values[lower:upper],
                step,
                rate,
                skip_gain,
                state,
                live,
            )
        )
    return jnp.concatenate(outputs, axis=0)


def run_attention(queries, new_keyvals, cache_pages, prefix_pages, new_counts):
    seq_dev = cache_pages.shape[0]
    length = queries.shape[0] // seq_dev
    order = jnp.arange(length)
    outputs = []
    for member in range(seq_dev):
        lower = member * length
        upper = lower + length
        live = (order < new_counts[member]).astype(jnp.float32)
        outputs.append(
            attend(
                queries[lower:upper],
                new_keyvals[lower:upper],
                cache_pages[member],
                prefix_pages[member],
                live,
            )
        )
    return jnp.concatenate(outputs, axis=0)


def body(
    tokens,
    x_weight,
    bc_weight,
    step_weight,
    step_bias,
    decay_log,
    skip_gain,
    queries,
    new_keyvals,
    page_pool,
    page_table,
    prefix_pages,
    new_counts,
):
    owners = lax.axis_size("dp")
    position = lax.axis_index("dp")
    seq_dev = page_table.shape[0]
    width = page_table.shape[1]
    pool_size = page_pool.shape[0]
    page_rows = page_pool.shape[1]
    page_cols = page_pool.shape[2]
    whole = lax.all_gather(tokens, "tensor", axis=1, tiled=True)
    gathered = (
        lax.all_gather(x_weight, "dp", axis=0, tiled=True),
        lax.all_gather(bc_weight, "dp", axis=0, tiled=True),
        lax.all_gather(step_weight, "dp", axis=0, tiled=True),
    )
    inner_sum = jnp.dot(whole, gathered[0], preferred_element_type=jnp.float32)
    column_sum = jnp.dot(whole, gathered[1], preferred_element_type=jnp.float32)
    step_raw = jnp.dot(whole, gathered[2], preferred_element_type=jnp.float32)
    inner = jax.nn.silu(inner_sum).astype(jnp.bfloat16)
    column_values = lax.all_gather(column_sum.astype(jnp.bfloat16), "tensor", axis=1, tiled=True)
    b_values = column_values[:, :NST]
    c_values = column_values[:, NST:]
    step_all = jax.nn.softplus(step_raw + step_bias[None, :])
    rate = jnp.exp(decay_log)
    all_tables = lax.all_gather(page_table, "dp", axis=0, tiled=True)
    requests = all_tables.reshape(owners, seq_dev, width)
    capacity = (seq_dev * width + owners - 1) // owners
    outgoing = send_pages(page_pool, requests.reshape(owners, seq_dev * width), position, capacity)
    incoming = lax.all_to_all(outgoing, "dp", split_axis=0, concat_axis=0, tiled=True)
    mine = take_pages(incoming, page_table.reshape(-1), pool_size, capacity)
    mine = mine.reshape(seq_dev, width, page_rows, page_cols)
    mamba_out = run_mamba(
        inner, b_values, c_values, step_all, rate, skip_gain, mine[:, :SP], new_counts
    )
    attention_out = run_attention(queries, new_keyvals, mine[:, SP:], prefix_pages, new_counts)
    return (mamba_out, attention_out)


def solution(mesh):
    placed = (
        P("dp", "tensor"),
        P("dp", "tensor"),
        P("dp", "tensor"),
        P("dp", "tensor"),
        P("tensor"),
        P("tensor"),
        P("tensor"),
        P("dp", "tensor"),
        P("dp", "tensor"),
        P("dp", None, "tensor"),
        P("dp", None),
        P("dp"),
        P("dp"),
    )
    return jax.shard_map(
        body,
        mesh=mesh,
        in_specs=placed,
        out_specs=(P("dp", "tensor"), P("dp", "tensor")),
        check_vma=False,
    )
```

profile of v0, /device:TPU:1, one launch (start us, length us, event | category | flops | bytes accessed | tf_op | source)
XLA Modules:
  0.0 496.1 jit_solution(16930950271847770097)
XLA Ops:
  7.2 0.7 all-gather.6.cloned.1.call-update
  7.9 0.7 all-gather.10.cloned.1.call-update
  8.7 0.7 all-gather.8.cloned.1.call-update
  9.4 48.4 %all-gather.1 = s32[64,2,48]{2,1,0:T(2,128)S(1)} all-gather(s32[1,2,48]{2,1,0:T(2,128)} %bitcast.176), channel_id=1, replica_groups=mesh['dp'=64,'tensor'=4] {'dp'}, dimensions={0}, use_global_device_ids=true | all-gather | bytes 24960 | tf_op jit(solution)/shard_map/all_gather | solution.py:178
  58.8 2.3 convert_reduce_fusion
  61.5 23.0 %scatter_custom_fusion = s32[129]{0:T(256)S(1)} fusion(s32[6144]{0:T(1024)S(1)} %bitcast.174, s32[6144]{0:T(1024)S(1)} %add_select_fusion.1, s32[]{:T(128)} %constant.66.clone.1), kind=kCustom, calls=%fused_computation.136 | custom fusion | bytes 520 | tf_op jit(solution)/shard_map/scatter | solution.py:81
  84.5 9.3 %gather_fusion = bf16[128,128,256]{2,1,0:T(8,128)(2,1)} fusion(bf16[96,128,256]{2,1,0:T(8,128)(2,1)} %param.22, s32[1024]{0:T(1024)S(1)} %pad_clamp_fusion.1), kind=kCustom, calls=%fused_computation | custom fusion | bytes 16777728 | tf_op jit(solution)/shard_map/gather | solution.py:82
  93.8 6.8 %all-to-all-start = ((bf16[64,2,128,256]{3,2,1,0:T(8,128)(2,1)}), bf16[64,2,128,256]{3,2,1,0:T(8,128)(2,1)}, u32[]{:S(2)}, u32[]{:S(2)}) async-start(bf16[64,2,128,256]{3,2,1,0:T(8,128)(2,1)} %bitcast.155), calls=%async_computation | async-start | bytes 16777216 | tf_op jit(solution)/shard_map/all_to_all | solution.py:182
  101.0 0.6 fusion.112
  101.6 0.7 fusion.91
  102.3 0.7 fusion.90
  103.0 274.9 %all-gather = bf16[64,64,32]{1,2,0:T(8,128)(2,1)S(1)} all-gather(bf16[1,64,32]{1,2,0:T(8,128)(2,1)S(1)} %bitcast.175), channel_id=1, replica_groups=mesh['dp'=64,'tensor'=4] {'dp'}, dimensions={0}, use_global_device_ids=true | all-gather | bytes 266240 | tf_op jit(solution)/shard_map/all_gather | solution.py:167
  378.6 0.8 copy.124
  379.5 0.8 copy.125
  380.3 0.6 fusion.113
  380.9 1.3 compare_convert_fusion
  382.4 0.6 pad_clamp_fusion
  383.0 0.6 iota_compare_fusion.1
  383.6 0.7 slice_bitcast_fusion.1
  384.3 4.3 pad_add_fusion.1
  388.6 2.5 compare_select_fusion.2
  391.1 0.6 negate_multiply_fusion.1
  392.0 0.7 copy.92
  393.0 0.7 copy.101
  393.9 1.9 convolution_convert_fusion
  395.8 9.9 %all_gather.22 = bf16[256,512]{1,0:T(8,128)(2,1)S(1)} all-gather(bf16[256,128]{1,0:T(8,128)(2,1)S(1)} %convolution_convert_fusion), channel_id=1, replica_groups=mesh['dp'=64,'tensor'=4] {'tensor'}, dimensions={1}, use_global_device_ids=true | all-gather | bytes 327680 | tf_op jit(solution)/shard_map/all_gather | solution.py:173
  405.8 0.8 fusion.80
  406.6 9.4 %gather_fusion.1 = bf16[96,128,256]{2,1,0:T(8,128)(2,1)} fusion(bf16[128,128,256]{2,1,0:T(8,128)(2,1)} %bitcast.10, s32[1024]{0:T(1024)} %pad_clamp_fusion), kind=kCustom, calls=%fused_computation.1 | custom fusion | bytes 12583296 | tf_op jit(solution)/shard_map/gather | solution.py:90
  416.1 2.5 fusion.108
  418.7 2.4 fusion.3
  421.2 8.3 %fusion.2 = (f32[8,128]{1,0:T(8,128)S(1)}, f32[4224,128,8]{1,0,2:T(8,128)}) fusion(pred[128,4224]{0,1:T(8,128)(4,1)S(1)} %get-tuple-element.20, bf16[128,8,128]{0,2,1:T(8,128)(2,1)S(1)} %bitcast.170, bf16[128,1,256]{2,0,1:T(8,128)(2,1)S(1)} %copy-done.9, bf16[4096,1,256]{2,0,1:T(8,128)(2,1)S(1)} %bitcast.168), kind=kOutput, calls=%fused_computation.11 | convolution fusion | flops 1122434048 | bytes 20271104 | tf_op jit(solution)/shard_map/jgrd,kgd->grjk/dot_general | solution.py:49
  429.5 2.8 copy-done
  432.2 10.6 %fusion = (f32[8,128]{1,0:T(8,128)S(1)}, f32[8,128]{1,0:T(8,128)}) fusion(f32[4224,128,8]{1,0,2:T(8,128)} %get-tuple-element.29, f32[8,128]{1,0:T(8,128)S(1)} %get-tuple-element.28, pred[128,4224]{0,1:T(8,128)(4,1)S(1)} %get-tuple-element.20, f32[8,128]{1,0:T(8,128)S(1)} %get-tuple-element.26, f32[4224,128,8]{1,0,2:T(8,128)S(1)} %get-tuple-element.27, ...), kind=kLoop, calls=%fused_computation.9 | loop fusion | flops 34600960 | bytes 35700736 | tf_op jit(solution)/shard_map/reduce_sum | solution.py:59
  442.8 9.8 %fusion.46 = bf16[1,128,8,128]{3,1,2,0:T(8,128)(2,1)} fusion(f32[8,128]{1,0:T(8,128)S(1)} %get-tuple-element.32, f32[8,128]{1,0:T(8,128)S(1)} %get-tuple-element.28, f32[4224,128,8]{1,0,2:T(8,128)} %get-tuple-element.29, pred[128,4224]{0,1:T(8,128)(4,1)S(1)} %get-tuple-element.20, bf16[4096,1,256]{2,0,1:T(8,128)(2,1)S(1)} %bitcast.169, ...), kind=kOutput, calls=%fused_computation.53 | convolution fusion | flops 1131347968 | bytes 20275712 | tf_op jit(solution)/shard_map/grjk,kgd->jgrd/dot_general | solution.py:60
  452.7 1.1 copy.114
  453.7 9.9 %fusion.49 = bf16[1,128,8,128]{3,1,2,0:T(8,128)(2,1)} fusion(f32[8,128]{1,0:T(8,128)} %get-tuple-element.33, f32[8,128]{1,0:T(8,128)} %copy-done.20, f32[4224,128,8]{1,0,2:T(8,128)} %copy-done, pred[128,4224]{0,1:T(8,128)(4,1)S(1)} %get-tuple-element.21, bf16[4096,1,256]{2,0,1:T(8,128)(2,1)} %bitcast.167, bf16[128,1,256]{2,0,1:T(8,128)(2,1)} %get-tuple-element.15, ...), kind=kOutput, calls=%fused_computation.54 | convolution fusion | flops 1131347968 | bytes 20275712 | tf_op jit(solution)/shard_map/grjk,kgd->jgrd/dot_general | solution.py:60
  463.6 1.1 copy.115
  464.7 0.8 pad_maximum_fusion.3
  465.5 2.7 fusion.109
  468.2 8.7 %multiply_convert_fusion = bf16[256,2048]{1,0:T(8,128)(2,1)S(1)} fusion(bf16[256,4096]{1,0:T(8,128)(2,1)S(1)} %copy-done.1, bf16[4096,2048]{1,0:T(8,128)(2,1)} %all-gather.8.cloned.1.call-done), kind=kOutput, calls=%fused_computation.36 | convolution fusion | flops 4297588736 | bytes 19922944 | tf_op jit(solution)/shard_map/dot_general | solution.py:169
  476.9 0.9 fusion.110
  478.1 1.4 copy.99
  479.6 3.2 fusion.20
  482.9 1.3 fusion.33
  484.1 1.3 copy.104
  485.4 2.4 fusion.23
  487.8 0.5 fusion.32
  488.5 1.0 pad_maximum_fusion.2
  (106 shorter events, 4.0 us)
Async XLA Ops:
  7.2 381.5 %all-gather.6.cloned.1.call-start = ((), (), s32[]{:S(2)}) async-start(), calls=%async_computation.1 | async-start | bytes 2621440 | tf_op jit(solution)/shard_map/all_gather | solution.py:163
  7.9 385.9 %all-gather.10.cloned.1.call-start = ((), (), s32[]{:S(2)}) async-start(), calls=%async_computation.3 | async-start | bytes 1064960 | tf_op jit(solution)/shard_map/all_gather | solution.py:166
  8.6 459.6 %all-gather.8.cloned.1.call-start = ((), (), s32[]{:S(2)}) async-start(), calls=%async_computation.2 | async-start | bytes 17039360 | tf_op jit(solution)/shard_map/all_gather | solution.py:165
  93.8 6.8 %copy-start.21 = (s32[2,48]{1,0:T(2,128)S(1)}, s32[2,48]{1,0:T(2,128)}, u32[]{:S(2)}) copy-start(s32[2,48]{1,0:T(2,128)} %param.23) | copy-start | bytes 1156
  93.8 7.2 %copy-start.27 = (f32[32]{0:T(128)S(1)}, f32[32]{0:T(128)}, u32[]{:S(2)}) copy-start(f32[32]{0:T(128)} %param.18) | copy-start | bytes 388
  93.8 7.2 %copy-start.24 = (s32[2]{0:T(128)S(1)}, s32[2]{0:T(128)}, u32[]{:S(2)}) copy-start(s32[2]{0:T(128)} %param.24) | copy-start | bytes 28
  93.8 9.2 %copy-start.14 = (bf16[64,32]{0,1:T(8,128)(2,1)S(1)}, bf16[64,32]{0,1:T(8,128)(2,1)}, u32[]{:S(2)}) copy-start(bf16[64,32]{0,1:T(8,128)(2,1)} %param.16) | copy-start | bytes 12292
  93.8 312.8 %all-to-all-start = ((bf16[64,2,128,256]{3,2,1,0:T(8,128)(2,1)}), bf16[64,2,128,256]{3,2,1,0:T(8,128)(2,1)}, u32[]{:S(2)}, u32[]{:S(2)}) async-start(bf16[64,2,128,256]{3,2,1,0:T(8,128)(2,1)} %bitcast.155), calls=%async_computation | async-start | bytes 16777216 | tf_op jit(solution)/shard_map/all_to_all | solution.py:182
  100.6 278.0 %copy-start.4 = (bf16[256,1024]{1,0:T(8,128)(2,1)S(1)}, bf16[256,1024]{1,0:T(8,128)(2,1)}, u32[]{:S(2)}) copy-start(bf16[256,1024]{1,0:T(8,128)(2,1)} %param.20) | copy-start | bytes 1572868
  102.9 277.4 %copy-start.25 = (s32[2]{0:T(128)S(1)}, s32[2]{0:T(128)}, u32[]{:S(2)}) copy-start(s32[2]{0:T(128)} %param.25) | copy-start | bytes 28
  103.0 280.7 %copy-start.7 = (bf16[256,256]{1,0:T(8,128)(2,1)S(1)}, bf16[256,256]{1,0:T(8,128)(2,1)}, u32[]{:S(2)}) copy-start(bf16[256,256]{1,0:T(8,128)(2,1)} %param.21) | copy-start | bytes 393220
  378.1 10.5 %copy-start.26 = (f32[32]{0:T(128)S(1)}, f32[32]{0:T(128)}, u32[]{:S(2)}) copy-start(f32[32]{0:T(128)} %param.17) | copy-start | bytes 388
  382.2 10.5 %copy-start.15 = (f32[128]{0:T(128)}, f32[128]{0:T(128)S(1)}, u32[]{:S(2)}) copy-start(f32[128]{0:T(128)S(1)} %get-tuple-element.30) | copy-start | bytes 1540
  382.2 10.5 %copy-start.17 = (f32[128]{0:T(128)}, f32[128]{0:T(128)S(1)}, u32[]{:S(2)}) copy-start(f32[128]{0:T(128)S(1)} %get-tuple-element.31) | copy-start | bytes 1540
  388.6 5.2 %copy-start.1 = (bf16[256,4096]{1,0:T(8,128)(2,1)S(1)}, bf16[256,4096]{1,0:T(8,128)(2,1)}, u32[]{:S(2)}) copy-start(bf16[256,4096]{1,0:T(8,128)(2,1)} %all-gather.6.cloned.1.call-done) | copy-start | bytes 6291460
  416.1 2.6 copy-start.6
  416.1 2.6 copy-start.8
  418.6 2.5 copy-start.3
  418.7 2.5 copy-start.5
  418.7 2.5 copy-start.9
  421.1 11.1 %copy-start = (f32[4224,128,8]{1,0,2:T(8,128)}, f32[4224,128,8]{1,0,2:T(8,128)S(1)}, u32[]{:S(2)}) copy-start(f32[4224,128,8]{1,0,2:T(8,128)S(1)} %get-tuple-element.27) | copy-start | bytes 51904516
  421.1 11.1 %copy-start.20 = (f32[8,128]{1,0:T(8,128)}, f32[8,128]{1,0:T(8,128)S(1)}, u32[]{:S(2)}) copy-start(f32[8,128]{1,0:T(8,128)S(1)} %get-tuple-element.26) | copy-start | bytes 12292
  432.2 10.6 %copy-start.18 = (f32[128]{0:T(128)S(1)}, f32[128]{0:T(128)}, u32[]{:S(2)}) copy-start(f32[128]{0:T(128)} %copy-done.17) | copy-start | bytes 1540
  476.9 2.6 copy-start.10
  476.9 2.6 copy-start.12
  478.1 4.7 copy-start.2
  479.5 3.3 copy-start.19
  479.5 3.3 copy-start.22
  482.8 2.6 copy-start.11
  482.8 2.6 copy-start.13
  484.1 3.7 copy-start.16
  484.1 3.7 copy-start.23
Sparse Core Ops, SparseCore 0:
  9.8 37.1 all-gather.5
  49.8 82.1 all-gather.9
  134.8 198.5 all-gather.7
where the time goes:
time: 498 us; the launch traced here: 496 us
  blocking collectives  333 us (67%)
  local copies, waits for them, and re-layouts  63.1 us (13%)
  matrix products  51.8 us (10%)
  other arithmetic  24.5 us (5%)
  between operations  14.4 us (3%)
  starting transfers between devices  6.93 us (1%)
    all_gather x1, blocking collectives, body(): lax.all_gather(step_weight, 'dp', axis=0, tiled=True)  275 us
    all_gather x1, blocking collectives, body(): all_tables = lax.all_gather(page_table, 'dp', axis=0, tiled=True)  48.4 us
    scatter x1, local copies, waits for them, and re-layouts, send_pages(): picks.at[targets.reshape(-1)].set((requests % pool_size).reshape(-1))  23 us
    dot_general x2, matrix products, attend(): jnp.einsum('grjk,kgd->jgrd', weights, values, preferred_element_type=jnp....  19.7 us
    dot_general x2, matrix products, attend(): jnp.einsum('jgrd,kgd->grjk', grouped, keys, preferred_element_type=jnp.fl...  10.7 us
    reduce_sum x1, other arithmetic, attend(): jnp.sum(weights, axis=-1, keepdims=True)  10.6 us
  transfers between devices with their start and end apart: 4, of which 0 were waited for; matrix products, arithmetic and copies ran while one was open for 23% of the time, Pallas kernels for 0%

commit v1 on v0

v1 whole, which is shorter than its diff:
```python
import math

import jax
import jax.numpy as jnp
from jax import lax
from jax.experimental import pallas as pl
from jax.experimental.pallas import tpu as pltpu
from jax.sharding import PartitionSpec as P

HP = 64
NST = 256
HD = 128
PAGE = 128
SP = 16
NY = 4
NZ = 8
NX = 4
VMEM = 48 * 1024 * 1024
ANY = pl.BlockSpec(memory_space=pl.ANY)
WHOLE = pl.BlockSpec(memory_space=pltpu.VMEM)
SCALARS = pl.BlockSpec(memory_space=pltpu.SMEM)


def shift_pairs(axis, by):
    pairs = []
    for y in range(NY):
        for z in range(NZ):
            for core in range(2):
                place = {"y": y, "z": z, "core": core}
                size = {"y": NY, "z": NZ, "core": 2}[axis]
                goal = dict(place)
                goal[axis] = (place[axis] + by) % size
                pairs.append(
                    ((y * NZ + z) * 2 + core, (goal["y"] * NZ + goal["z"]) * 2 + goal["core"])
                )
    return pairs


def move(array, axis, by):
    if axis == "x":
        return lax.ppermute(array, "tensor", [(i, (i + by) % NX) for i in range(NX)])
    return lax.ppermute(array, "dp", shift_pairs(axis, by))


def pack_kernel(picks, pool, out, sems):
    owners = out.shape[0]

    def start(d, carry):
        @pl.when(picks[d] >= 0)
        def _():
            pltpu.make_async_copy(pool.at[picks[d]], out.at[d], sems.at[d]).start()

        return carry

    def finish(d, carry):
        @pl.when(picks[d] >= 0)
        def _():
            pltpu.make_async_copy(pool.at[picks[d]], out.at[d], sems.at[d]).wait()

        return carry

    lax.fori_loop(0, owners, start, 0)
    lax.fori_loop(0, owners, finish, 0)


def pack_pages(picks, pool):
    owners = picks.shape[0]
    page = pool.shape[1:]
    return pl.pallas_call(
        pack_kernel,
        out_shape=jax.ShapeDtypeStruct((owners,) + page, pool.dtype),
        in_specs=[SCALARS, ANY],
        out_specs=ANY,
        scratch_shapes=[pltpu.SemaphoreType.DMA((owners,))],
        cost_estimate=pl.CostEstimate(
            flops=0, bytes_accessed=2 * owners * page[0] * page[1] * 2, transcendentals=0
        ),
        name="pack_pages",
    )(picks, pool)


def project_kernel(count_w, count_t, *refs):
    w_offs, t_rows, t_cols = refs[:3]
    w_pieces = refs[3 : 3 + count_w]
    t_pieces = refs[3 + count_w : 3 + count_w + count_t]
    mine, theirs, mine_extra, theirs_extra, w_all, t_all, sems = refs[3 + count_w + count_t :]
    copies = []
    for i, piece in enumerate(w_pieces):
        rows = piece.shape[0]
        at = pl.multiple_of(w_offs[i], 32)
        copies.append(
            pltpu.make_async_copy(piece, w_all.at[pl.ds(at, rows), :], sems.at[i])
        )
    for i, piece in enumerate(t_pieces):
        rows, cols = piece.shape
        at = pl.multiple_of(t_rows[i], 128)
        along = pl.multiple_of(t_cols[i], 1024)
        copies.append(
            pltpu.make_async_copy(
                piece, t_all.at[pl.ds(at, rows), pl.ds(along, cols)], sems.at[count_w + i]
            )
        )
    for copy in copies:
        copy.start()
    for copy in copies:
        copy.wait()
    half = mine.shape[0]
    wide = 256

    def tile(n, carry):
        at = pl.multiple_of(n * wide, wide)
        total = jnp.dot(
            t_all[...], w_all[:, pl.ds(at, wide)], preferred_element_type=jnp.float32
        )
        value = (total / (1.0 + jnp.exp(-total))).astype(jnp.bfloat16)
        mine[:, pl.ds(at, wide)] = value[:half]
        theirs[:, pl.ds(at, wide)] = value[half:]
        return carry

    main = mine.shape[1]
    lax.fori_loop(0, main // wide, tile, 0)
    extra = jnp.dot(t_all[...], w_all[:, main:], preferred_element_type=jnp.float32)
    mine_extra[...] = extra[:half]
    theirs_extra[...] = extra[half:]


def project(w_pieces, w_offs, t_pieces, t_rows, t_cols, half_rows, main, extra, depth):
    count_w, count_t = len(w_pieces), len(t_pieces)
    return pl.pallas_call(
        lambda *refs: project_kernel(count_w, count_t, *refs),
        out_shape=(
            jax.ShapeDtypeStruct((half_rows, main), jnp.bfloat16),
            jax.ShapeDtypeStruct((half_rows, main), jnp.bfloat16),
            jax.ShapeDtypeStruct((half_rows, extra), jnp.float32),
            jax.ShapeDtypeStruct((half_rows, extra), jnp.float32),
        ),
        in_specs=[SCALARS] * 3 + [ANY] * (count_w + count_t),
        out_specs=(WHOLE,) * 4,
        scratch_shapes=[
            pltpu.VMEM((depth, main + extra), jnp.bfloat16),
            pltpu.VMEM((2 * half_rows, depth), jnp.bfloat16),
            pltpu.SemaphoreType.DMA((count_w + count_t,)),
        ],
        compiler_params=pltpu.CompilerParams(vmem_limit_bytes=VMEM),
        cost_estimate=pl.CostEstimate(
            flops=4 * half_rows * depth * (main + extra),
            bytes_accessed=2 * depth * (main + extra + 2 * half_rows),
            transcendentals=2 * half_rows * main,
        ),
        name="project",
    )(w_offs, t_rows, t_cols, *w_pieces, *t_pieces)


def split_dot(left, right):
    high = left.astype(jnp.bfloat16)
    low = (left - high.astype(jnp.float32)).astype(jnp.bfloat16)
    return jnp.dot(high, right, preferred_element_type=jnp.float32) + jnp.dot(
        low, right, preferred_element_type=jnp.float32
    )


def local_kernel(inner, b_values, c_values, decay, decay_t, step_t, gain, out):
    length = PAGE
    row = lax.broadcasted_iota(jnp.int32, (length, length), 0)
    column = lax.broadcasted_iota(jnp.int32, (length, length), 1)
    causal = row >= column
    first = lax.broadcasted_iota(jnp.int32, (length, 2 * HP), 1) < HP
    for member in range(decay.shape[0]):
        rows = slice(member * length, (member + 1) * length)
        crossing = lax.dot_general(
            c_values[rows, :],
            b_values[rows, :],
            (((1,), (1,)), ((), ())),
            preferred_element_type=jnp.float32,
        )
        for pair in range(decay.shape[2] // 2):
            lanes = slice(pair * 2 * HP, (pair + 1) * 2 * HP)
            values = inner[rows, lanes]
            parts = []
            for head in (2 * pair, 2 * pair + 1):
                gaps = decay[member, :, head : head + 1] - decay_t[member, head : head + 1, :]
                gaps = jnp.where(causal, gaps, -jnp.inf)
                mixing = jnp.exp(gaps) * crossing * step_t[member, head : head + 1, :]
                parts.append(split_dot(mixing, values))
            local = jnp.where(first, parts[0], parts[1])
            out[rows, lanes] = local + gain[:, lanes] * values.astype(jnp.float32)


def mix_locally(inner, b_values, c_values, decay, decay_t, step_t, gain):
    rows, cols = inner.shape
    return pl.pallas_call(
        local_kernel,
        out_shape=jax.ShapeDtypeStruct((rows, cols), jnp.float32),
        in_specs=[WHOLE] * 7,
        out_specs=WHOLE,
        compiler_params=pltpu.CompilerParams(vmem_limit_bytes=VMEM),
        cost_estimate=pl.CostEstimate(
            flops=8 * rows * PAGE * cols, bytes_accessed=6 * rows * cols, transcendentals=rows * PAGE * 32
        ),
        name="mix_locally",
    )(inner, b_values, c_values, decay, decay_t, step_t, gain)


def carry_kernel(sources, incoming, c_values, decay, live, local, out, held, sems):
    members, pages = decay.shape[0], SP

    def copy(member, page):
        return pltpu.make_async_copy(
            incoming.at[sources[member, page]],
            held.at[member * pages + page],
            sems.at[member * pages + page],
        )

    for member in range(members):
        for page in range(pages):
            copy(member, page).start()
    first = lax.broadcasted_iota(jnp.int32, (PAGE, 2 * HP), 1) < HP
    for member in range(members):
        rows = slice(member * PAGE, (member + 1) * PAGE)
        fade = jnp.exp(decay[member])
        for page in range(pages):
            lanes = slice(page * 2 * HP, (page + 1) * 2 * HP)
            copy(member, page).wait()
            carried = lax.dot_general(
                c_values[rows, :],
                held[member * pages + page],
                (((1,), (1,)), ((), ())),
                preferred_element_type=jnp.float32,
            )
            factor = jnp.where(
                first, fade[:, 2 * page : 2 * page + 1], fade[:, 2 * page + 1 : 2 * page + 2]
            )
            total = (local[rows, lanes] + carried * factor) * live[rows, :]
            out[rows, lanes] = total.astype(jnp.bfloat16)


def carry_state(sources, incoming, c_values, decay, live, local):
    rows, cols = local.shape
    members = decay.shape[0]
    return pl.pallas_call(
        carry_kernel,
        out_shape=jax.ShapeDtypeStruct((rows, cols), jnp.bfloat16),
        in_specs=[SCALARS, ANY] + [WHOLE] * 4,
        out_specs=WHOLE,
        scratch_shapes=[
            pltpu.VMEM((members * SP,) + incoming.shape[1:], incoming.dtype),
            pltpu.SemaphoreType.DMA((members * SP,)),
        ],
        compiler_params=pltpu.CompilerParams(vmem_limit_bytes=VMEM),
        cost_estimate=pl.CostEstimate(
            flops=2 * rows * NST * cols, bytes_accessed=8 * rows * cols, transcendentals=0
        ),
        name="carry_state",
    )(sources, incoming, c_values, decay, live, local)


CHUNK = 8


def attend_kernel(sources, prefix, queries, fresh, live, incoming, out, stacked, held, top, total, sems):
    members, slots = sources.shape
    heads = queries.shape[1] // HD
    factor = math.log2(math.e) / math.sqrt(HD)
    nothing = -1e30

    def copy(member, slot):
        return pltpu.make_async_copy(
            incoming.at[sources[member, slot]],
            held.at[member, pl.ds(pl.multiple_of(slot * PAGE, PAGE), PAGE), :],
            sems.at[member, slot],
        )

    for member in range(members):

        def start(slot, carry):
            @pl.when(slot < prefix[member])
            def _():
                copy(member, slot).start()

            @pl.when(slot >= prefix[member])
            def _():
                held[member, pl.ds(pl.multiple_of(slot * PAGE, PAGE), PAGE), :] = jnp.zeros(
                    (PAGE, 2 * HD), held.dtype
                )

            return carry

        lax.fori_loop(0, slots, start, 0)

    wide = CHUNK * PAGE
    block = 2 * PAGE
    causal = lax.broadcasted_iota(jnp.int32, (block, PAGE), 0) % PAGE >= lax.broadcasted_iota(
        jnp.int32, (block, PAGE), 1
    )
    for member in range(members):
        rows = slice(member * PAGE, (member + 1) * PAGE)
        for head in range(heads):
            stacked[head * PAGE : (head + 1) * PAGE, :] = queries[rows, head * HD : (head + 1) * HD]
        new_keys = fresh[rows, :HD]
        new_values = jnp.concatenate([jnp.ones((PAGE, HD), jnp.bfloat16), fresh[rows, HD:]], axis=1)
        for part in range(heads // 2):
            at = slice(part * block, (part + 1) * block)
            scores = lax.dot_general(
                stacked[at, :], new_keys, (((1,), (1,)), ((), ())), preferred_element_type=jnp.float32
            )
            scores = jnp.where(causal, scores * factor, nothing)
            best = jnp.max(scores, axis=1, keepdims=True)
            weights = jnp.exp2(scores - best).astype(jnp.bfloat16)
            top[at, :] = jnp.broadcast_to(best, (block, HD))
            total[at, :] = jnp.dot(weights, new_values, preferred_element_type=jnp.float32)

        def chunk(index, carry):
            base = index * CHUNK

            def finish(slot, inside):
                @pl.when(base + slot < prefix[member])
                def _():
                    copy(member, base + slot).wait()

                return inside

            lax.fori_loop(0, CHUNK, finish, 0)
            span = pl.ds(pl.multiple_of(index * wide, wide), wide)
            keys = held[member, span, :HD]
            values = jnp.concatenate([jnp.ones((wide, HD), jnp.bfloat16), held[member, span, HD:]], axis=1)
            seen = index * wide + lax.broadcasted_iota(jnp.int32, (1, wide), 1) < prefix[member] * PAGE
            bias = jnp.where(seen, 0.0, nothing)
            for part in range(heads // 2):
                at = slice(part * block, (part + 1) * block)
                scores = lax.dot_general(
                    stacked[at, :], keys, (((1,), (1,)), ((), ())), preferred_element_type=jnp.float32
                )
                scores = scores * factor + bias
                before = top[at, :1]
                best = jnp.maximum(before, jnp.max(scores, axis=1, keepdims=True))
                weights = jnp.exp2(scores - best).astype(jnp.bfloat16)
                shrink = jnp.exp2(before - best)
                top[at, :] = jnp.broadcast_to(best, (block, HD))
                total[at, :] = total[at, :] * shrink + jnp.dot(
                    weights, values, preferred_element_type=jnp.float32
                )
            return carry

        lax.fori_loop(0, (prefix[member] + CHUNK - 1) // CHUNK, chunk, 0)
        for head in range(heads):
            at = slice(head * PAGE, (head + 1) * PAGE)
            mixed = total[at, HD:] / total[at, :HD] * live[rows, :]
            out[rows, head * HD : (head + 1) * HD] = mixed.astype(jnp.bfloat16)


def attend(sources, prefix, queries, fresh, live, incoming):
    rows, cols = queries.shape
    members, slots = sources.shape
    heads = cols // HD
    return pl.pallas_call(
        attend_kernel,
        out_shape=jax.ShapeDtypeStruct((rows, cols), jnp.bfloat16),
        in_specs=[SCALARS, SCALARS] + [WHOLE] * 3 + [ANY],
        out_specs=WHOLE,
        scratch_shapes=[
            pltpu.VMEM((heads * PAGE, HD), jnp.bfloat16),
            pltpu.VMEM((members, slots * PAGE, 2 * HD), jnp.bfloat16),
            pltpu.VMEM((heads * PAGE, HD), jnp.float32),
            pltpu.VMEM((heads * PAGE, 2 * HD), jnp.float32),
            pltpu.SemaphoreType.DMA((members, slots)),
        ],
        compiler_params=pltpu.CompilerParams(vmem_limit_bytes=VMEM),
        cost_estimate=pl.CostEstimate(
            flops=4 * rows * cols * slots * PAGE,
            bytes_accessed=members * slots * PAGE * 4 * HD,
            transcendentals=rows * heads * slots * PAGE,
        ),
        name="attend",
    )(sources, prefix, queries, fresh, live, incoming)


def gather_weights(block, y, z):
    rows = block.shape[0]
    half = rows // 2

    def first_row(along_y, along_z):
        return (((y + along_y) % NY) * NZ + (z + along_z) % NZ) * rows

    ring = [(block, 0, 0)]
    up = down = block
    for hop in range(1, NZ // 2):
        up, down = move(up, "z", 1), move(down, "z", -1)
        ring += [(up, -hop, 0), (down, hop, 0)]
    far = NZ // 2
    ring += [(move(up[:half], "z", 1), far, 0), (move(down[half:], "z", -1), far, half)]
    pieces, offsets = [], []
    for piece, along, inside in ring:
        middle = piece.shape[0] // 2
        up, down = move(piece, "y", 1), move(piece, "y", -1)
        pieces += [piece, up, down, move(up[:middle], "y", 1), move(down[middle:], "y", -1)]
        offsets += [
            first_row(0, along) + inside,
            first_row(-1, along) + inside,
            first_row(1, along) + inside,
            first_row(2, along) + inside,
            first_row(2, along) + inside + middle,
        ]
    return pieces, offsets


def gather_tokens(tokens, x):
    rows, cols = tokens.shape
    middle = rows // 2
    up, down = move(tokens, "x", 1), move(tokens, "x", -1)
    own = [
        (tokens, 0, x),
        (up, 0, (x - 1) % NX),
        (down, 0, (x + 1) % NX),
        (move(up[:middle], "x", 1), 0, (x + 2) % NX),
        (move(down[middle:], "x", -1), middle, (x + 2) % NX),
    ]
    partner = [(move(piece, "core", 1), rows + at, block) for piece, at, block in own]
    every = own + partner
    return [e[0] for e in every], [e[1] for e in every], [e[2] * cols for e in every]


def body(
    tokens,
    x_weight,
    bc_weight,
    step_weight,
    step_bias,
    decay_log,
    skip_gain,
    queries,
    new_keyvals,
    page_pool,
    page_table,
    prefix_pages,
    new_counts,
):
    owners = lax.axis_size("dp")
    position = lax.axis_index("dp")
    x = lax.axis_index("tensor")
    core = position % 2
    z = (position // 2) % NZ
    y = position // (2 * NZ)
    seq_dev = page_table.shape[0]
    pool_size = page_pool.shape[0]
    rows = tokens.shape[0]
    length = rows // seq_dev
    heads = step_bias.shape[0]

    sources = page_table // pool_size
    places = page_table % pool_size
    names = jnp.arange(owners, dtype=jnp.int32)[:, None]

    def wanted(part):
        asked = sources[:, part].reshape(1, -1) == names
        return jnp.max(jnp.where(asked, places[:, part].reshape(1, -1), -1), axis=1)

    asks = jnp.stack([wanted(slice(SP, None)), wanted(slice(0, SP))], axis=1)
    asks = jnp.pad(asks, ((0, 0), (0, 126))).reshape(owners, 1, 128)
    picks = lax.all_to_all(asks, "dp", split_axis=0, concat_axis=0, tiled=True)
    kv_out = pack_pages(picks[:, 0, 0], page_pool)
    kv_in = lax.all_to_all(kv_out, "dp", split_axis=0, concat_axis=0, tiled=True)
    state_out = pack_pages(picks[:, 0, 1], page_pool)
    state_in = lax.all_to_all(state_out, "dp", split_axis=0, concat_axis=0, tiled=True)

    main = x_weight.shape[1] // 2
    extra = bc_weight.shape[1]
    step_wide = jnp.pad(step_weight, ((0, 0), (0, extra - heads)))
    low = jnp.concatenate([x_weight[:, :main], bc_weight], axis=1)
    high = jnp.concatenate([x_weight[:, main:], step_wide], axis=1)
    own = jnp.where(core == 0, low, high)
    other = move(jnp.where(core == 0, high, low), "core", 1)
    block = jnp.where(
        core == 0, jnp.concatenate([own, other], axis=0), jnp.concatenate([other, own], axis=0)
    )
    w_pieces, w_offs = gather_weights(block, y, z)
    t_pieces, t_rows, t_cols = gather_tokens(tokens, x)
    mine, theirs, mine_extra, theirs_extra = project(
        w_pieces,
        jnp.stack(w_offs).astype(jnp.int32),
        t_pieces,
        jnp.array(t_rows, jnp.int32),
        jnp.stack(t_cols).astype(jnp.int32),
        rows,
        main,
        extra,
        owners * x_weight.shape[0],
    )
    got, got_extra = move(theirs, "core", 1), move(theirs_extra, "core", 1)
    inner = jnp.where(
        core == 0, jnp.concatenate([mine, got], axis=1), jnp.concatenate([got, mine], axis=1)
    )
    columns = jnp.where(core == 0, mine_extra, got_extra).astype(jnp.bfloat16)
    step_raw = jnp.where(core == 0, got_extra, mine_extra)[:, :heads]
    around = jnp.stack([columns] + [move(columns, "x", -k) for k in range(1, NX)])
    quarters = [lax.dynamic_index_in_dim(around, (t - x) % NX, 0, keepdims=False) for t in range(NX)]
    b_values = jnp.concatenate(quarters[:2], axis=1)
    c_values = jnp.concatenate(quarters[2:], axis=1)

    live = (jnp.arange(length)[None, :] < new_counts[:, None]).astype(jnp.float32)
    step = jax.nn.softplus(step_raw + step_bias[None, :]).reshape(seq_dev, length, heads)
    step = step * live[:, :, None]
    decay = jnp.cumsum(-step * jnp.exp(decay_log)[None, None, :], axis=1)
    gain = jnp.repeat(skip_gain, HP)[None, :]
    live_column = live.reshape(rows, 1)
    local = mix_locally(
        inner, b_values, c_values, decay, decay.transpose(0, 2, 1), step.transpose(0, 2, 1), gain
    )
    attention_out = attend(
        sources[:, SP:], prefix_pages, queries, new_keyvals, live_column, kv_in
    )
    mamba_out = carry_state(sources[:, :SP], state_in, c_values, decay, live_column, local)
    return (mamba_out, attention_out)


def solution(mesh):
    placed = (
        P("dp", "tensor"),
        P("dp", "tensor"),
        P("dp", "tensor"),
        P("dp", "tensor"),
        P("tensor"),
        P("tensor"),
        P("tensor"),
        P("dp", "tensor"),
        P("dp", "tensor"),
        P("dp", None, "tensor"),
        P("dp", None),
        P("dp"),
        P("dp"),
    )
    return jax.shard_map(
        body,
        mesh=mesh,
        in_specs=placed,
        out_specs=(P("dp", "tensor"), P("dp", "tensor")),
        check_vma=False,
    )
```

time: 498 us -> 527 us (1.058); the launches traced: 496 us -> 517 us
  blocking collectives: 333 us -> 22.3 us
  Pallas kernels: 0 us -> 238 us
  waiting for transfers between devices: 2.08 us -> 120 us
  starting transfers between devices: 6.93 us -> 102 us
  matrix products: 51.8 us -> 0 us
  local copies, waits for them, and re-layouts: 63.1 us -> 29.9 us
  other arithmetic: 24.5 us -> 3.2 us
  between operations: 14.4 us -> 2.15 us
    all_gather x3 -> x0, blocking collectives: 333 us -> none  [the longest x1 275 us: body(): lax.all_gather(step_weight, 'dp', axis=0, tiled=True)]
    pallas_call x0 -> x6, Pallas kernels: none -> 238 us  [the longest x2 195 us: pack_pages(): pl.pallas_call(pack_kernel, out_shape=jax.ShapeDtypeStruct((owners,) + pa...]
    ppermute x0 -> x59, waiting for transfers between devices: none -> 120 us  [the longest x52 117 us: move(): return lax.ppermute(array, 'dp', shift_pairs(axis, by))]
    ppermute x0 -> x59, starting transfers between devices: none -> 85.3 us  [the longest x52 76.1 us: move(): return lax.ppermute(array, 'dp', shift_pairs(axis, by))]
    dot_general x13 -> x0, matrix products: 51.8 us -> none  [the longest x2 19.7 us: attend(): jnp.einsum('grjk,kgd->jgrd', weights, values, preferred_element_type=jnp....]
    scatter x1 -> x0, local copies, waits for them, and re-layouts: 23 us -> none  [send_pages(): picks.at[targets.reshape(-1)].set((requests % pool_size).reshape(-1))]
    all_to_all x0 -> x1, blocking collectives: none -> 22.3 us  [body(): picks = lax.all_to_all(asks, 'dp', split_axis=0, concat_axis=0, tiled=True)]
    gather x2 -> x0, local copies, waits for them, and re-layouts: 18.8 us -> none  [the longest x1 9.45 us: take_pages(): return flat_incoming[own_sources * capacity + own_ranks]]
  transfers between devices with their start and end apart: 4 -> 61, of which waited for: 0 -> 12; matrix products, arithmetic and copies ran while one was open for 23% -> 1% of each run, Pallas kernels for 0% -> 30%
where the time goes in v1:
time: 527 us; the launch traced here: 517 us
  Pallas kernels  238 us (45%)
  waiting for transfers between devices  120 us (23%)
  starting transfers between devices  102 us (19%)
  local copies, waits for them, and re-layouts  29.9 us (6%)
  blocking collectives  22.3 us (4%)
    pallas_call x2, Pallas kernels, pack_pages(): pl.pallas_call(pack_kernel, out_shape=jax.ShapeDtypeStruct((owners,) + pa...  195 us
    ppermute x52, waiting for transfers between devices, move(): return lax.ppermute(array, 'dp', shift_pairs(axis, by))  117 us
    ppermute x52, starting transfers between devices, move(): return lax.ppermute(array, 'dp', shift_pairs(axis, by))  76.1 us
    all_to_all x1, blocking collectives, body(): picks = lax.all_to_all(asks, 'dp', split_axis=0, concat_axis=0, tiled=True)  22.3 us
    unnamed x127, local copies, waits for them, and re-layouts  22.2 us
    pallas_call x1, Pallas kernels, attend(): pl.pallas_call(attend_kernel, out_shape=jax.ShapeDtypeStruct((rows, cols)...  18.5 us
    pallas_call x1, Pallas kernels, project(): pl.pallas_call(lambda *refs: project_kernel(count_w, count_t, *refs), out...  13.7 us
    all_to_all x1, starting transfers between devices, body(): lax.all_to_all(kv_out, 'dp', split_axis=0, concat_axis=0, tiled=True)  10.8 us
  transfers between devices with their start and end apart: 61, of which 12 were waited for; matrix products, arithmetic and copies ran while one was open for 1% of the time, Pallas kernels for 30%

profile of v1, /device:TPU:1, one launch (start us, length us, event | category | flops | bytes accessed | tf_op | source)
XLA Modules:
  0.0 517.4 jit_solution(7612746445791077257)
XLA Ops:
  2.1 22.3 %all_to_all.15 = s32[64,1,128]{2,1,0:T(1,128)S(1)} all-to-all(s32[64,1,128]{2,1,0:T(1,128)S(1)} %copy.42), channel_id=1, replica_groups=mesh['dp'=64,'tensor'=4] {'dp'}, dimensions={0} | all-to-all | bytes 65536 | tf_op jit(solution)/shard_map/all_to_all | solution.py:459
  24.4 2.9 slice_reduce_fusion
  27.3 65.9 %pack_pages.2 = bf16[64,128,256]{2,1,0:T(8,128)(2,1)} custom-call(s32[64]{0:T(128)} %get-tuple-element.11.picks, bf16[96,128,256]{2,1,0:T(8,128)(2,1)} %pool.3), custom_call_target="tpu_custom_call" | custom-call | bytes 8388608 | tf_op jit(solution)/shard_map/pack_pages/pallas_call | solution.py:69
  93.2 5.7 %all-to-all-start.1 = ((bf16[64,128,256]{2,1,0:T(8,128)(2,1)}), bf16[64,128,256]{2,1,0:T(8,128)(2,1)}, u32[]{:S(2)}, u32[]{:S(2)}) async-start(bf16[64,128,256]{2,1,0:T(8,128)(2,1)} %pack_pages.2), calls=%async_computation.1 | async-start | bytes 8388608 | tf_op jit(solution)/shard_map/all_to_all | solution.py:463
  98.9 129.4 %pack_pages.3 = bf16[64,128,256]{2,1,0:T(8,128)(2,1)} custom-call(s32[64]{0:T(128)} %get-tuple-element.10.picks, bf16[96,128,256]{2,1,0:T(8,128)(2,1)} %pool.3), custom_call_target="tpu_custom_call" | custom-call | bytes 8388608 | tf_op jit(solution)/shard_map/pack_pages/pallas_call | solution.py:69
  228.4 10.8 %all-to-all-start.2 = ((bf16[64,128,256]{2,1,0:T(8,128)(2,1)}), bf16[64,128,256]{2,1,0:T(8,128)(2,1)}, u32[]{:S(2)}, u32[]{:S(2)}) async-start(bf16[64,128,256]{2,1,0:T(8,128)(2,1)} %pack_pages.3), calls=%async_computation.2 | async-start | bytes 8388608 | tf_op jit(solution)/shard_map/all_to_all | solution.py:461
  241.1 1.3 collective-permute-start.5
  242.4 1.5 collective-permute-start.10
  245.0 1.5 collective-permute-start.46
  246.5 1.5 collective-permute-start.49
  248.0 90.4 %collective-permute-done.5.refs_8_ = bf16[128,1152]{1,0:T(8,128)(2,1)S(1)} collective-permute-done((bf16[128,1152]{1,0:T(8,128)(2,1)S(1)}, bf16[128,1152]{1,0:T(8,128)(2,1)S(1)}, u32[]{:S(2)}, u32[]{:S(2)}) %collective-permute-start.5) | collective-permute-done | bytes 294944 | tf_op jit(solution)/shard_map/ppermute | solution.py:42
  338.4 1.3 collective-permute-start.1
  339.6 1.5 collective-permute-start.2
  341.2 6.1 %collective-permute-done.1.refs_4_ = bf16[128,1152]{1,0:T(8,128)(2,1)S(1)} collective-permute-done((bf16[128,1152]{1,0:T(8,128)(2,1)S(1)}, bf16[128,1152]{1,0:T(8,128)(2,1)S(1)}, u32[]{:S(2)}, u32[]{:S(2)}) %collective-permute-start.1) | collective-permute-done | bytes 294944 | tf_op jit(solution)/shard_map/ppermute | solution.py:42
  348.3 2.3 collective-permute-start.20
  351.9 1.6 collective-permute-start.4
  353.4 1.4 collective-permute-start.12
  354.8 1.4 collective-permute-done.4.refs_7_
  357.9 1.8 collective-permute-start.7
  359.7 1.3 collective-permute-start.47
  361.0 1.5 collective-permute-start.48
  363.2 1.5 collective-permute-done.6.refs_9_
  364.7 1.3 collective-permute-start.14
  368.4 2.5 collective-permute-start.9
  371.5 2.0 collective-permute-start.30
  375.0 2.7 collective-permute-start.17
  377.7 7.7 %collective-permute-start.50 = (bf16[256,1024]{1,0:T(8,128)(2,1)S(1)}, bf16[256,1024]{1,0:T(8,128)(2,1)S(1)}, u32[]{:S(2)}, u32[]{:S(2)}) collective-permute-start(bf16[256,1024]{1,0:T(8,128)(2,1)S(1)} %collective-permute-done.45.refs_49_), channel_id=1, source_target_pairs={{0,4},{4,0},{8,12},{12,8},{16,20},{20,16},{24,28},{28,24},{32,36},... | collective-permute-start | bytes 1572872 | tf_op jit(solution)/shard_map/ppermute | solution.py:42
  385.6 2.8 collective-permute-start.22
  388.4 1.8 collective-permute-start.52
  390.2 3.1 collective-permute-start.53
  393.8 2.7 collective-permute-start.40
  396.6 3.5 collective-permute-start.19
  400.1 2.7 collective-permute-start.37
  403.4 2.7 collective-permute-start.27
  406.9 2.6 collective-permute-start.32
  409.8 12.3 %collective-permute-done.41.refs_44_ = bf16[64,1152]{1,0:T(8,128)(2,1)S(1)} collective-permute-done((bf16[64,1152]{1,0:T(8,128)(2,1)S(1)}, bf16[64,1152]{1,0:T(8,128)(2,1)S(1)}, u32[]{:S(2)}, u32[]{:S(2)}) %collective-permute-start.41) | collective-permute-done | bytes 147488 | tf_op jit(solution)/shard_map/ppermute | solution.py:42
  422.1 2.7 collective-permute-start.24
  424.9 1.5 collective-permute-start.38
  432.0 2.6 collective-permute-start.29
  435.8 2.7 collective-permute-start.34
  441.0 2.2 collective-permute-done.44.refs_47_
  457.5 13.7 %project.1 = (bf16[256,1024]{1,0:T(8,128)(2,1)}, bf16[256,1024]{1,0:T(8,128)(2,1)}, f32[256,128]{1,0:T(8,128)S(1)}, f32[256,128]{1,0:T(8,128)S(1)}) custom-call(s32[45]{0:T(128)S(1)} %stack.231.refs_0_, s32[10]{0:T(128)S(1)} %copy-done.33, s32[10]{0:T(128)S(1)} %stack.236.refs_2_, bf16[128,1152]{1,0:T(8,128)(2,1)S(1)} %maximum_select_fusion.1.refs_3_, ...), custom_call_target="tpu_custom_call" | custom-call | flops 4831838208 | bytes 13631488 | tf_op jit(solution)/shard_map/project/pallas_call | solution.py:129
  471.2 6.7 %collective-permute-start.54 = (f32[256,128]{1,0:T(8,128)S(1)}, f32[256,128]{1,0:T(8,128)S(1)}, u32[]{:S(2)}, u32[]{:S(2)}) collective-permute-start(f32[256,128]{1,0:T(8,128)S(1)} %get-tuple-element.7), channel_id=1, source_target_pairs={{0,4},{4,0},{8,12},{12,8},{16,20},{20,16},{24,28},{28,24},{32,36},... | collective-permute-start | bytes 393224 | tf_op jit(solution)/shard_map/ppermute | solution.py:42
  479.0 2.6 collective-permute-start.55
  484.1 2.1 collective-permute-done.56
  487.9 2.0 mix_locally.1.local
  490.0 8.7 %carry_state.1 = bf16[256,2048]{1,0:T(8,128)(2,1)} custom-call(s32[2,16]{1,0:T(2,128)S(1)} %bitcast.74, bf16[64,128,256]{2,1,0:T(8,128)(2,1)} %all-to-all-done.1.incoming, bf16[256,256]{1,0:T(8,128)(2,1)S(1)} %pad_maximum_fusion.2.c_values, f32[2,128,32]{2,1,0:T(8,128)S(1)} %reduce_window_sum.11.decay, f32[256,1]{1,0:T(8,128)S(1)} %copy.48.live, ...), custom_call_target="tpu_custom_call" | custom-call | flops 268435456 | bytes 4194304 | tf_op jit(solution)/shard_map/carry_state/pallas_call | solution.py:240
  498.7 18.5 %attend.1 = bf16[256,1024]{1,0:T(8,128)(2,1)} custom-call(s32[2,32]{1,0:T(2,128)S(1)} %slice.96.sources, s32[2]{0:T(128)S(1)} %copy-done.32, bf16[256,1024]{1,0:T(8,128)(2,1)S(1)} %copy-done, bf16[256,256]{1,0:T(8,128)(2,1)S(1)} %copy-done.23, f32[256,1]{1,0:T(8,128)S(1)} %copy.48.live, bf16[64,128,256]{2,1,0:T(8,128)(2,1)} %all-to-all-done.2.incoming), custom_call_target="tpu_custom_call" | custom-call | flops 4294967296 | bytes 4194304 | tf_op jit(solution)/shard_map/attend/pallas_call | solution.py:355
  (265 shorter events, 44.3 us)
Async XLA Ops:
  93.2 135.2 %all-to-all-start.1 = ((bf16[64,128,256]{2,1,0:T(8,128)(2,1)}), bf16[64,128,256]{2,1,0:T(8,128)(2,1)}, u32[]{:S(2)}, u32[]{:S(2)}) async-start(bf16[64,128,256]{2,1,0:T(8,128)(2,1)} %pack_pages.2), calls=%async_computation.1 | async-start | bytes 8388608 | tf_op jit(solution)/shard_map/all_to_all | solution.py:463
  228.4 270.3 %all-to-all-start.2 = ((bf16[64,128,256]{2,1,0:T(8,128)(2,1)}), bf16[64,128,256]{2,1,0:T(8,128)(2,1)}, u32[]{:S(2)}, u32[]{:S(2)}) async-start(bf16[64,128,256]{2,1,0:T(8,128)(2,1)} %pack_pages.3), calls=%async_computation.2 | async-start | bytes 8388608 | tf_op jit(solution)/shard_map/all_to_all | solution.py:461
  241.1 97.3 %collective-permute-start.5 = (bf16[128,1152]{1,0:T(8,128)(2,1)S(1)}, bf16[128,1152]{1,0:T(8,128)(2,1)S(1)}, u32[]{:S(2)}, u32[]{:S(2)}) collective-permute-start(bf16[128,1152]{1,0:T(8,128)(2,1)S(1)} %maximum_select_fusion.1.refs_3_), channel_id=1, source_target_pairs={{0,8},{4,12},{8,16},{12,20},{16,24},{20,28},{24,32},{28,36},{32,40... | collective-permute-start | bytes 884744 | tf_op jit(solution)/shard_map/ppermute | solution.py:42
  242.4 97.3 %collective-permute-start.10 = (bf16[128,1152]{1,0:T(8,128)(2,1)S(1)}, bf16[128,1152]{1,0:T(8,128)(2,1)S(1)}, u32[]{:S(2)}, u32[]{:S(2)}) collective-permute-start(bf16[128,1152]{1,0:T(8,128)(2,1)S(1)} %maximum_select_fusion.1.refs_3_), channel_id=1, source_target_pairs={{0,56},{4,60},{8,0},{12,4},{16,8},{20,12},{24,16},{28,20},{32,24},... | collective-permute-start | bytes 884744 | tf_op jit(solution)/shard_map/ppermute | solution.py:42
  243.8 104.5 %collective-permute-start.45 = (bf16[256,1024]{1,0:T(8,128)(2,1)S(1)}, bf16[256,1024]{1,0:T(8,128)(2,1)S(1)}, u32[]{:S(2)}, u32[]{:S(2)}) collective-permute-start(bf16[256,1024]{1,0:T(8,128)(2,1)S(1)} %copy-done.55), channel_id=1, source_target_pairs={{0,1},{1,2},{2,3},{3,0},{4,5},{5,6},{6,7},{7,4},{8,9},{9,10},{10,1... | collective-permute-start | bytes 1572872 | tf_op jit(solution)/shard_map/ppermute | solution.py:41
  245.0 105.6 %collective-permute-start.46 = (bf16[256,1024]{1,0:T(8,128)(2,1)S(1)}, bf16[256,1024]{1,0:T(8,128)(2,1)S(1)}, u32[]{:S(2)}, u32[]{:S(2)}) collective-permute-start(bf16[256,1024]{1,0:T(8,128)(2,1)S(1)} %copy-done.55), channel_id=1, source_target_pairs={{0,3},{1,0},{2,1},{3,2},{4,7},{5,4},{6,5},{7,6},{8,11},{9,8},{10,9... | collective-permute-start | bytes 1572872 | tf_op jit(solution)/shard_map/ppermute | solution.py:41
  246.5 105.3 %collective-permute-start.49 = (bf16[256,1024]{1,0:T(8,128)(2,1)S(1)}, bf16[256,1024]{1,0:T(8,128)(2,1)S(1)}, u32[]{:S(2)}, u32[]{:S(2)}) collective-permute-start(bf16[256,1024]{1,0:T(8,128)(2,1)S(1)} %copy-done.55), channel_id=1, source_target_pairs={{0,4},{4,0},{8,12},{12,8},{16,20},{20,16},{24,28},{28,24},{32,36},... | collective-permute-start | bytes 1572872 | tf_op jit(solution)/shard_map/ppermute | solution.py:42
  338.4 8.9 %collective-permute-start.1 = (bf16[128,1152]{1,0:T(8,128)(2,1)S(1)}, bf16[128,1152]{1,0:T(8,128)(2,1)S(1)}, u32[]{:S(2)}, u32[]{:S(2)}) collective-permute-start(bf16[128,1152]{1,0:T(8,128)(2,1)S(1)} %maximum_select_fusion.1.refs_3_), channel_id=1, source_target_pairs={{0,64},{4,68},{8,72},{12,76},{16,80},{20,84},{24,88},{28,92},{32,9... | collective-permute-start | bytes 884744 | tf_op jit(solution)/shard_map/ppermute | solution.py:42
  339.6 8.1 %collective-permute-start.2 = (bf16[128,1152]{1,0:T(8,128)(2,1)S(1)}, bf16[128,1152]{1,0:T(8,128)(2,1)S(1)}, u32[]{:S(2)}, u32[]{:S(2)}) collective-permute-start(bf16[128,1152]{1,0:T(8,128)(2,1)S(1)} %maximum_select_fusion.1.refs_3_), channel_id=1, source_target_pairs={{0,192},{4,196},{8,200},{12,204},{16,208},{20,212},{24,216},{28,22... | collective-permute-start | bytes 884744 | tf_op jit(solution)/shard_map/ppermute | solution.py:42
  347.3 10.6 %collective-permute-start.15 = (bf16[128,1152]{1,0:T(8,128)(2,1)S(1)}, bf16[128,1152]{1,0:T(8,128)(2,1)S(1)}, u32[]{:S(2)}, u32[]{:S(2)}) collective-permute-start(bf16[128,1152]{1,0:T(8,128)(2,1)S(1)} %collective-permute-done.5.refs_8_), channel_id=1, source_target_pairs={{0,8},{4,12},{8,16},{12,20},{16,24},{20,28},{24,32},{28,36},{32,40... | collective-permute-start | bytes 884744 | tf_op jit(solution)/shard_map/ppermute | solution.py:42
  348.3 11.4 %collective-permute-start.20 = (bf16[128,1152]{1,0:T(8,128)(2,1)S(1)}, bf16[128,1152]{1,0:T(8,128)(2,1)S(1)}, u32[]{:S(2)}, u32[]{:S(2)}) collective-permute-start(bf16[128,1152]{1,0:T(8,128)(2,1)S(1)} %collective-permute-done.10.refs_13_), channel_id=1, source_target_pairs={{0,56},{4,60},{8,0},{12,4},{16,8},{20,12},{24,16},{28,20},{32,24},... | collective-permute-start | bytes 884744 | tf_op jit(solution)/shard_map/ppermute | solution.py:42
  350.6 10.4 %collective-permute-start.11 = (bf16[128,1152]{1,0:T(8,128)(2,1)S(1)}, bf16[128,1152]{1,0:T(8,128)(2,1)S(1)}, u32[]{:S(2)}, u32[]{:S(2)}) collective-permute-start(bf16[128,1152]{1,0:T(8,128)(2,1)S(1)} %collective-permute-done.10.refs_13_), channel_id=1, source_target_pairs={{0,64},{4,68},{8,72},{12,76},{16,80},{20,84},{24,88},{28,92},{32,9... | collective-permute-start | bytes 884744 | tf_op jit(solution)/shard_map/ppermute | solution.py:42
  353.4 9.1 %collective-permute-start.12 = (bf16[128,1152]{1,0:T(8,128)(2,1)S(1)}, bf16[128,1152]{1,0:T(8,128)(2,1)S(1)}, u32[]{:S(2)}, u32[]{:S(2)}) collective-permute-start(bf16[128,1152]{1,0:T(8,128)(2,1)S(1)} %collective-permute-done.10.refs_13_), channel_id=1, source_target_pairs={{0,192},{4,196},{8,200},{12,204},{16,208},{20,212},{24,216},{28,22... | collective-permute-start | bytes 884744 | tf_op jit(solution)/shard_map/ppermute | solution.py:42
  356.9 7.9 %collective-permute-start.6 = (bf16[128,1152]{1,0:T(8,128)(2,1)S(1)}, bf16[128,1152]{1,0:T(8,128)(2,1)S(1)}, u32[]{:S(2)}, u32[]{:S(2)}) collective-permute-start(bf16[128,1152]{1,0:T(8,128)(2,1)S(1)} %collective-permute-done.5.refs_8_), channel_id=1, source_target_pairs={{0,64},{4,68},{8,72},{12,76},{16,80},{20,84},{24,88},{28,92},{32,9... | collective-permute-start | bytes 884744 | tf_op jit(solution)/shard_map/ppermute | solution.py:42
  357.9 9.1 %collective-permute-start.7 = (bf16[128,1152]{1,0:T(8,128)(2,1)S(1)}, bf16[128,1152]{1,0:T(8,128)(2,1)S(1)}, u32[]{:S(2)}, u32[]{:S(2)}) collective-permute-start(bf16[128,1152]{1,0:T(8,128)(2,1)S(1)} %collective-permute-done.5.refs_8_), channel_id=1, source_target_pairs={{0,192},{4,196},{8,200},{12,204},{16,208},{20,212},{24,216},{28,22... | collective-permute-start | bytes 884744 | tf_op jit(solution)/shard_map/ppermute | solution.py:42
  359.7 8.4 %collective-permute-start.47 = (bf16[128,1024]{1,0:T(8,128)(2,1)S(1)}, bf16[128,1024]{1,0:T(8,128)(2,1)S(1)}, u32[]{:S(2)}, u32[]{:S(2)}) collective-permute-start(bf16[128,1024]{1,0:T(8,128)(2,1)S(1)} %slice.147), channel_id=1, source_target_pairs={{0,1},{1,2},{2,3},{3,0},{4,5},{5,6},{6,7},{7,4},{8,9},{9,10},{10,1... | collective-permute-start | bytes 786440 | tf_op jit(solution)/shard_map/ppermute | solution.py:41
  361.0 7.3 %collective-permute-start.48 = (bf16[128,1024]{1,0:T(8,128)(2,1)S(1)}, bf16[128,1024]{1,0:T(8,128)(2,1)S(1)}, u32[]{:S(2)}, u32[]{:S(2)}) collective-permute-start(bf16[128,1024]{1,0:T(8,128)(2,1)S(1)} %slice.148), channel_id=1, source_target_pairs={{0,3},{1,0},{2,1},{3,2},{4,7},{5,4},{6,5},{7,6},{8,11},{9,8},{10,9... | collective-permute-start | bytes 786440 | tf_op jit(solution)/shard_map/ppermute | solution.py:41
  362.5 8.3 %collective-permute-start.13 = (bf16[64,1152]{1,0:T(8,128)(2,1)S(1)}, bf16[64,1152]{1,0:T(8,128)(2,1)S(1)}, u32[]{:S(2)}, u32[]{:S(2)}) collective-permute-start(bf16[64,1152]{1,0:T(8,128)(2,1)S(1)} %slice.131), channel_id=1, source_target_pairs={{0,64},{4,68},{8,72},{12,76},{16,80},{20,84},{24,88},{28,92},{32,9... | collective-permute-start | bytes 442376 | tf_op jit(solution)/shard_map/ppermute | solution.py:42
  364.7 8.8 %collective-permute-start.14 = (bf16[64,1152]{1,0:T(8,128)(2,1)S(1)}, bf16[64,1152]{1,0:T(8,128)(2,1)S(1)}, u32[]{:S(2)}, u32[]{:S(2)}) collective-permute-start(bf16[64,1152]{1,0:T(8,128)(2,1)S(1)} %slice.132), channel_id=1, source_target_pairs={{0,192},{4,196},{8,200},{12,204},{16,208},{20,212},{24,216},{28,22... | collective-permute-start | bytes 442376 | tf_op jit(solution)/shard_map/ppermute | solution.py:42
  367.0 10.7 %collective-permute-start.25 = (bf16[128,1152]{1,0:T(8,128)(2,1)S(1)}, bf16[128,1152]{1,0:T(8,128)(2,1)S(1)}, u32[]{:S(2)}, u32[]{:S(2)}) collective-permute-start(bf16[128,1152]{1,0:T(8,128)(2,1)S(1)} %collective-permute-done.15.refs_18_), channel_id=1, source_target_pairs={{0,8},{4,12},{8,16},{12,20},{16,24},{20,28},{24,32},{28,36},{32,40... | collective-permute-start | bytes 884744 | tf_op jit(solution)/shard_map/ppermute | solution.py:42
  368.4 9.3 %collective-permute-start.9 = (bf16[64,1152]{1,0:T(8,128)(2,1)S(1)}, bf16[64,1152]{1,0:T(8,128)(2,1)S(1)}, u32[]{:S(2)}, u32[]{:S(2)}) collective-permute-start(bf16[64,1152]{1,0:T(8,128)(2,1)S(1)} %slice.130), channel_id=1, source_target_pairs={{0,192},{4,196},{8,200},{12,204},{16,208},{20,212},{24,216},{28,22... | collective-permute-start | bytes 442376 | tf_op jit(solution)/shard_map/ppermute | solution.py:42
  371.5 13.9 %collective-permute-start.30 = (bf16[128,1152]{1,0:T(8,128)(2,1)S(1)}, bf16[128,1152]{1,0:T(8,128)(2,1)S(1)}, u32[]{:S(2)}, u32[]{:S(2)}) collective-permute-start(bf16[128,1152]{1,0:T(8,128)(2,1)S(1)} %collective-permute-done.20.refs_23_), channel_id=1, source_target_pairs={{0,56},{4,60},{8,0},{12,4},{16,8},{20,12},{24,16},{28,20},{32,24},... | collective-permute-start | bytes 884744 | tf_op jit(solution)/shard_map/ppermute | solution.py:42
  374.2 11.3 %collective-permute-start.16 = (bf16[128,1152]{1,0:T(8,128)(2,1)S(1)}, bf16[128,1152]{1,0:T(8,128)(2,1)S(1)}, u32[]{:S(2)}, u32[]{:S(2)}) collective-permute-start(bf16[128,1152]{1,0:T(8,128)(2,1)S(1)} %collective-permute-done.15.refs_18_), channel_id=1, source_target_pairs={{0,64},{4,68},{8,72},{12,76},{16,80},{20,84},{24,88},{28,92},{32,9... | collective-permute-start | bytes 884744 | tf_op jit(solution)/shard_map/ppermute | solution.py:42
  375.0 13.4 %collective-permute-start.17 = (bf16[128,1152]{1,0:T(8,128)(2,1)S(1)}, bf16[128,1152]{1,0:T(8,128)(2,1)S(1)}, u32[]{:S(2)}, u32[]{:S(2)}) collective-permute-start(bf16[128,1152]{1,0:T(8,128)(2,1)S(1)} %collective-permute-done.15.refs_18_), channel_id=1, source_target_pairs={{0,192},{4,196},{8,200},{12,204},{16,208},{20,212},{24,216},{28,22... | collective-permute-start | bytes 884744 | tf_op jit(solution)/shard_map/ppermute | solution.py:42
  377.7 12.5 %collective-permute-start.21 = (bf16[128,1152]{1,0:T(8,128)(2,1)S(1)}, bf16[128,1152]{1,0:T(8,128)(2,1)S(1)}, u32[]{:S(2)}, u32[]{:S(2)}) collective-permute-start(bf16[128,1152]{1,0:T(8,128)(2,1)S(1)} %collective-permute-done.20.refs_23_), channel_id=1, source_target_pairs={{0,64},{4,68},{8,72},{12,76},{16,80},{20,84},{24,88},{28,92},{32,9... | collective-permute-start | bytes 884744 | tf_op jit(solution)/shard_map/ppermute | solution.py:42
  377.7 18.8 %collective-permute-start.50 = (bf16[256,1024]{1,0:T(8,128)(2,1)S(1)}, bf16[256,1024]{1,0:T(8,128)(2,1)S(1)}, u32[]{:S(2)}, u32[]{:S(2)}) collective-permute-start(bf16[256,1024]{1,0:T(8,128)(2,1)S(1)} %collective-permute-done.45.refs_49_), channel_id=1, source_target_pairs={{0,4},{4,0},{8,12},{12,8},{16,20},{20,16},{24,28},{28,24},{32,36},... | collective-permute-start | bytes 1572872 | tf_op jit(solution)/shard_map/ppermute | solution.py:42
  385.4 14.6 %collective-permute-start.51 = (bf16[256,1024]{1,0:T(8,128)(2,1)S(1)}, bf16[256,1024]{1,0:T(8,128)(2,1)S(1)}, u32[]{:S(2)}, u32[]{:S(2)}) collective-permute-start(bf16[256,1024]{1,0:T(8,128)(2,1)S(1)} %collective-permute-done.46.refs_50_), channel_id=1, source_target_pairs={{0,4},{4,0},{8,12},{12,8},{16,20},{20,16},{24,28},{28,24},{32,36},... | collective-permute-start | bytes 1572872 | tf_op jit(solution)/shard_map/ppermute | solution.py:42
  385.6 8.2 %collective-permute-start.22 = (bf16[128,1152]{1,0:T(8,128)(2,1)S(1)}, bf16[128,1152]{1,0:T(8,128)(2,1)S(1)}, u32[]{:S(2)}, u32[]{:S(2)}) collective-permute-start(bf16[128,1152]{1,0:T(8,128)(2,1)S(1)} %collective-permute-done.20.refs_23_), channel_id=1, source_target_pairs={{0,192},{4,196},{8,200},{12,204},{16,208},{20,212},{24,216},{28,22... | collective-permute-start | bytes 884744 | tf_op jit(solution)/shard_map/ppermute | solution.py:42
  393.8 9.6 %collective-permute-start.40 = (bf16[64,1152]{1,0:T(8,128)(2,1)S(1)}, bf16[64,1152]{1,0:T(8,128)(2,1)S(1)}, u32[]{:S(2)}, u32[]{:S(2)}) collective-permute-start(bf16[64,1152]{1,0:T(8,128)(2,1)S(1)} %slice.144), channel_id=1, source_target_pairs={{0,56},{4,60},{8,0},{12,4},{16,8},{20,12},{24,16},{28,20},{32,24},... | collective-permute-start | bytes 442376 | tf_op jit(solution)/shard_map/ppermute | solution.py:42
  396.6 9.6 %collective-permute-start.19 = (bf16[64,1152]{1,0:T(8,128)(2,1)S(1)}, bf16[64,1152]{1,0:T(8,128)(2,1)S(1)}, u32[]{:S(2)}, u32[]{:S(2)}) collective-permute-start(bf16[64,1152]{1,0:T(8,128)(2,1)S(1)} %slice.134), channel_id=1, source_target_pairs={{0,192},{4,196},{8,200},{12,204},{16,208},{20,212},{24,216},{28,22... | collective-permute-start | bytes 442376 | tf_op jit(solution)/shard_map/ppermute | solution.py:42
  400.1 9.4 %collective-permute-start.37 = (bf16[64,1152]{1,0:T(8,128)(2,1)S(1)}, bf16[64,1152]{1,0:T(8,128)(2,1)S(1)}, u32[]{:S(2)}, u32[]{:S(2)}) collective-permute-start(bf16[64,1152]{1,0:T(8,128)(2,1)S(1)} %collective-permute-done.35.refs_38_), channel_id=1, source_target_pairs={{0,192},{4,196},{8,200},{12,204},{16,208},{20,212},{24,216},{28,22... | collective-permute-start | bytes 442376 | tf_op jit(solution)/shard_map/ppermute | solution.py:42
  403.4 18.7 %collective-permute-start.26 = (bf16[128,1152]{1,0:T(8,128)(2,1)S(1)}, bf16[128,1152]{1,0:T(8,128)(2,1)S(1)}, u32[]{:S(2)}, u32[]{:S(2)}) collective-permute-start(bf16[128,1152]{1,0:T(8,128)(2,1)S(1)} %collective-permute-done.25.refs_28_), channel_id=1, source_target_pairs={{0,64},{4,68},{8,72},{12,76},{16,80},{20,84},{24,88},{28,92},{32,9... | collective-permute-start | bytes 884744 | tf_op jit(solution)/shard_map/ppermute | solution.py:42
  403.4 21.3 %collective-permute-start.27 = (bf16[128,1152]{1,0:T(8,128)(2,1)S(1)}, bf16[128,1152]{1,0:T(8,128)(2,1)S(1)}, u32[]{:S(2)}, u32[]{:S(2)}) collective-permute-start(bf16[128,1152]{1,0:T(8,128)(2,1)S(1)} %collective-permute-done.25.refs_28_), channel_id=1, source_target_pairs={{0,192},{4,196},{8,200},{12,204},{16,208},{20,212},{24,216},{28,22... | collective-permute-start | bytes 884744 | tf_op jit(solution)/shard_map/ppermute | solution.py:42
  406.8 18.1 %collective-permute-start.31 = (bf16[128,1152]{1,0:T(8,128)(2,1)S(1)}, bf16[128,1152]{1,0:T(8,128)(2,1)S(1)}, u32[]{:S(2)}, u32[]{:S(2)}) collective-permute-start(bf16[128,1152]{1,0:T(8,128)(2,1)S(1)} %collective-permute-done.30.refs_33_), channel_id=1, source_target_pairs={{0,64},{4,68},{8,72},{12,76},{16,80},{20,84},{24,88},{28,92},{32,9... | collective-permute-start | bytes 884744 | tf_op jit(solution)/shard_map/ppermute | solution.py:42
  406.9 19.5 %collective-permute-start.32 = (bf16[128,1152]{1,0:T(8,128)(2,1)S(1)}, bf16[128,1152]{1,0:T(8,128)(2,1)S(1)}, u32[]{:S(2)}, u32[]{:S(2)}) collective-permute-start(bf16[128,1152]{1,0:T(8,128)(2,1)S(1)} %collective-permute-done.30.refs_33_), channel_id=1, source_target_pairs={{0,192},{4,196},{8,200},{12,204},{16,208},{20,212},{24,216},{28,22... | collective-permute-start | bytes 884744 | tf_op jit(solution)/shard_map/ppermute | solution.py:42
  409.5 12.5 %collective-permute-start.41 = (bf16[64,1152]{1,0:T(8,128)(2,1)S(1)}, bf16[64,1152]{1,0:T(8,128)(2,1)S(1)}, u32[]{:S(2)}, u32[]{:S(2)}) collective-permute-start(bf16[64,1152]{1,0:T(8,128)(2,1)S(1)} %collective-permute-done.40.refs_43_), channel_id=1, source_target_pairs={{0,64},{4,68},{8,72},{12,76},{16,80},{20,84},{24,88},{28,92},{32,9... | collective-permute-start | bytes 442376 | tf_op jit(solution)/shard_map/ppermute | solution.py:42
  422.1 8.3 %collective-permute-start.23 = (bf16[64,1152]{1,0:T(8,128)(2,1)S(1)}, bf16[64,1152]{1,0:T(8,128)(2,1)S(1)}, u32[]{:S(2)}, u32[]{:S(2)}) collective-permute-start(bf16[64,1152]{1,0:T(8,128)(2,1)S(1)} %slice.135), channel_id=1, source_target_pairs={{0,64},{4,68},{8,72},{12,76},{16,80},{20,84},{24,88},{28,92},{32,9... | collective-permute-start | bytes 442376 | tf_op jit(solution)/shard_map/ppermute | solution.py:42
  422.1 9.1 %collective-permute-start.24 = (bf16[64,1152]{1,0:T(8,128)(2,1)S(1)}, bf16[64,1152]{1,0:T(8,128)(2,1)S(1)}, u32[]{:S(2)}, u32[]{:S(2)}) collective-permute-start(bf16[64,1152]{1,0:T(8,128)(2,1)S(1)} %slice.136), channel_id=1, source_target_pairs={{0,192},{4,196},{8,200},{12,204},{16,208},{20,212},{24,216},{28,22... | collective-permute-start | bytes 442376 | tf_op jit(solution)/shard_map/ppermute | solution.py:42
  424.8 7.2 %collective-permute-start.42 = (bf16[64,1152]{1,0:T(8,128)(2,1)S(1)}, bf16[64,1152]{1,0:T(8,128)(2,1)S(1)}, u32[]{:S(2)}, u32[]{:S(2)}) collective-permute-start(bf16[64,1152]{1,0:T(8,128)(2,1)S(1)} %collective-permute-done.40.refs_43_), channel_id=1, source_target_pairs={{0,192},{4,196},{8,200},{12,204},{16,208},{20,212},{24,216},{28,22... | collective-permute-start | bytes 442376 | tf_op jit(solution)/shard_map/ppermute | solution.py:42
  424.9 9.7 %collective-permute-start.38 = (bf16[32,1152]{1,0:T(8,128)(2,1)S(1)}, bf16[32,1152]{1,0:T(8,128)(2,1)S(1)}, u32[]{:S(2)}, u32[]{:S(2)}) collective-permute-start(bf16[32,1152]{1,0:T(8,128)(2,1)S(1)} %slice.142), channel_id=1, source_target_pairs={{0,64},{4,68},{8,72},{12,76},{16,80},{20,84},{24,88},{28,92},{32,9... | collective-permute-start | bytes 221192 | tf_op jit(solution)/shard_map/ppermute | solution.py:42
  426.4 8.8 %collective-permute-start.39 = (bf16[32,1152]{1,0:T(8,128)(2,1)S(1)}, bf16[32,1152]{1,0:T(8,128)(2,1)S(1)}, u32[]{:S(2)}, u32[]{:S(2)}) collective-permute-start(bf16[32,1152]{1,0:T(8,128)(2,1)S(1)} %slice.143), channel_id=1, source_target_pairs={{0,192},{4,196},{8,200},{12,204},{16,208},{20,212},{24,216},{28,22... | collective-permute-start | bytes 221192 | tf_op jit(solution)/shard_map/ppermute | solution.py:42
  431.0 7.5 %collective-permute-start.43 = (bf16[32,1152]{1,0:T(8,128)(2,1)S(1)}, bf16[32,1152]{1,0:T(8,128)(2,1)S(1)}, u32[]{:S(2)}, u32[]{:S(2)}) collective-permute-start(bf16[32,1152]{1,0:T(8,128)(2,1)S(1)} %slice.145), channel_id=1, source_target_pairs={{0,64},{4,68},{8,72},{12,76},{16,80},{20,84},{24,88},{28,92},{32,9... | collective-permute-start | bytes 221192 | tf_op jit(solution)/shard_map/ppermute | solution.py:42
  431.9 12.0 %collective-permute-start.28 = (bf16[64,1152]{1,0:T(8,128)(2,1)}, bf16[64,1152]{1,0:T(8,128)(2,1)}, u32[]{:S(2)}, u32[]{:S(2)}) collective-permute-start(bf16[64,1152]{1,0:T(8,128)(2,1)} %slice.137), channel_id=1, source_target_pairs={{0,64},{4,68},{8,72},{12,76},{16,80},{20,84},{24,88},{28,92},{32,9... | collective-permute-start | bytes 442376 | tf_op jit(solution)/shard_map/ppermute | solution.py:42
  432.0 11.9 %collective-permute-start.29 = (bf16[64,1152]{1,0:T(8,128)(2,1)}, bf16[64,1152]{1,0:T(8,128)(2,1)}, u32[]{:S(2)}, u32[]{:S(2)}) collective-permute-start(bf16[64,1152]{1,0:T(8,128)(2,1)} %slice.138), channel_id=1, source_target_pairs={{0,192},{4,196},{8,200},{12,204},{16,208},{20,212},{24,216},{28,22... | collective-permute-start | bytes 442376 | tf_op jit(solution)/shard_map/ppermute | solution.py:42
  435.2 8.7 %collective-permute-start.33 = (bf16[64,1152]{1,0:T(8,128)(2,1)}, bf16[64,1152]{1,0:T(8,128)(2,1)}, u32[]{:S(2)}, u32[]{:S(2)}) collective-permute-start(bf16[64,1152]{1,0:T(8,128)(2,1)} %slice.139), channel_id=1, source_target_pairs={{0,64},{4,68},{8,72},{12,76},{16,80},{20,84},{24,88},{28,92},{32,9... | collective-permute-start | bytes 442376 | tf_op jit(solution)/shard_map/ppermute | solution.py:42
  435.8 8.1 %collective-permute-start.34 = (bf16[64,1152]{1,0:T(8,128)(2,1)}, bf16[64,1152]{1,0:T(8,128)(2,1)}, u32[]{:S(2)}, u32[]{:S(2)}) collective-permute-start(bf16[64,1152]{1,0:T(8,128)(2,1)} %slice.140), channel_id=1, source_target_pairs={{0,192},{4,196},{8,200},{12,204},{16,208},{20,212},{24,216},{28,22... | collective-permute-start | bytes 442376 | tf_op jit(solution)/shard_map/ppermute | solution.py:42
  471.2 7.7 %collective-permute-start.54 = (f32[256,128]{1,0:T(8,128)S(1)}, f32[256,128]{1,0:T(8,128)S(1)}, u32[]{:S(2)}, u32[]{:S(2)}) collective-permute-start(f32[256,128]{1,0:T(8,128)S(1)} %get-tuple-element.7), channel_id=1, source_target_pairs={{0,4},{4,0},{8,12},{12,8},{16,20},{20,16},{24,28},{28,24},{32,36},... | collective-permute-start | bytes 393224 | tf_op jit(solution)/shard_map/ppermute | solution.py:42
  478.8 8.7 %collective-permute-start.58 = (bf16[256,1024]{1,0:T(8,128)(2,1)}, bf16[256,1024]{1,0:T(8,128)(2,1)S(1)}, u32[]{:S(2)}, u32[]{:S(2)}) collective-permute-start(bf16[256,1024]{1,0:T(8,128)(2,1)} %get-tuple-element.9), channel_id=1, source_target_pairs={{0,4},{4,0},{8,12},{12,8},{16,20},{20,16},{24,28},{28,24},{32,36},... | collective-permute-start | bytes 1572872 | tf_op jit(solution)/shard_map/ppermute | solution.py:42
  (76 other events, 1245.4 us)

commit v2 on v1

v2 whole, which is shorter than its diff:
```python
import functools
import math

import jax
import jax.numpy as jnp
from jax import lax
from jax.experimental import pallas as pl
from jax.experimental.pallas import tpu as pltpu
from jax.sharding import Mesh
from jax.sharding import PartitionSpec as P

HP = 64
NST = 256
HD = 128
PAGE = 128
SP = 16
NY = 4
NZ = 8
NX = 4
DP = ("y", "z", "core")
VMEM = 48 * 1024 * 1024
ANY = pl.BlockSpec(memory_space=pl.ANY)
HBM = pl.BlockSpec(memory_space=pltpu.HBM)
WHOLE = pl.BlockSpec(memory_space=pltpu.VMEM)
SCALARS = pl.BlockSpec(memory_space=pltpu.SMEM)


def around_x(array, by):
    return lax.ppermute(array, "tensor", [(i, (i + by) % NX) for i in range(NX)])


def pack_kernel(column, picks, pool, out, held, in_sems, out_sems):
    owners = out.shape[0]
    parts = in_sems.shape[0]
    span = owners // parts

    def fetch(r, part):
        pltpu.make_async_copy(pool.at[picks[r, 0, column]], held.at[r], in_sems.at[part]).start()
        return part

    def store(part):
        rows = pl.ds(part * span, span)
        return pltpu.make_async_copy(held.at[rows], out.at[rows], out_sems.at[part])

    for part in range(parts):
        lax.fori_loop(part * span, (part + 1) * span, fetch, part, unroll=8)
    for part in range(parts):
        rows = pl.ds(part * span, span)
        pltpu.make_async_copy(pool.at[pl.ds(0, span)], held.at[rows], in_sems.at[part]).wait()
        store(part).start()
    for part in range(parts):
        store(part).wait()


def pack_pages(picks, column, pool):
    owners = picks.shape[0]
    page = pool.shape[1:]
    return pl.pallas_call(
        functools.partial(pack_kernel, column),
        out_shape=jax.ShapeDtypeStruct((owners,) + page, pool.dtype),
        in_specs=[SCALARS, HBM],
        out_specs=HBM,
        scratch_shapes=[
            pltpu.VMEM((owners,) + page, pool.dtype),
            pltpu.SemaphoreType.DMA((4,)),
            pltpu.SemaphoreType.DMA((4,)),
        ],
        compiler_params=pltpu.CompilerParams(vmem_limit_bytes=62 * 1024 * 1024),
        cost_estimate=pl.CostEstimate(
            flops=0, bytes_accessed=4 * owners * page[0] * page[1], transcendentals=0
        ),
        name="pack_pages",
    )(picks, pool)


def project_kernel(x, weights, *refs):
    pieces = refs[:5]
    main_out, extra_out, w_all, t_all, w_sems, t_sems = refs[5:]
    tiles, wide = w_all.shape[0], w_all.shape[5]
    depth = t_all.shape[1]
    cols = pieces[0].shape[1]
    middle = pieces[3].shape[0]

    def columns(n):
        along = pl.ds(pl.multiple_of(n * wide, wide), wide)
        return [
            pltpu.make_async_copy(
                weights.at[y, core, :, :, along], w_all.at[n, y, :, core], w_sems.at[n, 2 * y + core]
            )
            for y in range(NY)
            for core in range(2)
        ]

    def start(n, carry):
        for copy in columns(n):
            copy.start()
        return carry

    copies = []
    for i, (first, by) in enumerate(((0, 0), (0, NX - 1), (0, 1), (0, 2), (middle, 2))):
        along = pl.multiple_of((x[0] + by) % NX * cols, cols)
        rows = pieces[i].shape[0]
        copies.append(
            pltpu.make_async_copy(
                pieces[i], t_all.at[pl.ds(first, rows), pl.ds(along, cols)], t_sems.at[i]
            )
        )
    for copy in copies:
        copy.start()
    lax.fori_loop(0, tiles, start, 0)
    for copy in copies:
        copy.wait()

    def product(n):
        for copy in columns(n):
            copy.wait()
        tile = w_all[n].reshape(depth, wide)
        return jnp.dot(t_all[...], tile, preferred_element_type=jnp.float32)

    def main_tile(n, carry):
        total = product(n)
        value = total / (1.0 + jnp.exp(-total))
        main_out[:, pl.ds(pl.multiple_of(n * wide, wide), wide)] = value.astype(jnp.bfloat16)
        return carry

    lax.fori_loop(0, tiles - 1, main_tile, 0)
    extra_out[...] = product(tiles - 1)


def project(x, weights, pieces, rows, wide):
    cols = weights.shape[-1]
    depth = weights.size // cols
    main = cols - wide
    return pl.pallas_call(
        project_kernel,
        out_shape=(
            jax.ShapeDtypeStruct((rows, main), jnp.bfloat16),
            jax.ShapeDtypeStruct((rows, wide), jnp.float32),
        ),
        in_specs=[SCALARS, HBM] + [ANY] * 5,
        out_specs=(WHOLE,) * 2,
        scratch_shapes=[
            pltpu.VMEM((cols // wide, NY, NZ, 2, depth // (2 * NY * NZ), wide), jnp.bfloat16),
            pltpu.VMEM((rows, depth), jnp.bfloat16),
            pltpu.SemaphoreType.DMA((cols // wide, 2 * NY)),
            pltpu.SemaphoreType.DMA((5,)),
        ],
        compiler_params=pltpu.CompilerParams(vmem_limit_bytes=VMEM),
        cost_estimate=pl.CostEstimate(
            flops=2 * rows * depth * cols, bytes_accessed=2 * depth * (cols + rows), transcendentals=rows * main
        ),
        name="project",
    )(x, weights, *pieces)


def split_dot(left, right):
    high = left.astype(jnp.bfloat16)
    low = (left - high.astype(jnp.float32)).astype(jnp.bfloat16)
    return jnp.dot(high, right, preferred_element_type=jnp.float32) + jnp.dot(
        low, right, preferred_element_type=jnp.float32
    )


def local_kernel(inner, b_values, c_values, decay, decay_t, step_t, gain, live, out, factor):
    length = PAGE
    row = lax.broadcasted_iota(jnp.int32, (length, length), 0)
    column = lax.broadcasted_iota(jnp.int32, (length, length), 1)
    causal = row >= column
    first = lax.broadcasted_iota(jnp.int32, (length, 2 * HP), 1) < HP
    for member in range(decay.shape[0]):
        rows = slice(member * length, (member + 1) * length)
        crossing = lax.dot_general(
            c_values[rows, :],
            b_values[rows, :],
            (((1,), (1,)), ((), ())),
            preferred_element_type=jnp.float32,
        )
        fades = jnp.exp(decay[member])
        for pair in range(decay.shape[2] // 2):
            lanes = slice(pair * 2 * HP, (pair + 1) * 2 * HP)
            values = inner[rows, lanes]
            parts = []
            for head in (2 * pair, 2 * pair + 1):
                gaps = decay[member, :, head : head + 1] - decay_t[member, head : head + 1, :]
                gaps = jnp.where(causal, gaps, -jnp.inf)
                mixing = jnp.exp(gaps) * crossing * step_t[member, head : head + 1, :]
                parts.append(split_dot(mixing, values))
            local = jnp.where(first, parts[0], parts[1])
            local = local + gain[:, lanes] * values.astype(jnp.float32)
            out[rows, lanes] = local * live[rows, :]
            fade = jnp.where(first, fades[:, 2 * pair : 2 * pair + 1], fades[:, 2 * pair + 1 : 2 * pair + 2])
            factor[rows, lanes] = fade * live[rows, :]


def mix_locally(inner, b_values, c_values, decay, decay_t, step_t, gain, live):
    rows, cols = inner.shape
    return pl.pallas_call(
        local_kernel,
        out_shape=(jax.ShapeDtypeStruct((rows, cols), jnp.float32),) * 2,
        in_specs=[WHOLE] * 8,
        out_specs=(WHOLE,) * 2,
        compiler_params=pltpu.CompilerParams(vmem_limit_bytes=VMEM),
        cost_estimate=pl.CostEstimate(
            flops=8 * rows * PAGE * cols, bytes_accessed=6 * rows * cols, transcendentals=rows * PAGE * 32
        ),
        name="mix_locally",
    )(inner, b_values, c_values, decay, decay_t, step_t, gain, live)


def carry_kernel(
    sources, incoming, c_values, factor, local, out, held, factors, locals_, ready, in_sems, out_sems
):
    members = sources.shape[0]
    span = 2 * PAGE

    def rows_of(member):
        return pl.ds(member * PAGE, PAGE)

    def bring(member):
        rows = rows_of(member)
        return [
            pltpu.make_async_copy(factor.at[rows, :], factors.at[rows, :], in_sems.at[member, 1]),
            pltpu.make_async_copy(local.at[rows, :], locals_.at[rows, :], in_sems.at[member, 2]),
        ]

    def store(member):
        rows = rows_of(member)
        return pltpu.make_async_copy(ready.at[rows, :], out.at[rows, :], out_sems.at[member])

    for member in range(members):
        for page in range(SP):
            pltpu.make_async_copy(
                incoming.at[sources[member, page]], held.at[member * SP + page], in_sems.at[member, 0]
            ).start()
        for copy in bring(member):
            copy.start()
    for member in range(members):
        rows = rows_of(member)
        pages = pl.ds(member * SP, SP)
        pltpu.make_async_copy(incoming.at[pl.ds(0, SP)], held.at[pages], in_sems.at[member, 0]).wait()
        for copy in bring(member):
            copy.wait()
        for page in range(0, SP, 2):
            lanes = slice(page * 2 * HP, page * 2 * HP + span)
            pair = held[member * SP + page : member * SP + page + 2].reshape(span, NST)
            carried = lax.dot_general(
                c_values[rows, :], pair, (((1,), (1,)), ((), ())), preferred_element_type=jnp.float32
            )
            total = locals_[rows, lanes] + carried * factors[rows, lanes]
            ready[rows, lanes] = total.astype(jnp.bfloat16)
        store(member).start()
    for member in range(members):
        store(member).wait()


def carry_state(sources, incoming, c_values, factor, local):
    rows, cols = local.shape
    members = sources.shape[0]
    return pl.pallas_call(
        carry_kernel,
        out_shape=jax.ShapeDtypeStruct((rows, cols), jnp.bfloat16),
        in_specs=[SCALARS, HBM, WHOLE, HBM, HBM],
        out_specs=HBM,
        scratch_shapes=[
            pltpu.VMEM((members * SP,) + incoming.shape[1:], incoming.dtype),
            pltpu.VMEM((rows, cols), jnp.float32),
            pltpu.VMEM((rows, cols), jnp.float32),
            pltpu.VMEM((rows, cols), jnp.bfloat16),
            pltpu.SemaphoreType.DMA((members, 3)),
            pltpu.SemaphoreType.DMA((members,)),
        ],
        compiler_params=pltpu.CompilerParams(vmem_limit_bytes=VMEM),
        cost_estimate=pl.CostEstimate(
            flops=2 * rows * NST * cols, bytes_accessed=8 * rows * cols, transcendentals=0
        ),
        name="carry_state",
    )(sources, incoming, c_values, factor, local)


CHUNK = 8


def attend_kernel(sources, prefix, queries, fresh, live, incoming, out, stacked, held, top, total, sems):
    members, slots = sources.shape
    heads = queries.shape[1] // HD
    factor = math.log2(math.e) / math.sqrt(HD)
    nothing = -1e30

    def copy(member, slot):
        return pltpu.make_async_copy(
            incoming.at[sources[member, slot]],
            held.at[member, pl.ds(pl.multiple_of(slot * PAGE, PAGE), PAGE), :],
            sems.at[member, slot],
        )

    for member in range(members):

        def start(slot, carry):
            @pl.when(slot < prefix[member])
            def _():
                copy(member, slot).start()

            @pl.when(slot >= prefix[member])
            def _():
                held[member, pl.ds(pl.multiple_of(slot * PAGE, PAGE), PAGE), :] = jnp.zeros(
                    (PAGE, 2 * HD), held.dtype
                )

            return carry

        lax.fori_loop(0, slots, start, 0)

    wide = CHUNK * PAGE
    block = 2 * PAGE
    causal = lax.broadcasted_iota(jnp.int32, (block, PAGE), 0) % PAGE >= lax.broadcasted_iota(
        jnp.int32, (block, PAGE), 1
    )
    for member in range(members):
        rows = slice(member * PAGE, (member + 1) * PAGE)
        for head in range(heads):
            stacked[head * PAGE : (head + 1) * PAGE, :] = queries[rows, head * HD : (head + 1) * HD]
        new_keys = fresh[rows, :HD]
        new_values = jnp.concatenate([jnp.ones((PAGE, HD), jnp.bfloat16), fresh[rows, HD:]], axis=1)
        for part in range(heads // 2):
            at = slice(part * block, (part + 1) * block)
            scores = lax.dot_general(
                stacked[at, :], new_keys, (((1,), (1,)), ((), ())), preferred_element_type=jnp.float32
            )
            scores = jnp.where(causal, scores * factor, nothing)
            best = jnp.max(scores, axis=1, keepdims=True)
            weights = jnp.exp2(scores - best).astype(jnp.bfloat16)
            top[at, :] = jnp.broadcast_to(best, (block, HD))
            total[at, :] = jnp.dot(weights, new_values, preferred_element_type=jnp.float32)

        def chunk(index, carry):
            base = index * CHUNK

            def finish(slot, inside):
                @pl.when(base + slot < prefix[member])
                def _():
                    copy(member, base + slot).wait()

                return inside

            lax.fori_loop(0, CHUNK, finish, 0)
            span = pl.ds(pl.multiple_of(index * wide, wide), wide)
            keys = held[member, span, :HD]
            values = jnp.concatenate([jnp.ones((wide, HD), jnp.bfloat16), held[member, span, HD:]], axis=1)
            seen = index * wide + lax.broadcasted_iota(jnp.int32, (1, wide), 1) < prefix[member] * PAGE
            bias = jnp.where(seen, 0.0, nothing)
            for part in range(heads // 2):
                at = slice(part * block, (part + 1) * block)
                scores = lax.dot_general(
                    stacked[at, :], keys, (((1,), (1,)), ((), ())), preferred_element_type=jnp.float32
                )
                scores = scores * factor + bias
                before = top[at, :1]
                best = jnp.maximum(before, jnp.max(scores, axis=1, keepdims=True))
                weights = jnp.exp2(scores - best).astype(jnp.bfloat16)
                shrink = jnp.exp2(before - best)
                top[at, :] = jnp.broadcast_to(best, (block, HD))
                total[at, :] = total[at, :] * shrink + jnp.dot(
                    weights, values, preferred_element_type=jnp.float32
                )
            return carry

        lax.fori_loop(0, (prefix[member] + CHUNK - 1) // CHUNK, chunk, 0)
        for head in range(heads):
            at = slice(head * PAGE, (head + 1) * PAGE)
            mixed = total[at, HD:] / total[at, :HD] * live[rows, :]
            out[rows, head * HD : (head + 1) * HD] = mixed.astype(jnp.bfloat16)


def attend(sources, prefix, queries, fresh, live, incoming):
    rows, cols = queries.shape
    members, slots = sources.shape
    heads = cols // HD
    return pl.pallas_call(
        attend_kernel,
        out_shape=jax.ShapeDtypeStruct((rows, cols), jnp.bfloat16),
        in_specs=[SCALARS, SCALARS] + [WHOLE] * 3 + [HBM],
        out_specs=WHOLE,
        scratch_shapes=[
            pltpu.VMEM((heads * PAGE, HD), jnp.bfloat16),
            pltpu.VMEM((members, slots * PAGE, 2 * HD), jnp.bfloat16),
            pltpu.VMEM((heads * PAGE, HD), jnp.float32),
            pltpu.VMEM((heads * PAGE, 2 * HD), jnp.float32),
            pltpu.SemaphoreType.DMA((members, slots)),
        ],
        compiler_params=pltpu.CompilerParams(vmem_limit_bytes=VMEM),
        cost_estimate=pl.CostEstimate(
            flops=4 * rows * cols * slots * PAGE,
            bytes_accessed=members * slots * PAGE * 4 * HD,
            transcendentals=rows * heads * slots * PAGE,
        ),
        name="attend",
    )(sources, prefix, queries, fresh, live, incoming)


def gather_tokens(tokens):
    middle = tokens.shape[0] // 2
    up, down = around_x(tokens, 1), around_x(tokens, -1)
    return [tokens, up, down, around_x(up[:middle], 1), around_x(down[middle:], -1)]


def body(
    tokens,
    x_weight,
    bc_weight,
    step_weight,
    step_bias,
    decay_log,
    skip_gain,
    queries,
    new_keyvals,
    page_pool,
    page_table,
    prefix_pages,
    new_counts,
):
    owners = lax.axis_size(DP)
    x = lax.axis_index("tensor")
    seq_dev = page_table.shape[0]
    pool_size = page_pool.shape[0]
    rows = tokens.shape[0]
    length = rows // seq_dev
    heads = step_bias.shape[0]

    sources = page_table // pool_size
    places = page_table % pool_size
    names = jnp.arange(owners, dtype=jnp.int32)[:, None]

    def wanted(part):
        asked = sources[:, part].reshape(1, -1) == names
        return jnp.max(jnp.where(asked, places[:, part].reshape(1, -1), 0), axis=1)

    asks = jnp.stack([wanted(slice(SP, None)), wanted(slice(0, SP))], axis=1)
    asks = jnp.pad(asks, ((0, 0), (0, 126))).reshape(owners, 1, 128)
    extra = bc_weight.shape[1]
    x_weight, bc_weight, step_weight, asks = lax.optimization_barrier(
        (x_weight, bc_weight, step_weight, asks)
    )
    step_wide = jnp.pad(step_weight, ((0, 0), (0, extra - heads)))
    weights = jnp.concatenate([x_weight, bc_weight, step_wide], axis=1)
    weights = lax.all_gather(weights, "z", axis=0)
    picks = lax.all_to_all(asks, DP, split_axis=0, concat_axis=0, tiled=True)
    kv_out = pack_pages(picks, 0, page_pool)
    kv_in = lax.all_to_all(kv_out, DP, split_axis=0, concat_axis=0, tiled=True)
    state_out = pack_pages(picks, 1, page_pool)
    state_in = lax.all_to_all(state_out, DP, split_axis=0, concat_axis=0, tiled=True)

    weights, _ = lax.optimization_barrier((weights, state_out))
    weights = lax.all_gather(weights, ("y", "core"), axis=0)
    weights = weights.reshape((NY, 2) + weights.shape[1:])
    tokens, _ = lax.optimization_barrier((tokens, kv_out))
    inner, extras = project(
        x.reshape(1).astype(jnp.int32), weights, gather_tokens(tokens), rows, 2 * extra
    )
    columns = extras[:, :extra].astype(jnp.bfloat16)
    step_raw = extras[:, extra : extra + heads]
    around = jnp.stack([columns] + [around_x(columns, -k) for k in range(1, NX)])
    quarters = [lax.dynamic_index_in_dim(around, (t - x) % NX, 0, keepdims=False) for t in range(NX)]
    b_values = jnp.concatenate(quarters[:2], axis=1)
    c_values = jnp.concatenate(quarters[2:], axis=1)

    live = (jnp.arange(length)[None, :] < new_counts[:, None]).astype(jnp.float32)
    step = jax.nn.softplus(step_raw + step_bias[None, :]).reshape(seq_dev, length, heads)
    step = step * live[:, :, None]
    decay = jnp.cumsum(-step * jnp.exp(decay_log)[None, None, :], axis=1)
    gain = jnp.repeat(skip_gain, HP)[None, :]
    live_column = live.reshape(rows, 1)
    local, factor = mix_locally(
        inner, b_values, c_values, decay, decay.transpose(0, 2, 1), step.transpose(0, 2, 1), gain, live_column
    )
    attention_out = attend(
        sources[:, SP:], prefix_pages, queries, new_keyvals, live_column, kv_in
    )
    mamba_out = carry_state(sources[:, :SP], state_in, c_values, factor, local)
    return (mamba_out, attention_out)


def solution(mesh):
    split = Mesh(mesh.devices.reshape(NY, NZ, 2, NX), DP + ("tensor",))
    placed = (
        P(DP, "tensor"),
        P(DP, "tensor"),
        P(DP, "tensor"),
        P(DP, "tensor"),
        P("tensor"),
        P("tensor"),
        P("tensor"),
        P(DP, "tensor"),
        P(DP, "tensor"),
        P(DP, None, "tensor"),
        P(DP, None),
        P(DP),
        P(DP),
    )
    return jax.shard_map(
        body,
        mesh=split,
        in_specs=placed,
        out_specs=(P(DP, "tensor"), P(DP, "tensor")),
        check_vma=False,
    )
```

time: 527 us -> 281 us (0.53); the launches traced: 517 us -> 280 us
  Pallas kernels: 238 us -> 54 us
  blocking collectives: 22.3 us -> 130 us
  starting transfers between devices: 102 us -> 16.1 us
  waiting for transfers between devices: 120 us -> 53.6 us
  local copies, waits for them, and re-layouts: 29.9 us -> 9.31 us
  between operations: 2.15 us -> 14.3 us
    pallas_call x4, Pallas kernels: 211 us -> 24.4 us  [the longest x2 11.4 us: pack_pages(): pl.pallas_call(functools.partial(pack_kernel, column), out_shape=jax.Shap...]
    all_to_all x1 -> x2, blocking collectives: 22.3 us -> 130 us  [the longest x1 107 us: body(): kv_in = lax.all_to_all(kv_out, DP, split_axis=0, concat_axis=0, tiled=True)]
    ppermute x59 -> x7, waiting for transfers between devices: 120 us -> 15.4 us  [around_x(): lax.ppermute(array, 'tensor', [(i, (i + by) % NX) for i in range(NX)])]
    ppermute x59 -> x7, starting transfers between devices: 85.3 us -> 9.8 us  [around_x(): lax.ppermute(array, 'tensor', [(i, (i + by) % NX) for i in range(NX)])]
    all_to_all x2 -> x1, waiting for transfers between devices: 0.01 us -> 24.6 us  [body(): lax.all_to_all(state_out, DP, split_axis=0, concat_axis=0, tiled=True)]
    unnamed x127 -> x27, local copies, waits for them, and re-layouts: 22.2 us -> 8.12 us
    all_gather x0 -> x2, waiting for transfers between devices: none -> 13.6 us  [the longest x1 13.5 us: body(): weights = lax.all_gather(weights, 'z', axis=0)]
    all_to_all x2 -> x1, starting transfers between devices: 16.5 us -> 6.24 us  [body(): lax.all_to_all(state_out, DP, split_axis=0, concat_axis=0, tiled=True)]
  transfers between devices with their start and end apart: 61 -> 10, of which waited for: 12 -> 6; matrix products, arithmetic and copies ran while one was open for 1% -> 0% of each run, Pallas kernels for 30% -> 18%
where the time goes in v2:
time: 281 us; the launch traced here: 280 us
  blocking collectives  130 us (46%)
  Pallas kernels  54 us (19%)
  waiting for transfers between devices  53.6 us (19%)
  starting transfers between devices  16.1 us (6%)
  between operations  14.3 us (5%)
  local copies, waits for them, and re-layouts  9.31 us (3%)
  other arithmetic  3.1 us (1%)
    all_to_all x1, blocking collectives, body(): kv_in = lax.all_to_all(kv_out, DP, split_axis=0, concat_axis=0, tiled=True)  107 us
    pallas_call x1, Pallas kernels, attend(): pl.pallas_call(attend_kernel, out_shape=jax.ShapeDtypeStruct((rows, cols)...  25.9 us
    all_to_all x1, waiting for transfers between devices, body(): lax.all_to_all(state_out, DP, split_axis=0, concat_axis=0, tiled=True)  24.6 us
    all_to_all x1, blocking collectives, body(): picks = lax.all_to_all(asks, DP, split_axis=0, concat_axis=0, tiled=True)  22.4 us
    ppermute x7, waiting for transfers between devices, around_x(): lax.ppermute(array, 'tensor', [(i, (i + by) % NX) for i in range(NX)])  15.4 us
    all_gather x1, waiting for transfers between devices, body(): weights = lax.all_gather(weights, 'z', axis=0)  13.5 us
    pallas_call x2, Pallas kernels, pack_pages(): pl.pallas_call(functools.partial(pack_kernel, column), out_shape=jax.Shap...  11.4 us
    ppermute x7, starting transfers between devices, around_x(): lax.ppermute(array, 'tensor', [(i, (i + by) % NX) for i in range(NX)])  9.8 us
  transfers between devices with their start and end apart: 10, of which 6 were waited for; matrix products, arithmetic and copies ran while one was open for 0% of the time, Pallas kernels for 18%

profile of v2, /device:TPU:1, one launch (start us, length us, event | category | flops | bytes accessed | tf_op | source)
XLA Modules:
  0.0 280.1 jit_solution(1435490874165924491)
XLA Ops:
  7.2 0.7 and_select_fusion
  7.9 0.1 slice.29
  8.0 0.1 broadcast_in_dim.40
  8.1 0.1 slice.28.sources
  8.1 0.1 eq.41
  8.2 0.1 eq.37
  8.3 0.1 broadcast_in_dim.37
  8.4 0.1 select_reduce_fusion.1
  8.5 0.1 select_reduce_fusion
  8.6 0.1 copy.37
  8.7 0.8 copy.47
  9.5 1.7 fusion.1
  11.3 22.4 %all_to_all.15.picks = s32[64,1,128]{2,1,0:T(1,128)} all-to-all(s32[64,1,128]{2,1,0:T(1,128)S(1)} %bitcast.32), channel_id=1, replica_groups=mesh['y'=4,'z'=8,'core'=2,'tensor'=4] {'y','z','core'}, dimensions={0} | all-to-all | bytes 65536 | tf_op jit(solution)/shard_map/all_to_all | solution.py:446
  33.6 6.7 %pack_pages.2 = bf16[64,128,256]{2,1,0:T(8,128)(2,1)} custom-call(s32[64,1,128]{2,1,0:T(1,128)} %all_to_all.15.picks, bf16[96,128,256]{2,1,0:T(8,128)(2,1)} %pool.3), custom_call_target="tpu_custom_call" | custom-call | bytes 8388608 | tf_op jit(solution)/shard_map/pack_pages/pallas_call | solution.py:58
  40.4 13.5 %all-gather.5.cloned.1.call-done = bf16[512,2304]{1,0:T(8,128)(2,1)} async-done(((bf16[64,2304]{1,0:T(8,128)(2,1)}), bf16[512,2304]{1,0:T(8,128)(2,1)}) %all-gather.5.cloned.1.call-update) | async-done | bytes 2359312 | tf_op jit(solution)/shard_map/all_gather | solution.py:445
  53.8 4.7 %pack_pages.3 = bf16[64,128,256]{2,1,0:T(8,128)(2,1)} custom-call(s32[64,1,128]{2,1,0:T(1,128)} %all_to_all.15.picks, bf16[96,128,256]{2,1,0:T(8,128)(2,1)} %pool.3), custom_call_target="tpu_custom_call" | custom-call | bytes 8388608 | tf_op jit(solution)/shard_map/pack_pages/pallas_call | solution.py:58
  58.5 107.4 %all_to_all.16.incoming = bf16[64,128,256]{2,1,0:T(8,128)(2,1)} all-to-all(bf16[64,128,256]{2,1,0:T(8,128)(2,1)} %pack_pages.3), channel_id=1, replica_groups=mesh['y'=4,'z'=8,'core'=2,'tensor'=4] {'y','z','core'}, dimensions={0} | all-to-all | bytes 8388608 | tf_op jit(solution)/shard_map/all_to_all | solution.py:448
  165.9 6.2 %all-to-all-start.1 = ((bf16[64,128,256]{2,1,0:T(8,128)(2,1)}), bf16[64,128,256]{2,1,0:T(8,128)(2,1)}, u32[]{:S(2)}, u32[]{:S(2)}) async-start(bf16[64,128,256]{2,1,0:T(8,128)(2,1)} %pack_pages.2), calls=%async_computation.1 | async-start | bytes 8388608 | tf_op jit(solution)/shard_map/all_to_all | solution.py:450
  172.2 2.5 collective-permute-start.1
  174.7 0.1 broadcast_in_dim.43
  174.8 0.1 broadcast_in_dim_reshape.3.gain
  174.9 0.1 compare_convert_fusion
  174.9 0.1 copy.43.live
  175.1 10.3 %collective-permute-done.1.refs_2_ = bf16[256,1024]{1,0:T(8,128)(2,1)S(1)} collective-permute-done((bf16[256,1024]{1,0:T(8,128)(2,1)S(1)}, bf16[256,1024]{1,0:T(8,128)(2,1)S(1)}, u32[]{:S(2)}, u32[]{:S(2)}) %collective-permute-start.1) | collective-permute-done | bytes 524320 | tf_op jit(solution)/shard_map/ppermute | solution.py:29
  185.5 3.6 %collective-permute-start.3 = (bf16[128,1024]{1,0:T(8,128)(2,1)S(1)}, bf16[128,1024]{1,0:T(8,128)(2,1)S(1)}, u32[]{:S(2)}, u32[]{:S(2)}) collective-permute-start(bf16[128,1024]{1,0:T(8,128)(2,1)S(1)} %slice.36), channel_id=1, source_target_pairs={{0,3},{1,0},{2,1},{3,2},{4,7},{5,4},{6,5},{7,6},{8,11},{9,8},{10,9... | collective-permute-start | bytes 786440 | tf_op jit(solution)/shard_map/ppermute | solution.py:29
  189.1 0.1 collective-permute-start.2
  189.2 2.2 copy-done
  191.4 25.9 %attend.1 = bf16[256,1024]{1,0:T(8,128)(2,1)} custom-call(s32[2,32]{1,0:T(2,128)S(1)} %slice.28.sources, s32[2]{0:T(128)S(1)} %copy-done.8, bf16[256,1024]{1,0:T(8,128)(2,1)S(1)} %copy-done.6, bf16[256,256]{1,0:T(8,128)(2,1)S(1)} %copy-done.7, f32[256,1]{1,0:T(8,128)S(1)} %copy.43.live, bf16[64,128,256]{2,1,0:T(8,128)(2,1)S(1)} %copy-done), custom_call_target="tpu_custom_call" | custom-call | flops 4294967296 | bytes 4194304 | tf_op jit(solution)/shard_map/attend/pallas_call | solution.py:378
  217.4 0.1 all-gather.7.cloned.1.call-done
  217.5 9.1 %project.1 = (bf16[256,2048]{1,0:T(8,128)(2,1)S(1)}, f32[256,256]{1,0:T(8,128)S(1)}) custom-call(s32[1]{0:T(128)} %bitcast.3.x, bf16[4,2,8,64,2304]{4,3,2,1,0:T(8,128)(2,1)} %bitcast.29, bf16[256,1024]{1,0:T(8,128)(2,1)S(1)} %copy-done.3, bf16[256,1024]{1,0:T(8,128)(2,1)S(1)} %collective-permute-done.refs_1_, ...), custom_call_target="tpu_custom_call" | custom-call | flops 4831838208 | bytes 20971520 | tf_op jit(solution)/shard_map/project/pallas_call | solution.py:134
  226.6 1.0 copy-done.4
  227.5 2.7 collective-permute-start.4
  230.2 0.4 collective-permute-start.5
  230.6 0.6 collective-permute-start.6
  231.2 0.1 compare_select_fusion
  231.3 0.1 copy.40
  231.4 0.1 multiply_bitcast_fusion
  231.4 0.1 copy.41
  231.5 0.2 reduce_window_sum.11.decay
  231.7 0.1 copy.42
  231.8 3.1 %collective-permute-done.5 = bf16[256,128]{1,0:T(8,128)(2,1)S(1)} collective-permute-done((bf16[256,128]{1,0:T(8,128)(2,1)S(1)}, bf16[256,128]{1,0:T(8,128)(2,1)S(1)}, u32[]{:S(2)}, u32[]{:S(2)}) %collective-permute-start.5) | collective-permute-done | bytes 65568 | tf_op jit(solution)/shard_map/ppermute | solution.py:29
  234.9 1.9 collective-permute-done.6
  237.0 1.2 copy-done.5
  238.2 4.0 %mix_locally.1 = (f32[256,2048]{1,0:T(8,128)S(1)}, f32[256,2048]{1,0:T(8,128)S(1)}) custom-call(bf16[256,2048]{1,0:T(8,128)(2,1)S(1)} %copy-done.5, bf16[256,256]{1,0:T(8,128)(2,1)S(1)} %pad_maximum_fusion.2.b_values, bf16[256,256]{1,0:T(8,128)(2,1)S(1)} %pad_maximum_fusion.1.c_values, f32[2,128,32]{2,1,0:T(8,128)S(1)} %reduce_window_sum.11.decay, ...), custom_call_target="tpu_custom_call" | custom-call | flops 536870912 | bytes 3145728 | tf_op jit(solution)/shard_map/mix_locally/pallas_call | solution.py:197
  242.2 1.3 copy-done.1
  243.5 24.6 %all-to-all-done.1.incoming = bf16[64,128,256]{2,1,0:T(8,128)(2,1)} async-done(((bf16[64,128,256]{2,1,0:T(8,128)(2,1)}), bf16[64,128,256]{2,1,0:T(8,128)(2,1)}, u32[]{:S(2)}, u32[]{:S(2)}) %all-to-all-start.1) | async-done | bytes 4194336 | tf_op jit(solution)/shard_map/all_to_all | solution.py:450
  268.1 1.6 copy-done.2
  269.7 3.6 %carry_state.1 = bf16[256,2048]{1,0:T(8,128)(2,1)} custom-call(s32[2,16]{1,0:T(2,128)S(1)} %bitcast.28, bf16[64,128,256]{2,1,0:T(8,128)(2,1)} %all-to-all-done.1.incoming, bf16[256,256]{1,0:T(8,128)(2,1)S(1)} %pad_maximum_fusion.1.c_values, f32[256,2048]{1,0:T(8,128)S(1)} %copy-done.2, f32[256,2048]{1,0:T(8,128)S(1)} %get-tuple-element.21.local), custom_call_target="tpu_custom_call" | custom-call | flops 268435456 | bytes 4194304 | tf_op jit(solution)/shard_map/carry_state/pallas_call | solution.py:259
  (41 shorter events, 0.4 us)
Async XLA Ops:
  7.2 46.6 %all-gather.5.cloned.1.call-start = ((), (), s32[]{:S(2)}) async-start(), calls=%async_computation.3 | async-start | bytes 2654208 | tf_op jit(solution)/shard_map/all_gather | solution.py:445
  11.2 206.3 %all-gather.7.cloned.1.call-start = ((), (), s32[]{:S(2)}) async-start(), calls=%async_computation.4 | async-start | bytes 21233664 | tf_op jit(solution)/shard_map/all_gather | solution.py:453
  165.9 6.3 %copy-start.3 = (bf16[256,1024]{1,0:T(8,128)(2,1)S(1)}, bf16[256,1024]{1,0:T(8,128)(2,1)}, u32[]{:S(2)}) copy-start(bf16[256,1024]{1,0:T(8,128)(2,1)} %refs_0_) | copy-start | bytes 1572868
  165.9 8.8 %copy-start.11 = (f32[32]{0:T(128)S(1)}, f32[32]{0:T(128)}, u32[]{:S(2)}) copy-start(f32[32]{0:T(128)} %param.18) | copy-start | bytes 388
  165.9 8.8 %copy-start.10 = (f32[32]{0:T(128)S(1)}, f32[32]{0:T(128)}, u32[]{:S(2)}) copy-start(f32[32]{0:T(128)} %param.19) | copy-start | bytes 388
  165.9 9.0 %copy-start.12 = (s32[2]{0:T(128)S(1)}, s32[2]{0:T(128)}, u32[]{:S(2)}) copy-start(s32[2]{0:T(128)} %param.25) | copy-start | bytes 28
  165.9 23.3 %copy-start.6 = (bf16[256,1024]{1,0:T(8,128)(2,1)S(1)}, bf16[256,1024]{1,0:T(8,128)(2,1)}, u32[]{:S(2)}) copy-start(bf16[256,1024]{1,0:T(8,128)(2,1)} %queries.1) | copy-start | bytes 1572868
  165.9 23.3 %copy-start.7 = (bf16[256,256]{1,0:T(8,128)(2,1)S(1)}, bf16[256,256]{1,0:T(8,128)(2,1)}, u32[]{:S(2)}) copy-start(bf16[256,256]{1,0:T(8,128)(2,1)} %fresh.1) | copy-start | bytes 393220
  165.9 23.3 %copy-start.8 = (s32[2]{0:T(128)S(1)}, s32[2]{0:T(128)}, u32[]{:S(2)}) copy-start(s32[2]{0:T(128)} %prefix.1) | copy-start | bytes 28
  165.9 102.1 %all-to-all-start.1 = ((bf16[64,128,256]{2,1,0:T(8,128)(2,1)}), bf16[64,128,256]{2,1,0:T(8,128)(2,1)}, u32[]{:S(2)}, u32[]{:S(2)}) async-start(bf16[64,128,256]{2,1,0:T(8,128)(2,1)} %pack_pages.2), calls=%async_computation.1 | async-start | bytes 8388608 | tf_op jit(solution)/shard_map/all_to_all | solution.py:450
  172.2 13.2 %collective-permute-start.1 = (bf16[256,1024]{1,0:T(8,128)(2,1)S(1)}, bf16[256,1024]{1,0:T(8,128)(2,1)S(1)}, u32[]{:S(2)}, u32[]{:S(2)}) collective-permute-start(bf16[256,1024]{1,0:T(8,128)(2,1)S(1)} %copy-done.3), channel_id=1, source_target_pairs={{0,3},{1,0},{2,1},{3,2},{4,7},{5,4},{6,5},{7,6},{8,11},{9,8},{10,9... | collective-permute-start | bytes 1572872 | tf_op jit(solution)/shard_map/ppermute | solution.py:29
  174.7 14.4 %collective-permute-start = (bf16[256,1024]{1,0:T(8,128)(2,1)S(1)}, bf16[256,1024]{1,0:T(8,128)(2,1)S(1)}, u32[]{:S(2)}, u32[]{:S(2)}) collective-permute-start(bf16[256,1024]{1,0:T(8,128)(2,1)S(1)} %copy-done.3), channel_id=1, source_target_pairs={{0,1},{1,2},{2,3},{3,0},{4,5},{5,6},{6,7},{7,4},{8,9},{9,10},{10,1... | collective-permute-start | bytes 1572872 | tf_op jit(solution)/shard_map/ppermute | solution.py:29
  185.5 31.9 %collective-permute-start.3 = (bf16[128,1024]{1,0:T(8,128)(2,1)S(1)}, bf16[128,1024]{1,0:T(8,128)(2,1)S(1)}, u32[]{:S(2)}, u32[]{:S(2)}) collective-permute-start(bf16[128,1024]{1,0:T(8,128)(2,1)S(1)} %slice.36), channel_id=1, source_target_pairs={{0,3},{1,0},{2,1},{3,2},{4,7},{5,4},{6,5},{7,6},{8,11},{9,8},{10,9... | collective-permute-start | bytes 786440 | tf_op jit(solution)/shard_map/ppermute | solution.py:29
  189.1 28.3 %collective-permute-start.2 = (bf16[128,1024]{1,0:T(8,128)(2,1)S(1)}, bf16[128,1024]{1,0:T(8,128)(2,1)S(1)}, u32[]{:S(2)}, u32[]{:S(2)}) collective-permute-start(bf16[128,1024]{1,0:T(8,128)(2,1)S(1)} %slice.35), channel_id=1, source_target_pairs={{0,1},{1,2},{2,3},{3,0},{4,5},{5,6},{6,7},{7,4},{8,9},{9,10},{10,1... | collective-permute-start | bytes 786440 | tf_op jit(solution)/shard_map/ppermute | solution.py:29
  189.2 2.2 copy-start
  217.5 13.7 %copy-start.9 = (f32[32]{0:T(128)S(1)}, f32[32]{0:T(128)}, u32[]{:S(2)}) copy-start(f32[32]{0:T(128)} %param.17) | copy-start | bytes 388
  226.6 1.0 copy-start.4
  227.5 4.3 %collective-permute-start.4 = (bf16[256,128]{1,0:T(8,128)(2,1)S(1)}, bf16[256,128]{1,0:T(8,128)(2,1)S(1)}, u32[]{:S(2)}, u32[]{:S(2)}) collective-permute-start(bf16[256,128]{1,0:T(8,128)(2,1)S(1)} %slice.40), channel_id=1, source_target_pairs={{0,3},{1,0},{2,1},{3,2},{4,7},{5,4},{6,5},{7,6},{8,11},{9,8},{10,9... | collective-permute-start | bytes 196616 | tf_op jit(solution)/shard_map/ppermute | solution.py:29
  230.2 4.7 %collective-permute-start.5 = (bf16[256,128]{1,0:T(8,128)(2,1)S(1)}, bf16[256,128]{1,0:T(8,128)(2,1)S(1)}, u32[]{:S(2)}, u32[]{:S(2)}) collective-permute-start(bf16[256,128]{1,0:T(8,128)(2,1)S(1)} %slice.40), channel_id=1, source_target_pairs={{0,2},{1,3},{2,0},{3,1},{4,6},{5,7},{6,4},{7,5},{8,10},{9,11},{10,... | collective-permute-start | bytes 196616 | tf_op jit(solution)/shard_map/ppermute | solution.py:29
  230.6 6.2 %collective-permute-start.6 = (bf16[256,128]{1,0:T(8,128)(2,1)S(1)}, bf16[256,128]{1,0:T(8,128)(2,1)S(1)}, u32[]{:S(2)}, u32[]{:S(2)}) collective-permute-start(bf16[256,128]{1,0:T(8,128)(2,1)S(1)} %slice.40), channel_id=1, source_target_pairs={{0,1},{1,2},{2,3},{3,0},{4,5},{5,6},{6,7},{7,4},{8,9},{9,10},{10,1... | collective-permute-start | bytes 196616 | tf_op jit(solution)/shard_map/ppermute | solution.py:29
  237.0 1.2 copy-start.5
  242.2 1.3 copy-start.1
  268.1 1.6 copy-start.2
Sparse Core Ops, SparseCore 0:
  11.3 42.4 all-gather.4
  55.6 161.8 all-gather.6

commit v3 on v2

--- a/solution.py
+++ b/solution.py
@@ -18,7 +18,7 @@
 NZ = 8
 NX = 4
 DP = ("y", "z", "core")
-VMEM = 48 * 1024 * 1024
+VMEM = 62 * 1024 * 1024
 ANY = pl.BlockSpec(memory_space=pl.ANY)
 HBM = pl.BlockSpec(memory_space=pltpu.HBM)
 WHOLE = pl.BlockSpec(memory_space=pltpu.VMEM)
@@ -65,7 +65,7 @@
             pltpu.SemaphoreType.DMA((4,)),
             pltpu.SemaphoreType.DMA((4,)),
         ],
-        compiler_params=pltpu.CompilerParams(vmem_limit_bytes=62 * 1024 * 1024),
+        compiler_params=pltpu.CompilerParams(vmem_limit_bytes=VMEM),
         cost_estimate=pl.CostEstimate(
             flops=0, bytes_accessed=4 * owners * page[0] * page[1], transcendentals=0
         ),
@@ -446,7 +446,8 @@
     picks = lax.all_to_all(asks, DP, split_axis=0, concat_axis=0, tiled=True)
     kv_out = pack_pages(picks, 0, page_pool)
     kv_in = lax.all_to_all(kv_out, DP, split_axis=0, concat_axis=0, tiled=True)
-    state_out = pack_pages(picks, 1, page_pool)
+    later_pool, _ = lax.optimization_barrier((page_pool, kv_out))
+    state_out = pack_pages(picks, 1, later_pool)
     state_in = lax.all_to_all(state_out, DP, split_axis=0, concat_axis=0, tiled=True)
 
     weights, _ = lax.optimization_barrier((weights, state_out))

time: 281 us -> 276 us (0.982)
  local copies, waits for them, and re-layouts: 9.31 us -> 6.43 us
    all_gather x1, waiting for transfers between devices: 0.12 us -> 10.2 us  [body(): weights = lax.all_gather(weights, ('y', 'core'), axis=0)]
    pallas_call x1, Pallas kernels: 25.9 us -> 17.4 us  [attend(): pl.pallas_call(attend_kernel, out_shape=jax.ShapeDtypeStruct((rows, cols)...]
    unnamed x27 -> x25, local copies, waits for them, and re-layouts: 8.12 us -> 0.83 us
    all_gather x1, waiting for transfers between devices: 13.5 us -> 8.59 us  [body(): weights = lax.all_gather(weights, 'z', axis=0)]
    ppermute x7, waiting for transfers between devices: 15.4 us -> 10.8 us  [around_x(): lax.ppermute(array, 'tensor', [(i, (i + by) % NX) for i in range(NX)])]
    pallas_call x1, Pallas kernels: 3.98 us -> 7.32 us  [mix_locally(): pl.pallas_call(local_kernel, out_shape=(jax.ShapeDtypeStruct((rows, cols)...]
    all_to_all x1, waiting for transfers between devices: 24.6 us -> 21.8 us  [body(): lax.all_to_all(state_out, DP, split_axis=0, concat_axis=0, tiled=True)]
  transfers between devices with their start and end apart: 10 -> 10, of which waited for: 6 -> 5; matrix products, arithmetic and copies ran while one was open for 0% -> 3% of each run, Pallas kernels for 18% -> 17%
where the time goes in v3:
time: 276 us; the launch traced here: 275 us
  blocking collectives  130 us (47%)
  Pallas kernels  51.7 us (19%)
  waiting for transfers between devices  51.4 us (19%)
  starting transfers between devices  16 us (6%)
  between operations  14.3 us (5%)
  local copies, waits for them, and re-layouts  6.43 us (2%)
  other arithmetic  5.84 us (2%)
    all_to_all x1, blocking collectives, body(): kv_in = lax.all_to_all(kv_out, DP, split_axis=0, concat_axis=0, tiled=True)  107 us
    all_to_all x1, blocking collectives, body(): picks = lax.all_to_all(asks, DP, split_axis=0, concat_axis=0, tiled=True)  22.4 us
    all_to_all x1, waiting for transfers between devices, body(): lax.all_to_all(state_out, DP, split_axis=0, concat_axis=0, tiled=True)  21.8 us
    pallas_call x1, Pallas kernels, attend(): pl.pallas_call(attend_kernel, out_shape=jax.ShapeDtypeStruct((rows, cols)...  17.4 us
    pallas_call x2, Pallas kernels, pack_pages(): pl.pallas_call(functools.partial(pack_kernel, column), out_shape=jax.Shap...  11.5 us
    ppermute x7, waiting for transfers between devices, around_x(): lax.ppermute(array, 'tensor', [(i, (i + by) % NX) for i in range(NX)])  10.8 us
    pallas_call x1, Pallas kernels, project(): pl.pallas_call(project_kernel, out_shape=(jax.ShapeDtypeStruct((rows, mai...  10.3 us
    all_gather x1, waiting for transfers between devices, body(): weights = lax.all_gather(weights, ('y', 'core'), axis=0)  10.2 us
  transfers between devices with their start and end apart: 10, of which 5 were waited for; matrix products, arithmetic and copies ran while one was open for 3% of the time, Pallas kernels for 17%

profile of v3, /device:TPU:1, one launch (start us, length us, event | category | flops | bytes accessed | tf_op | source)
XLA Modules:
  0.0 275.4 jit_solution(2137312462061959238)
XLA Ops:
  7.2 0.7 and_select_fusion
  7.9 0.1 slice.29
  8.0 0.1 broadcast_in_dim.40
  8.1 0.1 slice.28.sources
  8.1 0.1 eq.41
  8.2 0.1 eq.37
  8.3 0.1 broadcast_in_dim.37
  8.4 0.1 select_reduce_fusion.1
  8.5 0.1 select_reduce_fusion
  8.6 0.1 copy.37
  8.7 0.8 copy.47
  9.5 1.7 fusion.1
  11.2 0.0 all-gather.7.cloned.1.call-start
  11.3 22.4 %all_to_all.15.picks = s32[64,1,128]{2,1,0:T(1,128)} all-to-all(s32[64,1,128]{2,1,0:T(1,128)S(1)} %bitcast.29), channel_id=1, replica_groups=mesh['y'=4,'z'=8,'core'=2,'tensor'=4] {'y','z','core'}, dimensions={0} | all-to-all | bytes 65536 | tf_op jit(solution)/shard_map/all_to_all | solution.py:446
  33.7 4.8 %pack_pages.2 = bf16[64,128,256]{2,1,0:T(8,128)(2,1)} custom-call(s32[64,1,128]{2,1,0:T(1,128)} %all_to_all.15.picks, bf16[96,128,256]{2,1,0:T(8,128)(2,1)} %pool.2), custom_call_target="tpu_custom_call" | custom-call | bytes 8388608 | tf_op jit(solution)/shard_map/pack_pages/pallas_call | solution.py:58
  38.5 6.8 %pack_pages.3 = bf16[64,128,256]{2,1,0:T(8,128)(2,1)} custom-call(s32[64,1,128]{2,1,0:T(1,128)} %all_to_all.15.picks, bf16[96,128,256]{2,1,0:T(8,128)(2,1)} %pool.2), custom_call_target="tpu_custom_call" | custom-call | bytes 8388608 | tf_op jit(solution)/shard_map/pack_pages/pallas_call | solution.py:58
  45.2 8.6 %all-gather.5.cloned.1.call-done = bf16[512,2304]{1,0:T(8,128)(2,1)} async-done(((bf16[64,2304]{1,0:T(8,128)(2,1)}), bf16[512,2304]{1,0:T(8,128)(2,1)}) %all-gather.5.cloned.1.call-update) | async-done | bytes 2359312 | tf_op jit(solution)/shard_map/all_gather | solution.py:445
  53.8 107.4 %all_to_all.16.incoming = bf16[64,128,256]{2,1,0:T(8,128)(2,1)} all-to-all(bf16[64,128,256]{2,1,0:T(8,128)(2,1)} %pack_pages.2), channel_id=1, replica_groups=mesh['y'=4,'z'=8,'core'=2,'tensor'=4] {'y','z','core'}, dimensions={0} | all-to-all | bytes 8388608 | tf_op jit(solution)/shard_map/all_to_all | solution.py:448
  161.2 6.2 %all-to-all-start.1 = ((bf16[64,128,256]{2,1,0:T(8,128)(2,1)}), bf16[64,128,256]{2,1,0:T(8,128)(2,1)}, u32[]{:S(2)}, u32[]{:S(2)}) async-start(bf16[64,128,256]{2,1,0:T(8,128)(2,1)} %pack_pages.3), calls=%async_computation.1 | async-start | bytes 8388608 | tf_op jit(solution)/shard_map/all_to_all | solution.py:451
  167.5 2.5 collective-permute-start.1
  170.0 0.1 broadcast_in_dim.43
  170.1 0.7 broadcast_in_dim_reshape.3.gain
  170.8 0.1 compare_convert_fusion
  170.8 0.8 copy.43.live
  171.6 9.1 %collective-permute-done.1.refs_2_ = bf16[256,1024]{1,0:T(8,128)(2,1)S(1)} collective-permute-done((bf16[256,1024]{1,0:T(8,128)(2,1)S(1)}, bf16[256,1024]{1,0:T(8,128)(2,1)S(1)}, u32[]{:S(2)}, u32[]{:S(2)}) %collective-permute-start.1) | collective-permute-done | bytes 524320 | tf_op jit(solution)/shard_map/ppermute | solution.py:29
  180.7 0.8 slice.36
  181.5 3.5 %collective-permute-start.3 = (bf16[128,1024]{1,0:T(8,128)(2,1)}, bf16[128,1024]{1,0:T(8,128)(2,1)S(1)}, u32[]{:S(2)}, u32[]{:S(2)}) collective-permute-start(bf16[128,1024]{1,0:T(8,128)(2,1)} %slice.36), channel_id=1, source_target_pairs={{0,3},{1,0},{2,1},{3,2},{4,7},{5,4},{6,5},{7,6},{8,11},{9,8},{10,9... | collective-permute-start | bytes 786440 | tf_op jit(solution)/shard_map/ppermute | solution.py:29
  185.0 0.1 collective-permute-start.2
  185.1 17.4 %attend.1 = bf16[256,1024]{1,0:T(8,128)(2,1)} custom-call(s32[2,32]{1,0:T(2,128)} %copy-done.7, s32[2]{0:T(128)} %prefix.1, bf16[256,1024]{1,0:T(8,128)(2,1)} %queries.1, bf16[256,256]{1,0:T(8,128)(2,1)} %fresh.1, f32[256,1]{1,0:T(8,128)} %copy.43.live, bf16[64,128,256]{2,1,0:T(8,128)(2,1)} %all_to_all.16.incoming), custom_call_target="tpu_custom_call" | custom-call | flops 4294967296 | bytes 4194304 | tf_op jit(solution)/shard_map/attend/pallas_call | solution.py:378
  202.6 10.2 %all-gather.7.cloned.1.call-done = bf16[64,64,2304]{2,1,0:T(8,128)(2,1)} async-done(((bf16[8,64,2304]{2,1,0:T(8,128)(2,1)}), bf16[64,64,2304]{2,1,0:T(8,128)(2,1)}) %all-gather.7.cloned.1.call-update) | async-done | bytes 18874384 | tf_op jit(solution)/shard_map/all_gather | solution.py:454
  212.9 10.3 %project.1 = (bf16[256,2048]{1,0:T(8,128)(2,1)}, f32[256,256]{1,0:T(8,128)}) custom-call(s32[1]{0:T(128)} %bitcast.3.x, bf16[4,2,8,64,2304]{4,3,2,1,0:T(8,128)(2,1)} %bitcast.26, bf16[256,1024]{1,0:T(8,128)(2,1)} %refs_0_, bf16[256,1024]{1,0:T(8,128)(2,1)} %copy-done.1, bf16[256,1024]{1,0:T(8,128)(2,1)} %copy-done, bf16[128,1024]{1,0:T(8,128)(2,1)} %copy-done.5, ...), custom_call_target="tpu_custom_call" | custom-call | flops 4831838208 | bytes 20971520 | tf_op jit(solution)/shard_map/project/pallas_call | solution.py:134
  223.1 0.9 slice.40
  224.0 2.4 collective-permute-start.4
  226.5 0.6 collective-permute-start.5
  227.0 0.6 collective-permute-start.6
  227.6 1.0 compare_select_fusion
  228.6 0.1 copy.40
  228.7 0.9 slice_bitcast_fusion
  229.6 0.6 multiply_bitcast_fusion
  230.2 0.1 copy.41
  230.3 0.2 reduce_window_sum.11.decay
  230.5 0.7 copy.42
  231.2 1.7 collective-permute-done.6
  233.0 0.7 pad_maximum_fusion.2.b_values
  233.6 0.7 pad_maximum_fusion.1.c_values
  234.3 7.3 %mix_locally.1 = (f32[256,2048]{1,0:T(8,128)}, f32[256,2048]{1,0:T(8,128)}) custom-call(bf16[256,2048]{1,0:T(8,128)(2,1)} %get-tuple-element.21.inner, bf16[256,256]{1,0:T(8,128)(2,1)} %pad_maximum_fusion.2.b_values, bf16[256,256]{1,0:T(8,128)(2,1)} %pad_maximum_fusion.1.c_values, f32[2,128,32]{2,1,0:T(8,128)} %copy-done.3, f32[2,32,128]{2,1,0:T(8,128)} %bitcast.33, ...), custom_call_target="tpu_custom_call" | custom-call | flops 536870912 | bytes 3145728 | tf_op jit(solution)/shard_map/mix_locally/pallas_call | solution.py:197
  241.6 21.8 %all-to-all-done.1.incoming = bf16[64,128,256]{2,1,0:T(8,128)(2,1)} async-done(((bf16[64,128,256]{2,1,0:T(8,128)(2,1)}), bf16[64,128,256]{2,1,0:T(8,128)(2,1)}, u32[]{:S(2)}, u32[]{:S(2)}) %all-to-all-start.1) | async-done | bytes 4194336 | tf_op jit(solution)/shard_map/all_to_all | solution.py:451
  263.4 5.2 %carry_state.1 = bf16[256,2048]{1,0:T(8,128)(2,1)} custom-call(s32[2,16]{1,0:T(2,128)} %bitcast.35, bf16[64,128,256]{2,1,0:T(8,128)(2,1)} %all-to-all-done.1.incoming, bf16[256,256]{1,0:T(8,128)(2,1)} %pad_maximum_fusion.1.c_values, f32[256,2048]{1,0:T(8,128)} %get-tuple-element.22.factor, f32[256,2048]{1,0:T(8,128)} %get-tuple-element.23.local), custom_call_target="tpu_custom_call" | custom-call | flops 268435456 | bytes 4194304 | tf_op jit(solution)/shard_map/carry_state/pallas_call | solution.py:259
  (39 shorter events, 0.2 us)
Async XLA Ops:
  7.2 46.7 %all-gather.5.cloned.1.call-start = ((), (), s32[]{:S(2)}) async-start(), calls=%async_computation.3 | async-start | bytes 2654208 | tf_op jit(solution)/shard_map/all_gather | solution.py:445
  7.9 30.5 %copy-start.6 = (s32[2,48]{1,0:T(2,128)}, s32[2,48]{1,0:T(2,128)S(1)}, u32[]{:S(2)}) copy-start(s32[2,48]{1,0:T(2,128)S(1)} %get-tuple-element.31) | copy-start | bytes 1156
  8.1 30.3 %copy-start.7 = (s32[2,32]{1,0:T(2,128)}, s32[2,32]{1,0:T(2,128)S(1)}, u32[]{:S(2)}) copy-start(s32[2,32]{1,0:T(2,128)S(1)} %slice.28.sources) | copy-start | bytes 772
  11.2 201.6 %all-gather.7.cloned.1.call-start = ((), (), s32[]{:S(2)}) async-start(), calls=%async_computation.4 | async-start | bytes 21233664 | tf_op jit(solution)/shard_map/all_gather | solution.py:454
  161.2 6.3 %copy-start.2 = (bf16[256,1024]{1,0:T(8,128)(2,1)S(1)}, bf16[256,1024]{1,0:T(8,128)(2,1)}, u32[]{:S(2)}) copy-start(bf16[256,1024]{1,0:T(8,128)(2,1)} %refs_0_) | copy-start | bytes 1572868
  161.2 8.8 %copy-start.10 = (f32[32]{0:T(128)S(1)}, f32[32]{0:T(128)}, u32[]{:S(2)}) copy-start(f32[32]{0:T(128)} %param.18) | copy-start | bytes 388
  161.2 8.8 %copy-start.9 = (f32[32]{0:T(128)S(1)}, f32[32]{0:T(128)}, u32[]{:S(2)}) copy-start(f32[32]{0:T(128)} %param.19) | copy-start | bytes 388
  161.2 9.5 %copy-start.11 = (s32[2]{0:T(128)S(1)}, s32[2]{0:T(128)}, u32[]{:S(2)}) copy-start(s32[2]{0:T(128)} %param.25) | copy-start | bytes 28
  161.2 102.1 %all-to-all-start.1 = ((bf16[64,128,256]{2,1,0:T(8,128)(2,1)}), bf16[64,128,256]{2,1,0:T(8,128)(2,1)}, u32[]{:S(2)}, u32[]{:S(2)}) async-start(bf16[64,128,256]{2,1,0:T(8,128)(2,1)} %pack_pages.3), calls=%async_computation.1 | async-start | bytes 8388608 | tf_op jit(solution)/shard_map/all_to_all | solution.py:451
  167.5 13.2 %collective-permute-start.1 = (bf16[256,1024]{1,0:T(8,128)(2,1)S(1)}, bf16[256,1024]{1,0:T(8,128)(2,1)S(1)}, u32[]{:S(2)}, u32[]{:S(2)}) collective-permute-start(bf16[256,1024]{1,0:T(8,128)(2,1)S(1)} %copy-done.2), channel_id=1, source_target_pairs={{0,3},{1,0},{2,1},{3,2},{4,7},{5,4},{6,5},{7,6},{8,11},{9,8},{10,9... | collective-permute-start | bytes 1572872 | tf_op jit(solution)/shard_map/ppermute | solution.py:29
  170.0 15.0 %collective-permute-start = (bf16[256,1024]{1,0:T(8,128)(2,1)S(1)}, bf16[256,1024]{1,0:T(8,128)(2,1)S(1)}, u32[]{:S(2)}, u32[]{:S(2)}) collective-permute-start(bf16[256,1024]{1,0:T(8,128)(2,1)S(1)} %copy-done.2), channel_id=1, source_target_pairs={{0,1},{1,2},{2,3},{3,0},{4,5},{5,6},{6,7},{7,4},{8,9},{9,10},{10,1... | collective-permute-start | bytes 1572872 | tf_op jit(solution)/shard_map/ppermute | solution.py:29
  180.7 21.8 %copy-start = (bf16[256,1024]{1,0:T(8,128)(2,1)}, bf16[256,1024]{1,0:T(8,128)(2,1)S(1)}, u32[]{:S(2)}) copy-start(bf16[256,1024]{1,0:T(8,128)(2,1)S(1)} %collective-permute-done.1.refs_2_) | copy-start | bytes 1572868
  181.5 21.1 %collective-permute-start.3 = (bf16[128,1024]{1,0:T(8,128)(2,1)}, bf16[128,1024]{1,0:T(8,128)(2,1)S(1)}, u32[]{:S(2)}, u32[]{:S(2)}) collective-permute-start(bf16[128,1024]{1,0:T(8,128)(2,1)} %slice.36), channel_id=1, source_target_pairs={{0,3},{1,0},{2,1},{3,2},{4,7},{5,4},{6,5},{7,6},{8,11},{9,8},{10,9... | collective-permute-start | bytes 786440 | tf_op jit(solution)/shard_map/ppermute | solution.py:29
  185.0 17.6 %copy-start.1 = (bf16[256,1024]{1,0:T(8,128)(2,1)}, bf16[256,1024]{1,0:T(8,128)(2,1)S(1)}, u32[]{:S(2)}) copy-start(bf16[256,1024]{1,0:T(8,128)(2,1)S(1)} %collective-permute-done.refs_1_) | copy-start | bytes 1572868
  185.0 17.6 %collective-permute-start.2 = (bf16[128,1024]{1,0:T(8,128)(2,1)S(1)}, bf16[128,1024]{1,0:T(8,128)(2,1)S(1)}, u32[]{:S(2)}, u32[]{:S(2)}) collective-permute-start(bf16[128,1024]{1,0:T(8,128)(2,1)S(1)} %slice.35), channel_id=1, source_target_pairs={{0,1},{1,2},{2,3},{3,0},{4,5},{5,6},{6,7},{7,4},{8,9},{9,10},{10,1... | collective-permute-start | bytes 786440 | tf_op jit(solution)/shard_map/ppermute | solution.py:29
  202.6 10.3 %copy-start.4 = (bf16[128,1024]{1,0:T(8,128)(2,1)}, bf16[128,1024]{1,0:T(8,128)(2,1)S(1)}, u32[]{:S(2)}) copy-start(bf16[128,1024]{1,0:T(8,128)(2,1)S(1)} %collective-permute-done.3.refs_4_) | copy-start | bytes 786436
  202.6 10.2 %copy-start.5 = (bf16[128,1024]{1,0:T(8,128)(2,1)}, bf16[128,1024]{1,0:T(8,128)(2,1)S(1)}, u32[]{:S(2)}) copy-start(bf16[128,1024]{1,0:T(8,128)(2,1)S(1)} %collective-permute-done.2.refs_3_) | copy-start | bytes 786436
  212.9 14.8 %copy-start.8 = (f32[32]{0:T(128)S(1)}, f32[32]{0:T(128)}, u32[]{:S(2)}) copy-start(f32[32]{0:T(128)} %param.17) | copy-start | bytes 388
  224.0 7.1 %collective-permute-start.4 = (bf16[256,128]{1,0:T(8,128)(2,1)S(1)}, bf16[256,128]{1,0:T(8,128)(2,1)S(1)}, u32[]{:S(2)}, u32[]{:S(2)}) collective-permute-start(bf16[256,128]{1,0:T(8,128)(2,1)S(1)} %slice.40), channel_id=1, source_target_pairs={{0,3},{1,0},{2,1},{3,2},{4,7},{5,4},{6,5},{7,6},{8,11},{9,8},{10,9... | collective-permute-start | bytes 196616 | tf_op jit(solution)/shard_map/ppermute | solution.py:29
  226.5 4.7 %collective-permute-start.5 = (bf16[256,128]{1,0:T(8,128)(2,1)S(1)}, bf16[256,128]{1,0:T(8,128)(2,1)S(1)}, u32[]{:S(2)}, u32[]{:S(2)}) collective-permute-start(bf16[256,128]{1,0:T(8,128)(2,1)S(1)} %slice.40), channel_id=1, source_target_pairs={{0,2},{1,3},{2,0},{3,1},{4,6},{5,7},{6,4},{7,5},{8,10},{9,11},{10,... | collective-permute-start | bytes 196616 | tf_op jit(solution)/shard_map/ppermute | solution.py:29
  227.0 5.9 %collective-permute-start.6 = (bf16[256,128]{1,0:T(8,128)(2,1)S(1)}, bf16[256,128]{1,0:T(8,128)(2,1)S(1)}, u32[]{:S(2)}, u32[]{:S(2)}) collective-permute-start(bf16[256,128]{1,0:T(8,128)(2,1)S(1)} %slice.40), channel_id=1, source_target_pairs={{0,1},{1,2},{2,3},{3,0},{4,5},{5,6},{6,7},{7,4},{8,9},{9,10},{10,1... | collective-permute-start | bytes 196616 | tf_op jit(solution)/shard_map/ppermute | solution.py:29
  230.5 3.8 %copy-start.3 = (f32[2,128,32]{2,1,0:T(8,128)}, f32[2,128,32]{2,1,0:T(8,128)S(1)}, u32[]{:S(2)}) copy-start(f32[2,128,32]{2,1,0:T(8,128)S(1)} %reduce_window_sum.11.decay) | copy-start | bytes 98308
Sparse Core Ops, SparseCore 0:
  11.4 42.4 all-gather.4
  55.6 157.1 all-gather.6

commit v4 on v3

--- a/solution.py
+++ b/solution.py
@@ -52,7 +52,7 @@
         store(part).wait()
 
 
-def pack_pages(picks, column, pool):
+def pack_pages(picks, column, pool, weight=1):
     owners = picks.shape[0]
     page = pool.shape[1:]
     return pl.pallas_call(
@@ -67,7 +67,7 @@
         ],
         compiler_params=pltpu.CompilerParams(vmem_limit_bytes=VMEM),
         cost_estimate=pl.CostEstimate(
-            flops=0, bytes_accessed=4 * owners * page[0] * page[1], transcendentals=0
+            flops=0, bytes_accessed=4 * weight * owners * page[0] * page[1], transcendentals=0
         ),
         name="pack_pages",
     )(picks, pool)
@@ -389,7 +389,7 @@
         ],
         compiler_params=pltpu.CompilerParams(vmem_limit_bytes=VMEM),
         cost_estimate=pl.CostEstimate(
-            flops=4 * rows * cols * slots * PAGE,
+            flops=400 * rows * cols * slots * PAGE,
             bytes_accessed=members * slots * PAGE * 4 * HD,
             transcendentals=rows * heads * slots * PAGE,
         ),
@@ -444,16 +444,16 @@
     weights = jnp.concatenate([x_weight, bc_weight, step_wide], axis=1)
     weights = lax.all_gather(weights, "z", axis=0)
     picks = lax.all_to_all(asks, DP, split_axis=0, concat_axis=0, tiled=True)
-    kv_out = pack_pages(picks, 0, page_pool)
+    kv_out = pack_pages(picks, 0, page_pool, 0)
     kv_in = lax.all_to_all(kv_out, DP, split_axis=0, concat_axis=0, tiled=True)
-    later_pool, _ = lax.optimization_barrier((page_pool, kv_out))
-    state_out = pack_pages(picks, 1, later_pool)
+    later_pool, _, weights = lax.optimization_barrier((page_pool, kv_out, weights))
+    state_out = pack_pages(picks, 1, later_pool, 100)
     state_in = lax.all_to_all(state_out, DP, split_axis=0, concat_axis=0, tiled=True)
 
     weights, _ = lax.optimization_barrier((weights, state_out))
     weights = lax.all_gather(weights, ("y", "core"), axis=0)
     weights = weights.reshape((NY, 2) + weights.shape[1:])
-    tokens, _ = lax.optimization_barrier((tokens, kv_out))
+    tokens, _ = lax.optimization_barrier((tokens, kv_in))
     inner, extras = project(
         x.reshape(1).astype(jnp.int32), weights, gather_tokens(tokens), rows, 2 * extra
     )

time: 276 us -> 353 us (1.28)
  waiting for transfers between devices: 51.4 us -> 227 us
  blocking collectives: 130 us -> 22.4 us
  starting transfers between devices: 16 us -> 20.7 us
  Pallas kernels: 51.7 us -> 55.4 us
    all_to_all x0 -> x1, waiting for transfers between devices: none -> 117 us  [body(): kv_in = lax.all_to_all(kv_out, DP, split_axis=0, concat_axis=0, tiled=True)]
    all_to_all x1 -> x0, blocking collectives: 107 us -> none  [body(): kv_in = lax.all_to_all(kv_out, DP, split_axis=0, concat_axis=0, tiled=True)]
    all_gather x1, waiting for transfers between devices: 10.2 us -> 107 us  [body(): weights = lax.all_gather(weights, ('y', 'core'), axis=0)]
    all_to_all x1, waiting for transfers between devices: 21.8 us -> 0.01 us  [body(): lax.all_to_all(state_out, DP, split_axis=0, concat_axis=0, tiled=True)]
    ppermute x7, waiting for transfers between devices: 10.8 us -> 1.9 us  [around_x(): lax.ppermute(array, 'tensor', [(i, (i + by) % NX) for i in range(NX)])]
    all_gather x1, waiting for transfers between devices: 8.59 us -> 0.01 us  [body(): weights = lax.all_gather(weights, 'z', axis=0)]
    all_to_all x0 -> x1, starting transfers between devices: none -> 5.66 us  [body(): kv_in = lax.all_to_all(kv_out, DP, split_axis=0, concat_axis=0, tiled=True)]
    pallas_call x1, Pallas kernels: 17.4 us -> 21.2 us  [attend(): pl.pallas_call(attend_kernel, out_shape=jax.ShapeDtypeStruct((rows, cols)...]
  transfers between devices with their start and end apart: 10 -> 11, of which waited for: 5 -> 4; matrix products, arithmetic and copies ran while one was open for 3% -> 3% of each run, Pallas kernels for 17% -> 13%
where the time goes in v4:
time: 353 us; the launch traced here: 352 us
  waiting for transfers between devices  227 us (64%)
  Pallas kernels  55.4 us (16%)
  blocking collectives  22.4 us (6%)
  starting transfers between devices  20.7 us (6%)
  between operations  14.3 us (4%)
  local copies, waits for them, and re-layouts  7.65 us (2%)
  other arithmetic  4.86 us (1%)
    all_to_all x1, waiting for transfers between devices, body(): kv_in = lax.all_to_all(kv_out, DP, split_axis=0, concat_axis=0, tiled=True)  117 us
    all_gather x1, waiting for transfers between devices, body(): weights = lax.all_gather(weights, ('y', 'core'), axis=0)  107 us
    all_to_all x1, blocking collectives, body(): picks = lax.all_to_all(asks, DP, split_axis=0, concat_axis=0, tiled=True)  22.4 us
    pallas_call x1, Pallas kernels, attend(): pl.pallas_call(attend_kernel, out_shape=jax.ShapeDtypeStruct((rows, cols)...  21.2 us
    pallas_call x2, Pallas kernels, pack_pages(): pl.pallas_call(functools.partial(pack_kernel, column), out_shape=jax.Shap...  11.4 us
    pallas_call x1, Pallas kernels, project(): pl.pallas_call(project_kernel, out_shape=(jax.ShapeDtypeStruct((rows, mai...  10.3 us
    ppermute x7, starting transfers between devices, around_x(): lax.ppermute(array, 'tensor', [(i, (i + by) % NX) for i in range(NX)])  8.74 us
    pallas_call x1, Pallas kernels, mix_locally(): pl.pallas_call(local_kernel, out_shape=(jax.ShapeDtypeStruct((rows, cols)...  7.34 us
  transfers between devices with their start and end apart: 11, of which 4 were waited for; matrix products, arithmetic and copies ran while one was open for 3% of the time, Pallas kernels for 13%

profile of v4, /device:TPU:1, one launch (start us, length us, event | category | flops | bytes accessed | tf_op | source)
XLA Modules:
  0.0 352.2 jit_solution(597452517860336073)
XLA Ops:
  7.2 0.7 and_select_fusion
  7.9 0.1 slice.29
  7.9 0.1 broadcast_in_dim.40
  8.0 0.1 slice.28.sources
  8.1 0.1 eq.41
  8.2 0.1 eq.37
  8.3 0.1 broadcast_in_dim.37
  8.3 0.1 select_reduce_fusion.1
  8.4 0.1 select_reduce_fusion
  8.6 0.1 copy.37
  8.7 22.4 %all_to_all.15.picks = s32[64,1,128]{2,1,0:T(1,128)} all-to-all(s32[64,1,128]{2,1,0:T(1,128)S(1)} %bitcast.29), channel_id=1, replica_groups=mesh['y'=4,'z'=8,'core'=2,'tensor'=4] {'y','z','core'}, dimensions={0} | all-to-all | bytes 65536 | tf_op jit(solution)/shard_map/all_to_all | solution.py:446
  31.0 4.6 %pack_pages.2 = bf16[64,128,256]{2,1,0:T(8,128)(2,1)} custom-call(s32[64,1,128]{2,1,0:T(1,128)} %all_to_all.15.picks, bf16[96,128,256]{2,1,0:T(8,128)(2,1)} %pool.2), custom_call_target="tpu_custom_call" | custom-call | tf_op jit(solution)/shard_map/pack_pages/pallas_call | solution.py:58
  35.8 5.7 %all-to-all-start.2 = ((bf16[64,128,256]{2,1,0:T(8,128)(2,1)}), bf16[64,128,256]{2,1,0:T(8,128)(2,1)}, u32[]{:S(2)}, u32[]{:S(2)}) async-start(bf16[64,128,256]{2,1,0:T(8,128)(2,1)} %pack_pages.2), calls=%async_computation.2 | async-start | bytes 8388608 | tf_op jit(solution)/shard_map/all_to_all | solution.py:448
  41.5 0.1 copy.47
  41.6 0.7 fusion.1
  42.4 117.1 %all-to-all-done.2.incoming = bf16[64,128,256]{2,1,0:T(8,128)(2,1)} async-done(((bf16[64,128,256]{2,1,0:T(8,128)(2,1)}), bf16[64,128,256]{2,1,0:T(8,128)(2,1)}, u32[]{:S(2)}, u32[]{:S(2)}) %all-to-all-start.2) | async-done | bytes 4194336 | tf_op jit(solution)/shard_map/all_to_all | solution.py:448
  159.5 2.5 collective-permute-start.1
  162.0 0.6 exp.8
  162.6 0.1 broadcast_in_dim.43
  162.7 0.7 broadcast_in_dim_reshape.3.gain
  163.3 0.1 compare_convert_fusion
  163.4 0.5 copy-done.8
  163.9 0.8 copy.43.live
  164.7 6.7 %pack_pages.3 = bf16[64,128,256]{2,1,0:T(8,128)(2,1)} custom-call(s32[64,1,128]{2,1,0:T(1,128)} %all_to_all.15.picks, bf16[96,128,256]{2,1,0:T(8,128)(2,1)} %pool.2), custom_call_target="tpu_custom_call" | custom-call | bytes 838860800 | tf_op jit(solution)/shard_map/pack_pages/pallas_call | solution.py:58
  171.5 6.2 %all-to-all-start.1 = ((bf16[64,128,256]{2,1,0:T(8,128)(2,1)}), bf16[64,128,256]{2,1,0:T(8,128)(2,1)}, u32[]{:S(2)}, u32[]{:S(2)}) async-start(bf16[64,128,256]{2,1,0:T(8,128)(2,1)} %pack_pages.3), calls=%async_computation.1 | async-start | bytes 8388608 | tf_op jit(solution)/shard_map/all_to_all | solution.py:451
  177.7 0.7 all-gather.7.cloned.1.call-update
  178.4 0.8 slice.36
  179.2 3.0 collective-permute-start.3
  182.2 0.8 slice.35
  183.0 21.2 %attend.1 = bf16[256,1024]{1,0:T(8,128)(2,1)} custom-call(s32[2,32]{1,0:T(2,128)} %copy-done.10, s32[2]{0:T(128)} %prefix.1, bf16[256,1024]{1,0:T(8,128)(2,1)} %queries.1, bf16[256,256]{1,0:T(8,128)(2,1)} %fresh.1, f32[256,1]{1,0:T(8,128)} %copy.43.live, bf16[64,128,256]{2,1,0:T(8,128)(2,1)} %all-to-all-done.2.incoming), custom_call_target="tpu_custom_call" | custom-call | flops 429496729600 | bytes 4194304 | tf_op jit(solution)/shard_map/attend/pallas_call | solution.py:378
  204.2 107.2 %all-gather.7.cloned.1.call-done = bf16[64,64,2304]{2,1,0:T(8,128)(2,1)} async-done(((bf16[8,64,2304]{2,1,0:T(8,128)(2,1)}), bf16[64,64,2304]{2,1,0:T(8,128)(2,1)}) %all-gather.7.cloned.1.call-update) | async-done | bytes 18874384 | tf_op jit(solution)/shard_map/all_gather | solution.py:454
  311.4 10.3 %project.1 = (bf16[256,2048]{1,0:T(8,128)(2,1)}, f32[256,256]{1,0:T(8,128)}) custom-call(s32[1]{0:T(128)} %bitcast.4.x, bf16[4,2,8,64,2304]{4,3,2,1,0:T(8,128)(2,1)} %bitcast.26, bf16[256,1024]{1,0:T(8,128)(2,1)} %refs_0_, bf16[256,1024]{1,0:T(8,128)(2,1)} %copy-done.1, bf16[256,1024]{1,0:T(8,128)(2,1)} %copy-done, ...), custom_call_target="tpu_custom_call" | custom-call | flops 4831838208 | bytes 20971520 | tf_op jit(solution)/shard_map/project/pallas_call | solution.py:134
  321.7 0.9 slice.40
  322.6 2.6 collective-permute-start.4
  325.2 0.7 collective-permute-start.6
  325.9 1.0 compare_select_fusion
  326.9 0.1 copy.40
  327.0 0.9 slice_bitcast_fusion
  327.9 0.6 multiply_bitcast_fusion
  328.5 0.1 copy.41
  328.6 0.2 reduce_window_sum.11.decay
  328.8 0.7 copy.42
  329.5 0.5 collective-permute-done.5
  330.0 1.4 collective-permute-done.6
  331.5 0.7 pad_maximum_fusion.2.b_values
  332.1 0.7 pad_maximum_fusion.1.c_values
  332.8 7.3 %mix_locally.1 = (f32[256,2048]{1,0:T(8,128)}, f32[256,2048]{1,0:T(8,128)}) custom-call(bf16[256,2048]{1,0:T(8,128)(2,1)} %get-tuple-element.23.inner, bf16[256,256]{1,0:T(8,128)(2,1)} %pad_maximum_fusion.2.b_values, bf16[256,256]{1,0:T(8,128)(2,1)} %pad_maximum_fusion.1.c_values, f32[2,128,32]{2,1,0:T(8,128)} %copy-done.3, f32[2,32,128]{2,1,0:T(8,128)} %bitcast.33, ...), custom_call_target="tpu_custom_call" | custom-call | flops 536870912 | bytes 3145728 | tf_op jit(solution)/shard_map/mix_locally/pallas_call | solution.py:197
  340.1 5.2 %carry_state.1 = bf16[256,2048]{1,0:T(8,128)(2,1)} custom-call(s32[2,16]{1,0:T(2,128)} %bitcast.35, bf16[64,128,256]{2,1,0:T(8,128)(2,1)} %all-to-all-done.1.incoming, bf16[256,256]{1,0:T(8,128)(2,1)} %pad_maximum_fusion.1.c_values, f32[256,2048]{1,0:T(8,128)} %get-tuple-element.24.factor, f32[256,2048]{1,0:T(8,128)} %get-tuple-element.25.local), custom_call_target="tpu_custom_call" | custom-call | flops 268435456 | bytes 4194304 | tf_op jit(solution)/shard_map/carry_state/pallas_call | solution.py:259
  (48 shorter events, 0.3 us)
Async XLA Ops:
  7.9 0.7 copy-start.6
  8.1 27.6 %copy-start.10 = (s32[2,32]{1,0:T(2,128)}, s32[2,32]{1,0:T(2,128)S(1)}, u32[]{:S(2)}) copy-start(s32[2,32]{1,0:T(2,128)S(1)} %slice.28.sources) | copy-start | bytes 772
  35.7 5.8 %copy-start.7 = (bf16[64,32]{0,1:T(8,128)(2,1)S(1)}, bf16[64,32]{0,1:T(8,128)(2,1)}, u32[]{:S(2)}) copy-start(bf16[64,32]{0,1:T(8,128)(2,1)} %param.16) | copy-start | bytes 12292
  35.7 5.9 %copy-start.4 = (bf16[64,2048]{1,0:T(8,128)(2,1)S(1)}, bf16[64,2048]{1,0:T(8,128)(2,1)}, u32[]{:S(2)}) copy-start(bf16[64,2048]{1,0:T(8,128)(2,1)} %param.14) | copy-start | bytes 786436
  35.7 5.9 %copy-start.5 = (bf16[64,128]{1,0:T(8,128)(2,1)S(1)}, bf16[64,128]{1,0:T(8,128)(2,1)}, u32[]{:S(2)}) copy-start(bf16[64,128]{1,0:T(8,128)(2,1)} %param.15) | copy-start | bytes 49156
  35.7 123.8 %copy-start.2 = (bf16[256,1024]{1,0:T(8,128)(2,1)S(1)}, bf16[256,1024]{1,0:T(8,128)(2,1)}, u32[]{:S(2)}) copy-start(bf16[256,1024]{1,0:T(8,128)(2,1)} %refs_0_) | copy-start | bytes 1572868
  35.7 126.2 %copy-start.14 = (f32[32]{0:T(128)S(1)}, f32[32]{0:T(128)}, u32[]{:S(2)}) copy-start(f32[32]{0:T(128)} %param.18) | copy-start | bytes 388
  35.8 126.8 %copy-start.13 = (f32[32]{0:T(128)S(1)}, f32[32]{0:T(128)}, u32[]{:S(2)}) copy-start(f32[32]{0:T(128)} %param.19) | copy-start | bytes 388
  35.8 127.6 %copy-start.15 = (s32[2]{0:T(128)S(1)}, s32[2]{0:T(128)}, u32[]{:S(2)}) copy-start(s32[2]{0:T(128)} %param.25) | copy-start | bytes 28
  35.8 123.7 %all-to-all-start.2 = ((bf16[64,128,256]{2,1,0:T(8,128)(2,1)}), bf16[64,128,256]{2,1,0:T(8,128)(2,1)}, u32[]{:S(2)}, u32[]{:S(2)}) async-start(bf16[64,128,256]{2,1,0:T(8,128)(2,1)} %pack_pages.2), calls=%async_computation.2 | async-start | bytes 8388608 | tf_op jit(solution)/shard_map/all_to_all | solution.py:448
  41.5 123.3 %all-gather.5.cloned.1.call-start = ((), (), s32[]{:S(2)}) async-start(), calls=%async_computation.3 | async-start | bytes 2654208 | tf_op jit(solution)/shard_map/all_gather | solution.py:445
  159.5 18.9 %collective-permute-start.1 = (bf16[256,1024]{1,0:T(8,128)(2,1)S(1)}, bf16[256,1024]{1,0:T(8,128)(2,1)S(1)}, u32[]{:S(2)}, u32[]{:S(2)}) collective-permute-start(bf16[256,1024]{1,0:T(8,128)(2,1)S(1)} %copy-done.2), channel_id=1, source_target_pairs={{0,3},{1,0},{2,1},{3,2},{4,7},{5,4},{6,5},{7,6},{8,11},{9,8},{10,9... | collective-permute-start | bytes 1572872 | tf_op jit(solution)/shard_map/ppermute | solution.py:29
  162.0 20.2 %collective-permute-start = (bf16[256,1024]{1,0:T(8,128)(2,1)S(1)}, bf16[256,1024]{1,0:T(8,128)(2,1)S(1)}, u32[]{:S(2)}, u32[]{:S(2)}) collective-permute-start(bf16[256,1024]{1,0:T(8,128)(2,1)S(1)} %copy-done.2), channel_id=1, source_target_pairs={{0,1},{1,2},{2,3},{3,0},{4,5},{5,6},{6,7},{7,4},{8,9},{9,10},{10,1... | collective-permute-start | bytes 1572872 | tf_op jit(solution)/shard_map/ppermute | solution.py:29
  163.4 0.5 copy-start.8
  171.5 168.7 %all-to-all-start.1 = ((bf16[64,128,256]{2,1,0:T(8,128)(2,1)}), bf16[64,128,256]{2,1,0:T(8,128)(2,1)}, u32[]{:S(2)}, u32[]{:S(2)}) async-start(bf16[64,128,256]{2,1,0:T(8,128)(2,1)} %pack_pages.3), calls=%async_computation.1 | async-start | bytes 8388608 | tf_op jit(solution)/shard_map/all_to_all | solution.py:451
  177.7 133.7 %all-gather.7.cloned.1.call-start = ((), (), s32[]{:S(2)}) async-start(), calls=%async_computation.4 | async-start | bytes 21233664 | tf_op jit(solution)/shard_map/all_gather | solution.py:454
  178.4 25.7 %copy-start = (bf16[256,1024]{1,0:T(8,128)(2,1)}, bf16[256,1024]{1,0:T(8,128)(2,1)S(1)}, u32[]{:S(2)}) copy-start(bf16[256,1024]{1,0:T(8,128)(2,1)S(1)} %collective-permute-done.1.refs_2_) | copy-start | bytes 1572868
  179.2 25.0 %collective-permute-start.3 = (bf16[128,1024]{1,0:T(8,128)(2,1)}, bf16[128,1024]{1,0:T(8,128)(2,1)}, u32[]{:S(2)}, u32[]{:S(2)}) collective-permute-start(bf16[128,1024]{1,0:T(8,128)(2,1)} %slice.36), channel_id=1, source_target_pairs={{0,3},{1,0},{2,1},{3,2},{4,7},{5,4},{6,5},{7,6},{8,11},{9,8},{10,9... | collective-permute-start | bytes 786440 | tf_op jit(solution)/shard_map/ppermute | solution.py:29
  182.2 22.0 %copy-start.1 = (bf16[256,1024]{1,0:T(8,128)(2,1)}, bf16[256,1024]{1,0:T(8,128)(2,1)S(1)}, u32[]{:S(2)}) copy-start(bf16[256,1024]{1,0:T(8,128)(2,1)S(1)} %collective-permute-done.refs_1_) | copy-start | bytes 1572868
  183.0 21.2 %collective-permute-start.2 = (bf16[128,1024]{1,0:T(8,128)(2,1)}, bf16[128,1024]{1,0:T(8,128)(2,1)}, u32[]{:S(2)}, u32[]{:S(2)}) collective-permute-start(bf16[128,1024]{1,0:T(8,128)(2,1)} %slice.35), channel_id=1, source_target_pairs={{0,1},{1,2},{2,3},{3,0},{4,5},{5,6},{6,7},{7,4},{8,9},{9,10},{10,1... | collective-permute-start | bytes 786440 | tf_op jit(solution)/shard_map/ppermute | solution.py:29
  311.4 14.5 %copy-start.11 = (f32[32]{0:T(128)S(1)}, f32[32]{0:T(128)}, u32[]{:S(2)}) copy-start(f32[32]{0:T(128)} %param.17) | copy-start | bytes 388
  311.4 16.5 %copy-start.9 = (f32[2,128]{1,0:T(2,128)S(1)}, f32[2,128]{1,0:T(2,128)}, u32[]{:S(2)}) copy-start(f32[2,128]{1,0:T(2,128)} %copy-done.8) | copy-start | bytes 3076
  311.4 16.5 %copy-start.12 = (f32[32]{0:T(128)S(1)}, f32[32]{0:T(128)}, u32[]{:S(2)}) copy-start(f32[32]{0:T(128)} %exp.8) | copy-start | bytes 388
  322.6 6.9 %collective-permute-start.4 = (bf16[256,128]{1,0:T(8,128)(2,1)S(1)}, bf16[256,128]{1,0:T(8,128)(2,1)S(1)}, u32[]{:S(2)}, u32[]{:S(2)}) collective-permute-start(bf16[256,128]{1,0:T(8,128)(2,1)S(1)} %slice.40), channel_id=1, source_target_pairs={{0,3},{1,0},{2,1},{3,2},{4,7},{5,4},{6,5},{7,6},{8,11},{9,8},{10,9... | collective-permute-start | bytes 196616 | tf_op jit(solution)/shard_map/ppermute | solution.py:29
  325.2 4.7 %collective-permute-start.5 = (bf16[256,128]{1,0:T(8,128)(2,1)S(1)}, bf16[256,128]{1,0:T(8,128)(2,1)S(1)}, u32[]{:S(2)}, u32[]{:S(2)}) collective-permute-start(bf16[256,128]{1,0:T(8,128)(2,1)S(1)} %slice.40), channel_id=1, source_target_pairs={{0,2},{1,3},{2,0},{3,1},{4,6},{5,7},{6,4},{7,5},{8,10},{9,11},{10,... | collective-permute-start | bytes 196616 | tf_op jit(solution)/shard_map/ppermute | solution.py:29
  325.2 6.1 %collective-permute-start.6 = (bf16[256,128]{1,0:T(8,128)(2,1)S(1)}, bf16[256,128]{1,0:T(8,128)(2,1)S(1)}, u32[]{:S(2)}, u32[]{:S(2)}) collective-permute-start(bf16[256,128]{1,0:T(8,128)(2,1)S(1)} %slice.40), channel_id=1, source_target_pairs={{0,1},{1,2},{2,3},{3,0},{4,5},{5,6},{6,7},{7,4},{8,9},{9,10},{10,1... | collective-permute-start | bytes 196616 | tf_op jit(solution)/shard_map/ppermute | solution.py:29
  328.8 4.0 %copy-start.3 = (f32[2,128,32]{2,1,0:T(8,128)}, f32[2,128,32]{2,1,0:T(8,128)S(1)}, u32[]{:S(2)}) copy-start(f32[2,128,32]{2,1,0:T(8,128)S(1)} %reduce_window_sum.11.decay) | copy-start | bytes 98308
Sparse Core Ops, SparseCore 0:
  44.7 97.9 all-gather.4
  180.3 131.0 all-gather.6

commit v5 on v4

--- a/solution.py
+++ b/solution.py
@@ -389,7 +389,7 @@
         ],
         compiler_params=pltpu.CompilerParams(vmem_limit_bytes=VMEM),
         cost_estimate=pl.CostEstimate(
-            flops=400 * rows * cols * slots * PAGE,
+            flops=280 * rows * cols * slots * PAGE,
             bytes_accessed=members * slots * PAGE * 4 * HD,
             transcendentals=rows * heads * slots * PAGE,
         ),

time: 353 us -> 284 us (0.80)
  waiting for transfers between devices: 227 us -> 152 us
    all_gather x1, waiting for transfers between devices: 107 us -> 54.8 us  [body(): weights = lax.all_gather(weights, ('y', 'core'), axis=0)]
    all_to_all x1, waiting for transfers between devices: 117 us -> 69.7 us  [body(): kv_in = lax.all_to_all(kv_out, DP, split_axis=0, concat_axis=0, tiled=True)]
    all_gather x1, waiting for transfers between devices: 0.01 us -> 25.3 us  [body(): weights = lax.all_gather(weights, 'z', axis=0)]
  transfers between devices with their start and end apart: 11 -> 11, of which waited for: 4 -> 5; matrix products, arithmetic and copies ran while one was open for 3% -> 3% of each run, Pallas kernels for 13% -> 17%
where the time goes in v5:
time: 284 us; the launch traced here: 280 us
  waiting for transfers between devices  152 us (54%)
  Pallas kernels  53.7 us (19%)
  starting transfers between devices  22.6 us (8%)
  blocking collectives  22.4 us (8%)
  between operations  14.2 us (5%)
  local copies, waits for them, and re-layouts  9.33 us (3%)
  other arithmetic  5.86 us (2%)
    all_to_all x1, waiting for transfers between devices, body(): kv_in = lax.all_to_all(kv_out, DP, split_axis=0, concat_axis=0, tiled=True)  69.7 us
    all_gather x1, waiting for transfers between devices, body(): weights = lax.all_gather(weights, ('y', 'core'), axis=0)  54.8 us
    all_gather x1, waiting for transfers between devices, body(): weights = lax.all_gather(weights, 'z', axis=0)  25.3 us
    all_to_all x1, blocking collectives, body(): picks = lax.all_to_all(asks, DP, split_axis=0, concat_axis=0, tiled=True)  22.4 us
    pallas_call x1, Pallas kernels, attend(): pl.pallas_call(attend_kernel, out_shape=jax.ShapeDtypeStruct((rows, cols)...  19.3 us
    pallas_call x2, Pallas kernels, pack_pages(): pl.pallas_call(functools.partial(pack_kernel, column), out_shape=jax.Shap...  11.6 us
    pallas_call x1, Pallas kernels, project(): pl.pallas_call(project_kernel, out_shape=(jax.ShapeDtypeStruct((rows, mai...  10.2 us
    ppermute x7, starting transfers between devices, around_x(): lax.ppermute(array, 'tensor', [(i, (i + by) % NX) for i in range(NX)])  9.82 us
  transfers between devices with their start and end apart: 11, of which 5 were waited for; matrix products, arithmetic and copies ran while one was open for 3% of the time, Pallas kernels for 17%

profile of v5, /device:TPU:1, one launch (start us, length us, event | category | flops | bytes accessed | tf_op | source)
XLA Modules:
  0.0 280.2 jit_solution(16605545673065197672)
XLA Ops:
  7.2 0.7 and_select_fusion
  7.9 0.1 slice.29
  8.0 0.1 broadcast_in_dim.40
  8.1 0.1 slice.28.sources
  8.1 0.1 eq.41
  8.2 0.1 eq.37
  8.3 0.1 broadcast_in_dim.37
  8.4 0.1 select_reduce_fusion.1
  8.5 0.1 select_reduce_fusion
  8.6 0.1 copy.37
  8.7 0.8 copy.47
  9.5 1.7 fusion.1
  11.2 22.4 %all_to_all.15.picks = s32[64,1,128]{2,1,0:T(1,128)} all-to-all(s32[64,1,128]{2,1,0:T(1,128)S(1)} %bitcast.29), channel_id=1, replica_groups=mesh['y'=4,'z'=8,'core'=2,'tensor'=4] {'y','z','core'}, dimensions={0} | all-to-all | bytes 65536 | tf_op jit(solution)/shard_map/all_to_all | solution.py:446
  33.6 4.8 %pack_pages.2 = bf16[64,128,256]{2,1,0:T(8,128)(2,1)} custom-call(s32[64,1,128]{2,1,0:T(1,128)} %all_to_all.15.picks, bf16[96,128,256]{2,1,0:T(8,128)(2,1)} %pool.2), custom_call_target="tpu_custom_call" | custom-call | tf_op jit(solution)/shard_map/pack_pages/pallas_call | solution.py:58
  38.4 5.5 %all-to-all-start.2 = ((bf16[64,128,256]{2,1,0:T(8,128)(2,1)}), bf16[64,128,256]{2,1,0:T(8,128)(2,1)}, u32[]{:S(2)}, u32[]{:S(2)}) async-start(bf16[64,128,256]{2,1,0:T(8,128)(2,1)} %pack_pages.2), calls=%async_computation.2 | async-start | bytes 8388608 | tf_op jit(solution)/shard_map/all_to_all | solution.py:448
  44.0 25.3 %all-gather.5.cloned.1.call-done = bf16[512,2304]{1,0:T(8,128)(2,1)} async-done(((bf16[64,2304]{1,0:T(8,128)(2,1)}), bf16[512,2304]{1,0:T(8,128)(2,1)}) %all-gather.5.cloned.1.call-update) | async-done | bytes 2359312 | tf_op jit(solution)/shard_map/all_gather | solution.py:445
  69.3 6.9 %pack_pages.3 = bf16[64,128,256]{2,1,0:T(8,128)(2,1)} custom-call(s32[64,1,128]{2,1,0:T(1,128)} %all_to_all.15.picks, bf16[96,128,256]{2,1,0:T(8,128)(2,1)} %pool.2), custom_call_target="tpu_custom_call" | custom-call | bytes 838860800 | tf_op jit(solution)/shard_map/pack_pages/pallas_call | solution.py:58
  76.2 69.7 %all-to-all-done.2.incoming = bf16[64,128,256]{2,1,0:T(8,128)(2,1)} async-done(((bf16[64,128,256]{2,1,0:T(8,128)(2,1)}), bf16[64,128,256]{2,1,0:T(8,128)(2,1)}, u32[]{:S(2)}, u32[]{:S(2)}) %all-to-all-start.2) | async-done | bytes 4194336 | tf_op jit(solution)/shard_map/all_to_all | solution.py:448
  145.9 2.4 collective-permute-start.1
  148.3 0.5 exp.8
  149.0 0.7 broadcast_in_dim_reshape.3.gain
  149.6 0.1 compare_convert_fusion
  149.7 0.8 copy.43.live
  150.5 7.2 %all-to-all-start.1 = ((bf16[64,128,256]{2,1,0:T(8,128)(2,1)}), bf16[64,128,256]{2,1,0:T(8,128)(2,1)}, u32[]{:S(2)}, u32[]{:S(2)}) async-start(bf16[64,128,256]{2,1,0:T(8,128)(2,1)} %pack_pages.3), calls=%async_computation.1 | async-start | bytes 8388608 | tf_op jit(solution)/shard_map/all_to_all | solution.py:451
  157.7 0.8 collective-permute-done.1.refs_2_
  158.5 0.8 copy-done
  159.3 0.7 slice.36
  160.1 3.5 %collective-permute-start.3 = (bf16[128,1024]{1,0:T(8,128)(2,1)}, bf16[128,1024]{1,0:T(8,128)(2,1)}, u32[]{:S(2)}, u32[]{:S(2)}) collective-permute-start(bf16[128,1024]{1,0:T(8,128)(2,1)} %slice.36), channel_id=1, source_target_pairs={{0,3},{1,0},{2,1},{3,2},{4,7},{5,4},{6,5},{7,6},{8,11},{9,8},{10,9... | collective-permute-start | bytes 786440 | tf_op jit(solution)/shard_map/ppermute | solution.py:29
  163.6 0.8 copy-done.1
  164.4 0.7 slice.35
  165.2 19.3 %attend.1 = bf16[256,1024]{1,0:T(8,128)(2,1)} custom-call(s32[2,32]{1,0:T(2,128)} %copy-done.7, s32[2]{0:T(128)} %prefix.1, bf16[256,1024]{1,0:T(8,128)(2,1)} %queries.1, bf16[256,256]{1,0:T(8,128)(2,1)} %fresh.1, f32[256,1]{1,0:T(8,128)} %copy.43.live, bf16[64,128,256]{2,1,0:T(8,128)(2,1)} %all-to-all-done.2.incoming), custom_call_target="tpu_custom_call" | custom-call | flops 300647710720 | bytes 4194304 | tf_op jit(solution)/shard_map/attend/pallas_call | solution.py:378
  184.5 54.8 %all-gather.7.cloned.1.call-done = bf16[64,64,2304]{2,1,0:T(8,128)(2,1)} async-done(((bf16[8,64,2304]{2,1,0:T(8,128)(2,1)}), bf16[64,64,2304]{2,1,0:T(8,128)(2,1)}) %all-gather.7.cloned.1.call-update) | async-done | bytes 18874384 | tf_op jit(solution)/shard_map/all_gather | solution.py:454
  239.3 10.2 %project.1 = (bf16[256,2048]{1,0:T(8,128)(2,1)}, f32[256,256]{1,0:T(8,128)}) custom-call(s32[1]{0:T(128)} %bitcast.4.x, bf16[4,2,8,64,2304]{4,3,2,1,0:T(8,128)(2,1)} %bitcast.26, bf16[256,1024]{1,0:T(8,128)(2,1)} %refs_0_, bf16[256,1024]{1,0:T(8,128)(2,1)} %copy-done.1, bf16[256,1024]{1,0:T(8,128)(2,1)} %copy-done, ...), custom_call_target="tpu_custom_call" | custom-call | flops 4831838208 | bytes 20971520 | tf_op jit(solution)/shard_map/project/pallas_call | solution.py:134
  249.6 0.9 slice.40
  250.5 2.2 collective-permute-start.4
  252.7 1.4 collective-permute-start.5
  254.1 0.3 collective-permute-start.6
  254.4 1.0 compare_select_fusion
  255.4 0.9 slice_bitcast_fusion
  256.4 0.6 multiply_bitcast_fusion
  257.0 0.1 copy.41
  257.1 0.2 reduce_window_sum.11.decay
  257.3 0.7 copy.42
  258.0 1.4 collective-permute-done.6
  259.5 0.7 pad_maximum_fusion.2.b_values
  260.1 0.7 pad_maximum_fusion.1.c_values
  260.8 7.4 %mix_locally.1 = (f32[256,2048]{1,0:T(8,128)}, f32[256,2048]{1,0:T(8,128)}) custom-call(bf16[256,2048]{1,0:T(8,128)(2,1)} %get-tuple-element.23.inner, bf16[256,256]{1,0:T(8,128)(2,1)} %pad_maximum_fusion.2.b_values, bf16[256,256]{1,0:T(8,128)(2,1)} %pad_maximum_fusion.1.c_values, f32[2,128,32]{2,1,0:T(8,128)} %copy-done.3, f32[2,32,128]{2,1,0:T(8,128)} %bitcast.33, ...), custom_call_target="tpu_custom_call" | custom-call | flops 536870912 | bytes 3145728 | tf_op jit(solution)/shard_map/mix_locally/pallas_call | solution.py:197
  268.2 5.2 %carry_state.1 = bf16[256,2048]{1,0:T(8,128)(2,1)} custom-call(s32[2,16]{1,0:T(2,128)} %bitcast.35, bf16[64,128,256]{2,1,0:T(8,128)(2,1)} %all-to-all-done.1.incoming, bf16[256,256]{1,0:T(8,128)(2,1)} %pad_maximum_fusion.1.c_values, f32[256,2048]{1,0:T(8,128)} %get-tuple-element.24.factor, f32[256,2048]{1,0:T(8,128)} %get-tuple-element.25.local), custom_call_target="tpu_custom_call" | custom-call | flops 268435456 | bytes 4194304 | tf_op jit(solution)/shard_map/carry_state/pallas_call | solution.py:259
  (42 shorter events, 0.4 us)
Async XLA Ops:
  7.2 62.2 %all-gather.5.cloned.1.call-start = ((), (), s32[]{:S(2)}) async-start(), calls=%async_computation.3 | async-start | bytes 2654208 | tf_op jit(solution)/shard_map/all_gather | solution.py:445
  7.9 0.7 copy-start.4
  8.1 30.3 %copy-start.7 = (s32[2,32]{1,0:T(2,128)}, s32[2,32]{1,0:T(2,128)S(1)}, u32[]{:S(2)}) copy-start(s32[2,32]{1,0:T(2,128)S(1)} %slice.28.sources) | copy-start | bytes 772
  38.4 107.5 %all-to-all-start.2 = ((bf16[64,128,256]{2,1,0:T(8,128)(2,1)}), bf16[64,128,256]{2,1,0:T(8,128)(2,1)}, u32[]{:S(2)}, u32[]{:S(2)}) async-start(bf16[64,128,256]{2,1,0:T(8,128)(2,1)} %pack_pages.2), calls=%async_computation.2 | async-start | bytes 8388608 | tf_op jit(solution)/shard_map/all_to_all | solution.py:448
  44.0 195.4 %all-gather.7.cloned.1.call-start = ((), (), s32[]{:S(2)}) async-start(), calls=%async_computation.4 | async-start | bytes 21233664 | tf_op jit(solution)/shard_map/all_gather | solution.py:454
  69.3 76.6 %copy-start.2 = (bf16[256,1024]{1,0:T(8,128)(2,1)S(1)}, bf16[256,1024]{1,0:T(8,128)(2,1)}, u32[]{:S(2)}) copy-start(bf16[256,1024]{1,0:T(8,128)(2,1)} %refs_0_) | copy-start | bytes 1572868
  69.3 79.0 %copy-start.11 = (f32[32]{0:T(128)S(1)}, f32[32]{0:T(128)}, u32[]{:S(2)}) copy-start(f32[32]{0:T(128)} %param.18) | copy-start | bytes 388
  69.3 79.6 %copy-start.10 = (f32[32]{0:T(128)S(1)}, f32[32]{0:T(128)}, u32[]{:S(2)}) copy-start(f32[32]{0:T(128)} %param.19) | copy-start | bytes 388
  69.3 80.3 %copy-start.12 = (s32[2]{0:T(128)S(1)}, s32[2]{0:T(128)}, u32[]{:S(2)}) copy-start(s32[2]{0:T(128)} %param.25) | copy-start | bytes 28
  145.9 12.6 %collective-permute-start.1 = (bf16[256,1024]{1,0:T(8,128)(2,1)S(1)}, bf16[256,1024]{1,0:T(8,128)(2,1)S(1)}, u32[]{:S(2)}, u32[]{:S(2)}) collective-permute-start(bf16[256,1024]{1,0:T(8,128)(2,1)S(1)} %copy-done.2), channel_id=1, source_target_pairs={{0,3},{1,0},{2,1},{3,2},{4,7},{5,4},{6,5},{7,6},{8,11},{9,8},{10,9... | collective-permute-start | bytes 1572872 | tf_op jit(solution)/shard_map/ppermute | solution.py:29
  148.3 15.3 %collective-permute-start = (bf16[256,1024]{1,0:T(8,128)(2,1)S(1)}, bf16[256,1024]{1,0:T(8,128)(2,1)S(1)}, u32[]{:S(2)}, u32[]{:S(2)}) collective-permute-start(bf16[256,1024]{1,0:T(8,128)(2,1)S(1)} %copy-done.2), channel_id=1, source_target_pairs={{0,1},{1,2},{2,3},{3,0},{4,5},{5,6},{6,7},{7,4},{8,9},{9,10},{10,1... | collective-permute-start | bytes 1572872 | tf_op jit(solution)/shard_map/ppermute | solution.py:29
  149.7 0.8 copy-start.5
  150.5 117.7 %all-to-all-start.1 = ((bf16[64,128,256]{2,1,0:T(8,128)(2,1)}), bf16[64,128,256]{2,1,0:T(8,128)(2,1)}, u32[]{:S(2)}, u32[]{:S(2)}) async-start(bf16[64,128,256]{2,1,0:T(8,128)(2,1)} %pack_pages.3), calls=%async_computation.1 | async-start | bytes 8388608 | tf_op jit(solution)/shard_map/all_to_all | solution.py:451
  158.5 0.8 copy-start
  160.1 24.4 %collective-permute-start.3 = (bf16[128,1024]{1,0:T(8,128)(2,1)}, bf16[128,1024]{1,0:T(8,128)(2,1)}, u32[]{:S(2)}, u32[]{:S(2)}) collective-permute-start(bf16[128,1024]{1,0:T(8,128)(2,1)} %slice.36), channel_id=1, source_target_pairs={{0,3},{1,0},{2,1},{3,2},{4,7},{5,4},{6,5},{7,6},{8,11},{9,8},{10,9... | collective-permute-start | bytes 786440 | tf_op jit(solution)/shard_map/ppermute | solution.py:29
  163.6 0.8 copy-start.1
  165.2 19.3 %collective-permute-start.2 = (bf16[128,1024]{1,0:T(8,128)(2,1)}, bf16[128,1024]{1,0:T(8,128)(2,1)}, u32[]{:S(2)}, u32[]{:S(2)}) collective-permute-start(bf16[128,1024]{1,0:T(8,128)(2,1)} %slice.35), channel_id=1, source_target_pairs={{0,1},{1,2},{2,3},{3,0},{4,5},{5,6},{6,7},{7,4},{8,9},{9,10},{10,1... | collective-permute-start | bytes 786440 | tf_op jit(solution)/shard_map/ppermute | solution.py:29
  239.3 15.1 %copy-start.8 = (f32[32]{0:T(128)S(1)}, f32[32]{0:T(128)}, u32[]{:S(2)}) copy-start(f32[32]{0:T(128)} %param.17) | copy-start | bytes 388
  239.3 17.0 %copy-start.6 = (f32[2,128]{1,0:T(2,128)S(1)}, f32[2,128]{1,0:T(2,128)}, u32[]{:S(2)}) copy-start(f32[2,128]{1,0:T(2,128)} %copy-done.5) | copy-start | bytes 3076
  239.3 17.0 %copy-start.9 = (f32[32]{0:T(128)S(1)}, f32[32]{0:T(128)}, u32[]{:S(2)}) copy-start(f32[32]{0:T(128)} %exp.8) | copy-start | bytes 388
  250.5 7.5 %collective-permute-start.4 = (bf16[256,128]{1,0:T(8,128)(2,1)S(1)}, bf16[256,128]{1,0:T(8,128)(2,1)S(1)}, u32[]{:S(2)}, u32[]{:S(2)}) collective-permute-start(bf16[256,128]{1,0:T(8,128)(2,1)S(1)} %slice.40), channel_id=1, source_target_pairs={{0,3},{1,0},{2,1},{3,2},{4,7},{5,4},{6,5},{7,6},{8,11},{9,8},{10,9... | collective-permute-start | bytes 196616 | tf_op jit(solution)/shard_map/ppermute | solution.py:29
  252.7 5.3 %collective-permute-start.5 = (bf16[256,128]{1,0:T(8,128)(2,1)S(1)}, bf16[256,128]{1,0:T(8,128)(2,1)S(1)}, u32[]{:S(2)}, u32[]{:S(2)}) collective-permute-start(bf16[256,128]{1,0:T(8,128)(2,1)S(1)} %slice.40), channel_id=1, source_target_pairs={{0,2},{1,3},{2,0},{3,1},{4,6},{5,7},{6,4},{7,5},{8,10},{9,11},{10,... | collective-permute-start | bytes 196616 | tf_op jit(solution)/shard_map/ppermute | solution.py:29
  254.1 5.3 %collective-permute-start.6 = (bf16[256,128]{1,0:T(8,128)(2,1)S(1)}, bf16[256,128]{1,0:T(8,128)(2,1)S(1)}, u32[]{:S(2)}, u32[]{:S(2)}) collective-permute-start(bf16[256,128]{1,0:T(8,128)(2,1)S(1)} %slice.40), channel_id=1, source_target_pairs={{0,1},{1,2},{2,3},{3,0},{4,5},{5,6},{6,7},{7,4},{8,9},{9,10},{10,1... | collective-permute-start | bytes 196616 | tf_op jit(solution)/shard_map/ppermute | solution.py:29
  257.3 3.5 %copy-start.3 = (f32[2,128,32]{2,1,0:T(8,128)}, f32[2,128,32]{2,1,0:T(8,128)S(1)}, u32[]{:S(2)}) copy-start(f32[2,128,32]{2,1,0:T(8,128)S(1)} %reduce_window_sum.11.decay) | copy-start | bytes 98308
Sparse Core Ops, SparseCore 0:
  11.4 57.9 all-gather.4
  76.3 162.9 all-gather.6

commit v6 on v3

--- a/solution.py
+++ b/solution.py
@@ -17,6 +17,8 @@
 NY = 4
 NZ = 8
 NX = 4
+TILE = 256
+EARLY = 768
 DP = ("y", "z", "core")
 VMEM = 62 * 1024 * 1024
 ANY = pl.BlockSpec(memory_space=pl.ANY)
@@ -73,9 +75,10 @@
     )(picks, pool)
 
 
-def project_kernel(x, weights, *refs):
+def project_kernel(raw, x, weights, *refs):
     pieces = refs[:5]
-    main_out, extra_out, w_all, t_all, w_sems, t_sems = refs[5:]
+    outs = refs[5 : 6 + raw]
+    w_all, t_all, w_sems, t_sems = refs[6 + raw :]
     tiles, wide = w_all.shape[0], w_all.shape[5]
     depth = t_all.shape[1]
     cols = pieces[0].shape[1]
@@ -117,37 +120,37 @@
         tile = w_all[n].reshape(depth, wide)
         return jnp.dot(t_all[...], tile, preferred_element_type=jnp.float32)
 
-    def main_tile(n, carry):
+    def gated(n, carry):
         total = product(n)
         value = total / (1.0 + jnp.exp(-total))
-        main_out[:, pl.ds(pl.multiple_of(n * wide, wide), wide)] = value.astype(jnp.bfloat16)
+        outs[0][:, pl.ds(pl.multiple_of(n * wide, wide), wide)] = value.astype(jnp.bfloat16)
         return carry
 
-    lax.fori_loop(0, tiles - 1, main_tile, 0)
-    extra_out[...] = product(tiles - 1)
-
-
-def project(x, weights, pieces, rows, wide):
+    lax.fori_loop(0, tiles - raw, gated, 0)
+    if raw:
+        outs[1][...] = product(tiles - 1)
+
+
+def project(x, weights, pieces, rows, raw):
     cols = weights.shape[-1]
     depth = weights.size // cols
-    main = cols - wide
+    shapes = [jax.ShapeDtypeStruct((rows, cols - raw * TILE), jnp.bfloat16)]
+    if raw:
+        shapes.append(jax.ShapeDtypeStruct((rows, TILE), jnp.float32))
     return pl.pallas_call(
-        project_kernel,
-        out_shape=(
-            jax.ShapeDtypeStruct((rows, main), jnp.bfloat16),
-            jax.ShapeDtypeStruct((rows, wide), jnp.float32),
-        ),
+        functools.partial(project_kernel, raw),
+        out_shape=tuple(shapes),
         in_specs=[SCALARS, HBM] + [ANY] * 5,
-        out_specs=(WHOLE,) * 2,
+        out_specs=(WHOLE,) * len(shapes),
         scratch_shapes=[
-            pltpu.VMEM((cols // wide, NY, NZ, 2, depth // (2 * NY * NZ), wide), jnp.bfloat16),
+            pltpu.VMEM((cols // TILE, NY, NZ, 2, depth // (2 * NY * NZ), TILE), jnp.bfloat16),
             pltpu.VMEM((rows, depth), jnp.bfloat16),
-            pltpu.SemaphoreType.DMA((cols // wide, 2 * NY)),
+            pltpu.SemaphoreType.DMA((cols // TILE, 2 * NY)),
             pltpu.SemaphoreType.DMA((5,)),
         ],
         compiler_params=pltpu.CompilerParams(vmem_limit_bytes=VMEM),
         cost_estimate=pl.CostEstimate(
-            flops=2 * rows * depth * cols, bytes_accessed=2 * depth * (cols + rows), transcendentals=rows * main
+            flops=2 * rows * depth * cols, bytes_accessed=2 * depth * (cols + rows), transcendentals=rows * cols
         ),
         name="project",
     )(x, weights, *pieces)
@@ -161,7 +164,7 @@
     )
 
 
-def local_kernel(inner, b_values, c_values, decay, decay_t, step_t, gain, live, out, factor):
+def local_kernel(inner_a, inner_b, b_values, c_values, decay, decay_t, step_t, gain, live, out, factor):
     length = PAGE
     row = lax.broadcasted_iota(jnp.int32, (length, length), 0)
     column = lax.broadcasted_iota(jnp.int32, (length, length), 1)
@@ -178,7 +181,10 @@
         fades = jnp.exp(decay[member])
         for pair in range(decay.shape[2] // 2):
             lanes = slice(pair * 2 * HP, (pair + 1) * 2 * HP)
-            values = inner[rows, lanes]
+            if pair * 2 * HP < EARLY:
+                values = inner_a[rows, lanes]
+            else:
+                values = inner_b[rows, pair * 2 * HP - EARLY : (pair + 1) * 2 * HP - EARLY]
             parts = []
             for head in (2 * pair, 2 * pair + 1):
                 gaps = decay[member, :, head : head + 1] - decay_t[member, head : head + 1, :]
@@ -192,19 +198,19 @@
             factor[rows, lanes] = fade * live[rows, :]
 
 
-def mix_locally(inner, b_values, c_values, decay, decay_t, step_t, gain, live):
-    rows, cols = inner.shape
+def mix_locally(inner_a, inner_b, b_values, c_values, decay, decay_t, step_t, gain, live):
+    rows, cols = inner_a.shape[0], gain.shape[1]
     return pl.pallas_call(
         local_kernel,
         out_shape=(jax.ShapeDtypeStruct((rows, cols), jnp.float32),) * 2,
-        in_specs=[WHOLE] * 8,
+        in_specs=[WHOLE] * 9,
         out_specs=(WHOLE,) * 2,
         compiler_params=pltpu.CompilerParams(vmem_limit_bytes=VMEM),
         cost_estimate=pl.CostEstimate(
             flops=8 * rows * PAGE * cols, bytes_accessed=6 * rows * cols, transcendentals=rows * PAGE * 32
         ),
         name="mix_locally",
-    )(inner, b_values, c_values, decay, decay_t, step_t, gain, live)
+    )(inner_a, inner_b, b_values, c_values, decay, decay_t, step_t, gain, live)
 
 
 def carry_kernel(
@@ -441,8 +447,9 @@
         (x_weight, bc_weight, step_weight, asks)
     )
     step_wide = jnp.pad(step_weight, ((0, 0), (0, extra - heads)))
-    weights = jnp.concatenate([x_weight, bc_weight, step_wide], axis=1)
-    weights = lax.all_gather(weights, "z", axis=0)
+    part_a = jnp.concatenate([x_weight[:, :EARLY], bc_weight, step_wide], axis=1)
+    part_a = lax.all_gather(part_a, "z", axis=0)
+    part_b = lax.all_gather(x_weight[:, EARLY:], "z", axis=0)
     picks = lax.all_to_all(asks, DP, split_axis=0, concat_axis=0, tiled=True)
     kv_out = pack_pages(picks, 0, page_pool)
     kv_in = lax.all_to_all(kv_out, DP, split_axis=0, concat_axis=0, tiled=True)
@@ -450,13 +457,14 @@
     state_out = pack_pages(picks, 1, later_pool)
     state_in = lax.all_to_all(state_out, DP, split_axis=0, concat_axis=0, tiled=True)
 
-    weights, _ = lax.optimization_barrier((weights, state_out))
-    weights = lax.all_gather(weights, ("y", "core"), axis=0)
-    weights = weights.reshape((NY, 2) + weights.shape[1:])
-    tokens, _ = lax.optimization_barrier((tokens, kv_out))
-    inner, extras = project(
-        x.reshape(1).astype(jnp.int32), weights, gather_tokens(tokens), rows, 2 * extra
-    )
+    part_a, _ = lax.optimization_barrier((part_a, kv_out))
+    part_a = lax.all_gather(part_a, ("y", "core"), axis=0)
+    part_b, tokens, _, _ = lax.optimization_barrier((part_b, tokens, kv_in, state_out))
+    part_b = lax.all_gather(part_b, ("y", "core"), axis=0)
+    pieces = gather_tokens(tokens)
+    at = x.reshape(1).astype(jnp.int32)
+    inner_a, extras = project(at, part_a.reshape((NY, 2) + part_a.shape[1:]), pieces, rows, 1)
+    (inner_b,) = project(at, part_b.reshape((NY, 2) + part_b.shape[1:]), pieces, rows, 0)
     columns = extras[:, :extra].astype(jnp.bfloat16)
     step_raw = extras[:, extra : extra + heads]
     around = jnp.stack([columns] + [around_x(columns, -k) for k in range(1, NX)])
@@ -471,7 +479,7 @@
     gain = jnp.repeat(skip_gain, HP)[None, :]
     live_column = live.reshape(rows, 1)
     local, factor = mix_locally(
-        inner, b_values, c_values, decay, decay.transpose(0, 2, 1), step.transpose(0, 2, 1), gain, live_column
+        inner_a, inner_b, b_values, c_values, decay, decay.transpose(0, 2, 1), step.transpose(0, 2, 1), gain, live_column
     )
     attention_out = attend(
         sources[:, SP:], prefix_pages, queries, new_keyvals, live_column, kv_in

time: 276 us -> 317 us (1.15)
  waiting for transfers between devices: 51.4 us -> 178 us
  blocking collectives: 130 us -> 22.4 us
  starting transfers between devices: 16 us -> 26.8 us
  Pallas kernels: 51.7 us -> 59.4 us
  local copies, waits for them, and re-layouts: 6.43 us -> 9.72 us
    all_to_all x1 -> x0, blocking collectives: 107 us -> none  [body(): kv_in = lax.all_to_all(kv_out, DP, split_axis=0, concat_axis=0, tiled=True)]
    all_gather x2 -> x4, waiting for transfers between devices: 18.8 us -> 112 us  [the longest x1 55.6 us: body(): part_b = lax.all_gather(part_b, ('y', 'core'), axis=0)]
    all_to_all x0 -> x1, waiting for transfers between devices: none -> 54.5 us  [body(): kv_in = lax.all_to_all(kv_out, DP, split_axis=0, concat_axis=0, tiled=True)]
    all_to_all x1, waiting for transfers between devices: 21.8 us -> 0.01 us  [body(): lax.all_to_all(state_out, DP, split_axis=0, concat_axis=0, tiled=True)]
    all_to_all x0 -> x1, starting transfers between devices: none -> 12.3 us  [body(): kv_in = lax.all_to_all(kv_out, DP, split_axis=0, concat_axis=0, tiled=True)]
    pallas_call x1 -> x2, Pallas kernels: 10.3 us -> 14.1 us  [project(): pl.pallas_call(functools.partial(project_kernel, raw), out_shape=tuple(sh...]
    pallas_call x1, Pallas kernels: 17.4 us -> 21.2 us  [attend(): pl.pallas_call(attend_kernel, out_shape=jax.ShapeDtypeStruct((rows, cols)...]
  transfers between devices with their start and end apart: 10 -> 13, of which waited for: 5 -> 6; matrix products, arithmetic and copies ran while one was open for 3% -> 3% of each run, Pallas kernels for 17% -> 17%
where the time goes in v6:
time: 317 us; the launch traced here: 316 us
  waiting for transfers between devices  178 us (56%)
  Pallas kernels  59.4 us (19%)
  starting transfers between devices  26.8 us (8%)
  blocking collectives  22.4 us (7%)
  between operations  14 us (4%)
  local copies, waits for them, and re-layouts  9.72 us (3%)
  other arithmetic  5.5 us (2%)
    all_gather x1, waiting for transfers between devices, body(): part_b = lax.all_gather(part_b, ('y', 'core'), axis=0)  55.6 us
    all_to_all x1, waiting for transfers between devices, body(): kv_in = lax.all_to_all(kv_out, DP, split_axis=0, concat_axis=0, tiled=True)  54.5 us
    all_gather x1, waiting for transfers between devices, body(): part_b = lax.all_gather(x_weight[:, EARLY:], 'z', axis=0)  46.8 us
    all_to_all x1, blocking collectives, body(): picks = lax.all_to_all(asks, DP, split_axis=0, concat_axis=0, tiled=True)  22.4 us
    pallas_call x1, Pallas kernels, attend(): pl.pallas_call(attend_kernel, out_shape=jax.ShapeDtypeStruct((rows, cols)...  21.2 us
    pallas_call x2, Pallas kernels, project(): pl.pallas_call(functools.partial(project_kernel, raw), out_shape=tuple(sh...  14.1 us
    all_to_all x1, starting transfers between devices, body(): kv_in = lax.all_to_all(kv_out, DP, split_axis=0, concat_axis=0, tiled=True)  12.3 us
    pallas_call x2, Pallas kernels, pack_pages(): pl.pallas_call(functools.partial(pack_kernel, column), out_shape=jax.Shap...  11.6 us
  transfers between devices with their start and end apart: 13, of which 6 were waited for; matrix products, arithmetic and copies ran while one was open for 3% of the time, Pallas kernels for 17%

profile of v6, /device:TPU:1, one launch (start us, length us, event | category | flops | bytes accessed | tf_op | source)
XLA Modules:
  0.0 315.9 jit_solution(12000855079866858869)
XLA Ops:
  7.2 0.7 and_select_fusion
  7.9 0.1 slice.34.sources
  8.0 0.1 eq.37
  8.1 0.1 slice.35
  8.1 0.1 broadcast_in_dim.37
  8.2 0.1 eq.41
  8.3 0.1 broadcast_in_dim.40
  8.4 0.1 select_reduce_fusion
  8.5 0.1 select_reduce_fusion.1
  8.6 0.1 copy.37
  8.7 0.9 slice.37
  9.6 0.8 copy.47
  10.4 1.4 fusion.1
  11.9 1.6 slice.38
  13.5 22.4 %all_to_all.15.picks = s32[64,1,128]{2,1,0:T(1,128)} all-to-all(s32[64,1,128]{2,1,0:T(1,128)S(1)} %bitcast.33), channel_id=1, replica_groups=mesh['y'=4,'z'=8,'core'=2,'tensor'=4] {'y','z','core'}, dimensions={0} | all-to-all | bytes 65536 | tf_op jit(solution)/shard_map/all_to_all | solution.py:453
  35.9 4.8 %pack_pages.2 = bf16[64,128,256]{2,1,0:T(8,128)(2,1)} custom-call(s32[64,1,128]{2,1,0:T(1,128)} %all_to_all.15.picks, bf16[96,128,256]{2,1,0:T(8,128)(2,1)} %pool.2), custom_call_target="tpu_custom_call" | custom-call | bytes 8388608 | tf_op jit(solution)/shard_map/pack_pages/pallas_call | solution.py:60
  40.7 9.7 %all-gather.9.cloned.1.call-done = bf16[512,1024]{1,0:T(8,128)(2,1)} async-done(((bf16[64,1024]{1,0:T(8,128)(2,1)}), bf16[512,1024]{1,0:T(8,128)(2,1)}) %all-gather.9.cloned.1.call-update) | async-done | bytes 1048592 | tf_op jit(solution)/shard_map/all_gather | solution.py:451
  50.4 12.3 %all-to-all-start.2 = ((bf16[64,128,256]{2,1,0:T(8,128)(2,1)}), bf16[64,128,256]{2,1,0:T(8,128)(2,1)}, u32[]{:S(2)}, u32[]{:S(2)}) async-start(bf16[64,128,256]{2,1,0:T(8,128)(2,1)} %pack_pages.2), calls=%async_computation.2 | async-start | bytes 8388608 | tf_op jit(solution)/shard_map/all_to_all | solution.py:455
  62.8 6.8 %pack_pages.3 = bf16[64,128,256]{2,1,0:T(8,128)(2,1)} custom-call(s32[64,1,128]{2,1,0:T(1,128)} %all_to_all.15.picks, bf16[96,128,256]{2,1,0:T(8,128)(2,1)} %pool.2), custom_call_target="tpu_custom_call" | custom-call | bytes 8388608 | tf_op jit(solution)/shard_map/pack_pages/pallas_call | solution.py:60
  69.6 46.8 %all-gather.13.cloned.1.call-done = bf16[512,1280]{1,0:T(8,128)(2,1)} async-done(((bf16[64,1280]{1,0:T(8,128)(2,1)}), bf16[512,1280]{1,0:T(8,128)(2,1)}) %all-gather.13.cloned.1.call-update) | async-done | bytes 1310736 | tf_op jit(solution)/shard_map/all_gather | solution.py:452
  116.4 54.5 %all-to-all-done.2.incoming = bf16[64,128,256]{2,1,0:T(8,128)(2,1)} async-done(((bf16[64,128,256]{2,1,0:T(8,128)(2,1)}), bf16[64,128,256]{2,1,0:T(8,128)(2,1)}, u32[]{:S(2)}, u32[]{:S(2)}) %all-to-all-start.2) | async-done | bytes 4194336 | tf_op jit(solution)/shard_map/all_to_all | solution.py:455
  171.0 6.2 %all-to-all-start.1 = ((bf16[64,128,256]{2,1,0:T(8,128)(2,1)}), bf16[64,128,256]{2,1,0:T(8,128)(2,1)}, u32[]{:S(2)}, u32[]{:S(2)}) async-start(bf16[64,128,256]{2,1,0:T(8,128)(2,1)} %pack_pages.3), calls=%async_computation.1 | async-start | bytes 8388608 | tf_op jit(solution)/shard_map/all_to_all | solution.py:458
  177.2 1.3 collective-permute-start
  178.5 1.5 collective-permute-start.1
  180.0 0.8 copy.43.live
  180.9 0.7 broadcast_in_dim_reshape.3.gain
  181.6 10.0 %collective-permute-done.refs_1_ = bf16[256,1024]{1,0:T(8,128)(2,1)S(1)} collective-permute-done((bf16[256,1024]{1,0:T(8,128)(2,1)S(1)}, bf16[256,1024]{1,0:T(8,128)(2,1)S(1)}, u32[]{:S(2)}, u32[]{:S(2)}) %collective-permute-start) | collective-permute-done | bytes 524320 | tf_op jit(solution)/shard_map/ppermute | solution.py:31
  191.5 0.8 slice.43
  192.3 2.7 collective-permute-start.3
  195.1 21.2 %attend.1 = bf16[256,1024]{1,0:T(8,128)(2,1)} custom-call(s32[2,32]{1,0:T(2,128)} %copy-done.7, s32[2]{0:T(128)} %prefix.1, bf16[256,1024]{1,0:T(8,128)(2,1)} %queries.1, bf16[256,256]{1,0:T(8,128)(2,1)} %fresh.1, f32[256,1]{1,0:T(8,128)} %copy.43.live, bf16[64,128,256]{2,1,0:T(8,128)(2,1)} %all-to-all-done.2.incoming), custom_call_target="tpu_custom_call" | custom-call | flops 4294967296 | bytes 4194304 | tf_op jit(solution)/shard_map/attend/pallas_call | solution.py:384
  216.4 0.7 copy-done.3
  217.0 0.1 copy-done.4
  217.1 7.0 %project.2 = (bf16[256,768]{1,0:T(8,128)(2,1)}, f32[256,256]{1,0:T(8,128)}) custom-call(s32[1]{0:T(128)} %bitcast.3.x, bf16[4,2,8,64,1024]{4,3,2,1,0:T(8,128)(2,1)} %bitcast.29, bf16[256,1024]{1,0:T(8,128)(2,1)} %refs_0_.1, bf16[256,1024]{1,0:T(8,128)(2,1)} %copy-done, bf16[256,1024]{1,0:T(8,128)(2,1)} %copy-done.1, bf16[128,1024]{1,0:T(8,128)(2,1)} %copy-done.3, ...), custom_call_target="tpu_custom_call" | custom-call | flops 2147483648 | bytes 10485760 | tf_op jit(solution)/shard_map/project/pallas_call | solution.py:140
  224.2 0.9 slice.48
  225.1 2.7 collective-permute-start.4
  227.8 1.0 compare_select_fusion
  228.8 0.9 slice_bitcast_fusion
  229.8 0.6 multiply_bitcast_fusion
  230.4 0.1 copy.41
  230.5 0.2 reduce_window_sum.11.decay
  230.7 0.7 copy.42
  231.4 1.4 collective-permute-done.5
  232.9 0.7 pad_maximum_fusion.2.b_values
  233.5 0.7 pad_maximum_fusion.1.c_values
  234.2 55.6 %all-gather.15.cloned.1.call-done = bf16[64,64,1280]{2,1,0:T(8,128)(2,1)} async-done(((bf16[8,64,1280]{2,1,0:T(8,128)(2,1)}), bf16[64,64,1280]{2,1,0:T(8,128)(2,1)}) %all-gather.15.cloned.1.call-update) | async-done | bytes 10485776 | tf_op jit(solution)/shard_map/all_gather | solution.py:463
  289.8 7.1 %project.3.inner_b = bf16[256,1280]{1,0:T(8,128)(2,1)} custom-call(s32[1]{0:T(128)} %bitcast.3.x, bf16[4,2,8,64,1280]{4,3,2,1,0:T(8,128)(2,1)} %bitcast.28, bf16[256,1024]{1,0:T(8,128)(2,1)} %refs_0_.1, bf16[256,1024]{1,0:T(8,128)(2,1)} %copy-done, bf16[256,1024]{1,0:T(8,128)(2,1)} %copy-done.1, bf16[128,1024]{1,0:T(8,128)(2,1)} %copy-done.3, ...), custom_call_target="tpu_custom_call" | custom-call | flops 2684354560 | bytes 12582912 | tf_op jit(solution)/shard_map/project/pallas_call | solution.py:140
  296.9 7.3 %mix_locally.1 = (f32[256,2048]{1,0:T(8,128)}, f32[256,2048]{1,0:T(8,128)}) custom-call(bf16[256,768]{1,0:T(8,128)(2,1)} %get-tuple-element.22.inner_a, bf16[256,1280]{1,0:T(8,128)(2,1)} %project.3.inner_b, bf16[256,256]{1,0:T(8,128)(2,1)} %pad_maximum_fusion.2.b_values, bf16[256,256]{1,0:T(8,128)(2,1)} %pad_maximum_fusion.1.c_values, ...), custom_call_target="tpu_custom_call" | custom-call | flops 536870912 | bytes 3145728 | tf_op jit(solution)/shard_map/mix_locally/pallas_call | solution.py:203
  304.2 5.2 %carry_state.1 = bf16[256,2048]{1,0:T(8,128)(2,1)} custom-call(s32[2,16]{1,0:T(2,128)} %bitcast.39, bf16[64,128,256]{2,1,0:T(8,128)(2,1)} %all-to-all-done.1.incoming, bf16[256,256]{1,0:T(8,128)(2,1)} %pad_maximum_fusion.1.c_values, f32[256,2048]{1,0:T(8,128)} %get-tuple-element.24.factor, f32[256,2048]{1,0:T(8,128)} %get-tuple-element.25.local), custom_call_target="tpu_custom_call" | custom-call | flops 268435456 | bytes 4194304 | tf_op jit(solution)/shard_map/carry_state/pallas_call | solution.py:265
  (49 shorter events, 0.6 us)
Async XLA Ops:
  7.2 43.3 %all-gather.9.cloned.1.call-start = ((), (), s32[]{:S(2)}) async-start(), calls=%async_computation.3 | async-start | bytes 1179648 | tf_op jit(solution)/shard_map/all_gather | solution.py:451
  7.9 32.8 %copy-start.6 = (s32[2,48]{1,0:T(2,128)}, s32[2,48]{1,0:T(2,128)S(1)}, u32[]{:S(2)}) copy-start(s32[2,48]{1,0:T(2,128)S(1)} %get-tuple-element.33) | copy-start | bytes 1156
  8.0 32.7 %copy-start.7 = (s32[2,32]{1,0:T(2,128)}, s32[2,32]{1,0:T(2,128)S(1)}, u32[]{:S(2)}) copy-start(s32[2,32]{1,0:T(2,128)S(1)} %slice.34.sources) | copy-start | bytes 772
  11.8 104.6 %all-gather.13.cloned.1.call-start = ((), (), s32[]{:S(2)}) async-start(), calls=%async_computation.5 | async-start | bytes 1474560 | tf_op jit(solution)/shard_map/all_gather | solution.py:452
  13.5 202.9 %all-gather.11.cloned.1.call-start = ((), (), s32[]{:S(2)}) async-start(), calls=%async_computation.4 | async-start | bytes 9437184 | tf_op jit(solution)/shard_map/all_gather | solution.py:461
  50.4 120.4 %all-to-all-start.2 = ((bf16[64,128,256]{2,1,0:T(8,128)(2,1)}), bf16[64,128,256]{2,1,0:T(8,128)(2,1)}, u32[]{:S(2)}, u32[]{:S(2)}) async-start(bf16[64,128,256]{2,1,0:T(8,128)(2,1)} %pack_pages.2), calls=%async_computation.2 | async-start | bytes 8388608 | tf_op jit(solution)/shard_map/all_to_all | solution.py:455
  62.7 227.1 %all-gather.15.cloned.1.call-start = ((), (), s32[]{:S(2)}) async-start(), calls=%async_computation.6 | async-start | bytes 11796480 | tf_op jit(solution)/shard_map/all_gather | solution.py:463
  170.9 6.2 %copy-start.2 = (bf16[256,1024]{1,0:T(8,128)(2,1)S(1)}, bf16[256,1024]{1,0:T(8,128)(2,1)}, u32[]{:S(2)}) copy-start(bf16[256,1024]{1,0:T(8,128)(2,1)} %refs_0_.1) | copy-start | bytes 1572868
  170.9 9.0 %copy-start.10 = (f32[32]{0:T(128)S(1)}, f32[32]{0:T(128)}, u32[]{:S(2)}) copy-start(f32[32]{0:T(128)} %param.18) | copy-start | bytes 388
  170.9 9.0 %copy-start.11 = (s32[2]{0:T(128)S(1)}, s32[2]{0:T(128)}, u32[]{:S(2)}) copy-start(s32[2]{0:T(128)} %param.25) | copy-start | bytes 28
  170.9 9.9 %copy-start.9 = (f32[32]{0:T(128)S(1)}, f32[32]{0:T(128)}, u32[]{:S(2)}) copy-start(f32[32]{0:T(128)} %param.19) | copy-start | bytes 388
  171.0 133.2 %all-to-all-start.1 = ((bf16[64,128,256]{2,1,0:T(8,128)(2,1)}), bf16[64,128,256]{2,1,0:T(8,128)(2,1)}, u32[]{:S(2)}, u32[]{:S(2)}) async-start(bf16[64,128,256]{2,1,0:T(8,128)(2,1)} %pack_pages.3), calls=%async_computation.1 | async-start | bytes 8388608 | tf_op jit(solution)/shard_map/all_to_all | solution.py:458
  177.2 14.3 %collective-permute-start = (bf16[256,1024]{1,0:T(8,128)(2,1)S(1)}, bf16[256,1024]{1,0:T(8,128)(2,1)S(1)}, u32[]{:S(2)}, u32[]{:S(2)}) collective-permute-start(bf16[256,1024]{1,0:T(8,128)(2,1)S(1)} %copy-done.2), channel_id=1, source_target_pairs={{0,1},{1,2},{2,3},{3,0},{4,5},{5,6},{6,7},{7,4},{8,9},{9,10},{10,1... | collective-permute-start | bytes 1572872 | tf_op jit(solution)/shard_map/ppermute | solution.py:31
  178.5 13.8 %collective-permute-start.1 = (bf16[256,1024]{1,0:T(8,128)(2,1)S(1)}, bf16[256,1024]{1,0:T(8,128)(2,1)S(1)}, u32[]{:S(2)}, u32[]{:S(2)}) collective-permute-start(bf16[256,1024]{1,0:T(8,128)(2,1)S(1)} %copy-done.2), channel_id=1, source_target_pairs={{0,3},{1,0},{2,1},{3,2},{4,7},{5,4},{6,5},{7,6},{8,11},{9,8},{10,9... | collective-permute-start | bytes 1572872 | tf_op jit(solution)/shard_map/ppermute | solution.py:31
  191.5 24.8 %copy-start = (bf16[256,1024]{1,0:T(8,128)(2,1)}, bf16[256,1024]{1,0:T(8,128)(2,1)S(1)}, u32[]{:S(2)}) copy-start(bf16[256,1024]{1,0:T(8,128)(2,1)S(1)} %collective-permute-done.refs_1_) | copy-start | bytes 1572868
  192.3 24.0 %collective-permute-start.2 = (bf16[128,1024]{1,0:T(8,128)(2,1)}, bf16[128,1024]{1,0:T(8,128)(2,1)S(1)}, u32[]{:S(2)}, u32[]{:S(2)}) collective-permute-start(bf16[128,1024]{1,0:T(8,128)(2,1)} %slice.43), channel_id=1, source_target_pairs={{0,1},{1,2},{2,3},{3,0},{4,5},{5,6},{6,7},{7,4},{8,9},{9,10},{10,1... | collective-permute-start | bytes 786440 | tf_op jit(solution)/shard_map/ppermute | solution.py:31
  192.3 24.0 %copy-start.1 = (bf16[256,1024]{1,0:T(8,128)(2,1)}, bf16[256,1024]{1,0:T(8,128)(2,1)S(1)}, u32[]{:S(2)}) copy-start(bf16[256,1024]{1,0:T(8,128)(2,1)S(1)} %collective-permute-done.1.refs_2_) | copy-start | bytes 1572868
  192.3 24.0 %collective-permute-start.3 = (bf16[128,1024]{1,0:T(8,128)(2,1)S(1)}, bf16[128,1024]{1,0:T(8,128)(2,1)S(1)}, u32[]{:S(2)}, u32[]{:S(2)}) collective-permute-start(bf16[128,1024]{1,0:T(8,128)(2,1)S(1)} %slice.44), channel_id=1, source_target_pairs={{0,3},{1,0},{2,1},{3,2},{4,7},{5,4},{6,5},{7,6},{8,11},{9,8},{10,9... | collective-permute-start | bytes 786440 | tf_op jit(solution)/shard_map/ppermute | solution.py:31
  216.3 0.7 copy-start.3
  216.3 0.8 copy-start.4
  217.1 10.7 %copy-start.8 = (f32[32]{0:T(128)S(1)}, f32[32]{0:T(128)}, u32[]{:S(2)}) copy-start(f32[32]{0:T(128)} %param.17) | copy-start | bytes 388
  225.1 6.2 %collective-permute-start.6 = (bf16[256,128]{1,0:T(8,128)(2,1)S(1)}, bf16[256,128]{1,0:T(8,128)(2,1)S(1)}, u32[]{:S(2)}, u32[]{:S(2)}) collective-permute-start(bf16[256,128]{1,0:T(8,128)(2,1)S(1)} %slice.48), channel_id=1, source_target_pairs={{0,1},{1,2},{2,3},{3,0},{4,5},{5,6},{6,7},{7,4},{8,9},{9,10},{10,1... | collective-permute-start | bytes 196616 | tf_op jit(solution)/shard_map/ppermute | solution.py:31
  225.1 6.2 %collective-permute-start.4 = (bf16[256,128]{1,0:T(8,128)(2,1)S(1)}, bf16[256,128]{1,0:T(8,128)(2,1)S(1)}, u32[]{:S(2)}, u32[]{:S(2)}) collective-permute-start(bf16[256,128]{1,0:T(8,128)(2,1)S(1)} %slice.48), channel_id=1, source_target_pairs={{0,3},{1,0},{2,1},{3,2},{4,7},{5,4},{6,5},{7,6},{8,11},{9,8},{10,9... | collective-permute-start | bytes 196616 | tf_op jit(solution)/shard_map/ppermute | solution.py:31
  227.8 5.0 %collective-permute-start.5 = (bf16[256,128]{1,0:T(8,128)(2,1)S(1)}, bf16[256,128]{1,0:T(8,128)(2,1)S(1)}, u32[]{:S(2)}, u32[]{:S(2)}) collective-permute-start(bf16[256,128]{1,0:T(8,128)(2,1)S(1)} %slice.48), channel_id=1, source_target_pairs={{0,2},{1,3},{2,0},{3,1},{4,6},{5,7},{6,4},{7,5},{8,10},{9,11},{10,... | collective-permute-start | bytes 196616 | tf_op jit(solution)/shard_map/ppermute | solution.py:31
  230.7 66.2 %copy-start.5 = (f32[2,128,32]{2,1,0:T(8,128)}, f32[2,128,32]{2,1,0:T(8,128)S(1)}, u32[]{:S(2)}) copy-start(f32[2,128,32]{2,1,0:T(8,128)S(1)} %reduce_window_sum.11.decay) | copy-start | bytes 98308
Sparse Core Ops, SparseCore 0:
  11.9 38.4 all-gather.8
  52.8 63.5 all-gather.12
  118.3 76.3 all-gather.10
  196.4 93.3 all-gather.14

commit v7 on v3

--- a/solution.py
+++ b/solution.py
@@ -19,6 +19,7 @@
 NX = 4
 DP = ("y", "z", "core")
 VMEM = 62 * 1024 * 1024
+PASS_COST = 840 * 1024 * 1024
 ANY = pl.BlockSpec(memory_space=pl.ANY)
 HBM = pl.BlockSpec(memory_space=pltpu.HBM)
 WHOLE = pl.BlockSpec(memory_space=pltpu.VMEM)
@@ -71,6 +72,23 @@
         ),
         name="pack_pages",
     )(picks, pool)
+
+
+def pass_kernel(weights, out):
+    pass
+
+
+def pass_on(weights):
+    return pl.pallas_call(
+        pass_kernel,
+        out_shape=jax.ShapeDtypeStruct(weights.shape, weights.dtype),
+        in_specs=[HBM],
+        out_specs=HBM,
+        input_output_aliases={0: 0},
+        compiler_params=pltpu.CompilerParams(vmem_limit_bytes=VMEM),
+        cost_estimate=pl.CostEstimate(flops=0, bytes_accessed=PASS_COST, transcendentals=0),
+        name="pass_on",
+    )(weights)
 
 
 def project_kernel(x, weights, *refs):
@@ -389,7 +407,7 @@
         ],
         compiler_params=pltpu.CompilerParams(vmem_limit_bytes=VMEM),
         cost_estimate=pl.CostEstimate(
-            flops=4 * rows * cols * slots * PAGE,
+            flops=272 * rows * cols * slots * PAGE,
             bytes_accessed=members * slots * PAGE * 4 * HD,
             transcendentals=rows * heads * slots * PAGE,
         ),
@@ -445,15 +463,16 @@
     weights = lax.all_gather(weights, "z", axis=0)
     picks = lax.all_to_all(asks, DP, split_axis=0, concat_axis=0, tiled=True)
     kv_out = pack_pages(picks, 0, page_pool)
+    state_out = pack_pages(picks, 1, page_pool)
+    kv_out, state_out = lax.optimization_barrier((kv_out, state_out))
     kv_in = lax.all_to_all(kv_out, DP, split_axis=0, concat_axis=0, tiled=True)
-    later_pool, _ = lax.optimization_barrier((page_pool, kv_out))
-    state_out = pack_pages(picks, 1, later_pool)
     state_in = lax.all_to_all(state_out, DP, split_axis=0, concat_axis=0, tiled=True)
 
     weights, _ = lax.optimization_barrier((weights, state_out))
+    weights = pass_on(weights)
     weights = lax.all_gather(weights, ("y", "core"), axis=0)
     weights = weights.reshape((NY, 2) + weights.shape[1:])
-    tokens, _ = lax.optimization_barrier((tokens, kv_out))
+    tokens, _ = lax.optimization_barrier((tokens, kv_in))
     inner, extras = project(
         x.reshape(1).astype(jnp.int32), weights, gather_tokens(tokens), rows, 2 * extra
     )

time: 276 us -> 269 us (0.975)
  blocking collectives: 130 us -> 22.2 us
  waiting for transfers between devices: 51.4 us -> 139 us
  starting transfers between devices: 16 us -> 23 us
  local copies, waits for them, and re-layouts: 6.43 us -> 9.92 us
    all_to_all x1 -> x0, blocking collectives: 107 us -> none  [body(): kv_in = lax.all_to_all(kv_out, DP, split_axis=0, concat_axis=0, tiled=True)]
    all_to_all x0 -> x1, waiting for transfers between devices: none -> 93.4 us  [body(): kv_in = lax.all_to_all(kv_out, DP, split_axis=0, concat_axis=0, tiled=True)]
    all_gather x1, waiting for transfers between devices: 10.2 us -> 28.4 us  [body(): weights = lax.all_gather(weights, ('y', 'core'), axis=0)]
    all_to_all x1, waiting for transfers between devices: 21.8 us -> 10.3 us  [body(): lax.all_to_all(state_out, DP, split_axis=0, concat_axis=0, tiled=True)]
    ppermute x7, waiting for transfers between devices: 10.8 us -> 3.57 us  [around_x(): lax.ppermute(array, 'tensor', [(i, (i + by) % NX) for i in range(NX)])]
    all_to_all x0 -> x1, starting transfers between devices: none -> 5.85 us  [body(): kv_in = lax.all_to_all(kv_out, DP, split_axis=0, concat_axis=0, tiled=True)]
    all_gather x1, waiting for transfers between devices: 8.59 us -> 3.19 us  [body(): weights = lax.all_gather(weights, 'z', axis=0)]
  transfers between devices with their start and end apart: 10 -> 11, of which waited for: 5 -> 6; matrix products, arithmetic and copies ran while one was open for 3% -> 4% of each run, Pallas kernels for 17% -> 18%
where the time goes in v7:
time: 269 us; the launch traced here: 268 us
  waiting for transfers between devices  139 us (52%)
  Pallas kernels  53.4 us (20%)
  starting transfers between devices  23 us (9%)
  blocking collectives  22.2 us (8%)
  between operations  14.2 us (5%)
  local copies, waits for them, and re-layouts  9.92 us (4%)
  other arithmetic  5.86 us (2%)
    all_to_all x1, waiting for transfers between devices, body(): kv_in = lax.all_to_all(kv_out, DP, split_axis=0, concat_axis=0, tiled=True)  93.4 us
    all_gather x1, waiting for transfers between devices, body(): weights = lax.all_gather(weights, ('y', 'core'), axis=0)  28.4 us
    all_to_all x1, blocking collectives, body(): picks = lax.all_to_all(asks, DP, split_axis=0, concat_axis=0, tiled=True)  22.2 us
    pallas_call x1, Pallas kernels, attend(): pl.pallas_call(attend_kernel, out_shape=jax.ShapeDtypeStruct((rows, cols)...  19.2 us
    pallas_call x2, Pallas kernels, pack_pages(): pl.pallas_call(functools.partial(pack_kernel, column), out_shape=jax.Shap...  11.4 us
    ppermute x7, starting transfers between devices, around_x(): lax.ppermute(array, 'tensor', [(i, (i + by) % NX) for i in range(NX)])  10.3 us
    all_to_all x1, waiting for transfers between devices, body(): lax.all_to_all(state_out, DP, split_axis=0, concat_axis=0, tiled=True)  10.3 us
    pallas_call x1, Pallas kernels, project(): pl.pallas_call(project_kernel, out_shape=(jax.ShapeDtypeStruct((rows, mai...  10.2 us
  transfers between devices with their start and end apart: 11, of which 6 were waited for; matrix products, arithmetic and copies ran while one was open for 4% of the time, Pallas kernels for 18%

profile of v7, /device:TPU:1, one launch (start us, length us, event | category | flops | bytes accessed | tf_op | source)
XLA Modules:
  0.0 267.6 jit_solution(14308377418290929446)
XLA Ops:
  7.2 0.7 and_select_fusion
  8.0 0.1 eq.37
  8.1 0.1 broadcast_in_dim.37
  8.2 0.1 eq.41
  8.3 0.1 broadcast_in_dim.40
  8.4 0.1 select_reduce_fusion
  8.5 0.1 select_reduce_fusion.1
  8.6 0.1 copy.38
  8.7 0.8 copy.48
  9.5 1.7 fusion.1
  11.2 22.2 %all_to_all.15.picks = s32[64,1,128]{2,1,0:T(1,128)} all-to-all(s32[64,1,128]{2,1,0:T(1,128)S(1)} %bitcast.29), channel_id=1, replica_groups=mesh['y'=4,'z'=8,'core'=2,'tensor'=4] {'y','z','core'}, dimensions={0} | all-to-all | bytes 65536 | tf_op jit(solution)/shard_map/all_to_all | solution.py:464
  33.5 4.7 %pack_pages.2 = bf16[64,128,256]{2,1,0:T(8,128)(2,1)} custom-call(s32[64,1,128]{2,1,0:T(1,128)} %all_to_all.15.picks, bf16[96,128,256]{2,1,0:T(8,128)(2,1)} %pool.3), custom_call_target="tpu_custom_call" | custom-call | bytes 8388608 | tf_op jit(solution)/shard_map/pack_pages/pallas_call | solution.py:59
  38.2 6.7 %pack_pages.3 = bf16[64,128,256]{2,1,0:T(8,128)(2,1)} custom-call(s32[64,1,128]{2,1,0:T(1,128)} %all_to_all.15.picks, bf16[96,128,256]{2,1,0:T(8,128)(2,1)} %pool.3), custom_call_target="tpu_custom_call" | custom-call | bytes 8388608 | tf_op jit(solution)/shard_map/pack_pages/pallas_call | solution.py:59
  44.9 5.8 %all-to-all-start.2 = ((bf16[64,128,256]{2,1,0:T(8,128)(2,1)}), bf16[64,128,256]{2,1,0:T(8,128)(2,1)}, u32[]{:S(2)}, u32[]{:S(2)}) async-start(bf16[64,128,256]{2,1,0:T(8,128)(2,1)} %pack_pages.2), calls=%async_computation.2 | async-start | bytes 8388608 | tf_op jit(solution)/shard_map/all_to_all | solution.py:468
  50.9 3.2 %all-gather.5.cloned.1.call-done = bf16[512,2304]{1,0:T(8,128)(2,1)} async-done(((bf16[64,2304]{1,0:T(8,128)(2,1)}), bf16[512,2304]{1,0:T(8,128)(2,1)}) %all-gather.5.cloned.1.call-update) | async-done | bytes 2359312 | tf_op jit(solution)/shard_map/all_gather | solution.py:463
  54.1 93.4 %all-to-all-done.2.incoming = bf16[64,128,256]{2,1,0:T(8,128)(2,1)} async-done(((bf16[64,128,256]{2,1,0:T(8,128)(2,1)}), bf16[64,128,256]{2,1,0:T(8,128)(2,1)}, u32[]{:S(2)}, u32[]{:S(2)}) %all-to-all-start.2) | async-done | bytes 4194336 | tf_op jit(solution)/shard_map/all_to_all | solution.py:468
  147.5 1.2 collective-permute-start
  148.7 1.5 collective-permute-start.1
  150.2 0.5 exp.8
  150.8 0.6 copy-done.5
  151.4 0.8 copy.44.live
  152.3 0.7 broadcast_in_dim_reshape.3.gain
  152.9 6.8 %all-to-all-start.1 = ((bf16[64,128,256]{2,1,0:T(8,128)(2,1)}), bf16[64,128,256]{2,1,0:T(8,128)(2,1)}, u32[]{:S(2)}, u32[]{:S(2)}) async-start(bf16[64,128,256]{2,1,0:T(8,128)(2,1)} %pack_pages.3), calls=%async_computation.1 | async-start | bytes 8388608 | tf_op jit(solution)/shard_map/all_to_all | solution.py:469
  159.7 2.1 collective-permute-done.refs_1_
  161.8 0.8 copy-done
  162.6 0.7 slice.35
  163.4 0.8 copy-done.1
  164.2 0.7 slice.36
  164.9 2.7 collective-permute-start.3
  167.6 19.2 %attend.1 = bf16[256,1024]{1,0:T(8,128)(2,1)} custom-call(s32[2,32]{1,0:T(2,128)} %copy-done.7, s32[2]{0:T(128)} %prefix.1, bf16[256,1024]{1,0:T(8,128)(2,1)} %queries.1, bf16[256,256]{1,0:T(8,128)(2,1)} %fresh.1, f32[256,1]{1,0:T(8,128)} %copy.44.live, bf16[64,128,256]{2,1,0:T(8,128)(2,1)} %all-to-all-done.2.incoming), custom_call_target="tpu_custom_call" | custom-call | flops 292057776128 | bytes 4194304 | tf_op jit(solution)/shard_map/attend/pallas_call | solution.py:396
  186.9 28.4 %all-gather.7.cloned.1.call-done = bf16[64,64,2304]{2,1,0:T(8,128)(2,1)} async-done(((bf16[8,64,2304]{2,1,0:T(8,128)(2,1)}), bf16[64,64,2304]{2,1,0:T(8,128)(2,1)}) %all-gather.7.cloned.1.call-update) | async-done | bytes 18874384 | tf_op jit(solution)/shard_map/all_gather | solution.py:473
  215.3 10.2 %project.1 = (bf16[256,2048]{1,0:T(8,128)(2,1)}, f32[256,256]{1,0:T(8,128)}) custom-call(s32[1]{0:T(128)} %bitcast.3.x, bf16[4,2,8,64,2304]{4,3,2,1,0:T(8,128)(2,1)} %bitcast.26, bf16[256,1024]{1,0:T(8,128)(2,1)} %refs_0_, bf16[256,1024]{1,0:T(8,128)(2,1)} %copy-done, bf16[256,1024]{1,0:T(8,128)(2,1)} %copy-done.1, ...), custom_call_target="tpu_custom_call" | custom-call | flops 4831838208 | bytes 20971520 | tf_op jit(solution)/shard_map/project/pallas_call | solution.py:152
  225.5 0.9 slice.40
  226.4 3.3 %collective-permute-start.4 = (bf16[256,128]{1,0:T(8,128)(2,1)S(1)}, bf16[256,128]{1,0:T(8,128)(2,1)S(1)}, u32[]{:S(2)}, u32[]{:S(2)}) collective-permute-start(bf16[256,128]{1,0:T(8,128)(2,1)S(1)} %slice.40), channel_id=1, source_target_pairs={{0,3},{1,0},{2,1},{3,2},{4,7},{5,4},{6,5},{7,6},{8,11},{9,8},{10,9... | collective-permute-start | bytes 196616 | tf_op jit(solution)/shard_map/ppermute | solution.py:30
  229.7 1.2 collective-permute-start.5
  231.0 0.5 collective-permute-start.6
  231.4 1.0 compare_select_fusion
  232.5 0.9 slice_bitcast_fusion
  233.4 0.6 multiply_bitcast_fusion
  234.0 0.1 copy.42
  234.1 0.2 reduce_window_sum.11.decay
  234.3 0.7 copy.43
  235.0 1.4 collective-permute-done.6
  236.6 0.7 pad_maximum_fusion.2.b_values
  237.2 0.7 pad_maximum_fusion.1.c_values
  237.9 7.4 %mix_locally.1 = (f32[256,2048]{1,0:T(8,128)}, f32[256,2048]{1,0:T(8,128)}) custom-call(bf16[256,2048]{1,0:T(8,128)(2,1)} %get-tuple-element.23.inner, bf16[256,256]{1,0:T(8,128)(2,1)} %pad_maximum_fusion.2.b_values, bf16[256,256]{1,0:T(8,128)(2,1)} %pad_maximum_fusion.1.c_values, f32[2,128,32]{2,1,0:T(8,128)} %copy-done.3, f32[2,32,128]{2,1,0:T(8,128)} %bitcast.33, ...), custom_call_target="tpu_custom_call" | custom-call | flops 536870912 | bytes 3145728 | tf_op jit(solution)/shard_map/mix_locally/pallas_call | solution.py:215
  245.3 10.3 %all-to-all-done.1.incoming = bf16[64,128,256]{2,1,0:T(8,128)(2,1)} async-done(((bf16[64,128,256]{2,1,0:T(8,128)(2,1)}), bf16[64,128,256]{2,1,0:T(8,128)(2,1)}, u32[]{:S(2)}, u32[]{:S(2)}) %all-to-all-start.1) | async-done | bytes 4194336 | tf_op jit(solution)/shard_map/all_to_all | solution.py:469
  255.6 5.2 %carry_state.1 = bf16[256,2048]{1,0:T(8,128)(2,1)} custom-call(s32[2,16]{1,0:T(2,128)} %bitcast.35, bf16[64,128,256]{2,1,0:T(8,128)(2,1)} %all-to-all-done.1.incoming, bf16[256,256]{1,0:T(8,128)(2,1)} %pad_maximum_fusion.1.c_values, f32[256,2048]{1,0:T(8,128)} %get-tuple-element.24.factor, f32[256,2048]{1,0:T(8,128)} %get-tuple-element.25.local), custom_call_target="tpu_custom_call" | custom-call | flops 268435456 | bytes 4194304 | tf_op jit(solution)/shard_map/carry_state/pallas_call | solution.py:277
  (43 shorter events, 0.6 us)
Async XLA Ops:
  7.2 46.9 %all-gather.5.cloned.1.call-start = ((), (), s32[]{:S(2)}) async-start(), calls=%async_computation.3 | async-start | bytes 2654208 | tf_op jit(solution)/shard_map/all_gather | solution.py:463
  7.9 0.7 copy-start.4
  8.0 30.2 %copy-start.7 = (s32[2,32]{1,0:T(2,128)}, s32[2,32]{1,0:T(2,128)S(1)}, u32[]{:S(2)}) copy-start(s32[2,32]{1,0:T(2,128)S(1)} %slice.28.sources) | copy-start | bytes 772
  44.9 102.6 %all-to-all-start.2 = ((bf16[64,128,256]{2,1,0:T(8,128)(2,1)}), bf16[64,128,256]{2,1,0:T(8,128)(2,1)}, u32[]{:S(2)}, u32[]{:S(2)}) async-start(bf16[64,128,256]{2,1,0:T(8,128)(2,1)} %pack_pages.2), calls=%async_computation.2 | async-start | bytes 8388608 | tf_op jit(solution)/shard_map/all_to_all | solution.py:468
  50.8 96.7 %copy-start.2 = (bf16[256,1024]{1,0:T(8,128)(2,1)S(1)}, bf16[256,1024]{1,0:T(8,128)(2,1)}, u32[]{:S(2)}) copy-start(bf16[256,1024]{1,0:T(8,128)(2,1)} %refs_0_) | copy-start | bytes 1572868
  50.8 99.4 %copy-start.11 = (f32[32]{0:T(128)S(1)}, f32[32]{0:T(128)}, u32[]{:S(2)}) copy-start(f32[32]{0:T(128)} %param.18) | copy-start | bytes 388
  50.8 99.9 %copy-start.12 = (s32[2]{0:T(128)S(1)}, s32[2]{0:T(128)}, u32[]{:S(2)}) copy-start(s32[2]{0:T(128)} %param.25) | copy-start | bytes 28
  50.8 101.4 %copy-start.10 = (f32[32]{0:T(128)S(1)}, f32[32]{0:T(128)}, u32[]{:S(2)}) copy-start(f32[32]{0:T(128)} %param.19) | copy-start | bytes 388
  50.8 164.4 %all-gather.7.cloned.1.call-start = ((), (), s32[]{:S(2)}) async-start(), calls=%async_computation.4 | async-start | bytes 21233664 | tf_op jit(solution)/shard_map/all_gather | solution.py:473
  147.5 14.3 %collective-permute-start = (bf16[256,1024]{1,0:T(8,128)(2,1)S(1)}, bf16[256,1024]{1,0:T(8,128)(2,1)S(1)}, u32[]{:S(2)}, u32[]{:S(2)}) collective-permute-start(bf16[256,1024]{1,0:T(8,128)(2,1)S(1)} %copy-done.2), channel_id=1, source_target_pairs={{0,1},{1,2},{2,3},{3,0},{4,5},{5,6},{6,7},{7,4},{8,9},{9,10},{10,1... | collective-permute-start | bytes 1572872 | tf_op jit(solution)/shard_map/ppermute | solution.py:30
  148.7 14.7 %collective-permute-start.1 = (bf16[256,1024]{1,0:T(8,128)(2,1)S(1)}, bf16[256,1024]{1,0:T(8,128)(2,1)S(1)}, u32[]{:S(2)}, u32[]{:S(2)}) collective-permute-start(bf16[256,1024]{1,0:T(8,128)(2,1)S(1)} %copy-done.2), channel_id=1, source_target_pairs={{0,3},{1,0},{2,1},{3,2},{4,7},{5,4},{6,5},{7,6},{8,11},{9,8},{10,9... | collective-permute-start | bytes 1572872 | tf_op jit(solution)/shard_map/ppermute | solution.py:30
  150.8 0.6 copy-start.5
  152.9 102.7 %all-to-all-start.1 = ((bf16[64,128,256]{2,1,0:T(8,128)(2,1)}), bf16[64,128,256]{2,1,0:T(8,128)(2,1)}, u32[]{:S(2)}, u32[]{:S(2)}) async-start(bf16[64,128,256]{2,1,0:T(8,128)(2,1)} %pack_pages.3), calls=%async_computation.1 | async-start | bytes 8388608 | tf_op jit(solution)/shard_map/all_to_all | solution.py:469
  161.8 0.8 copy-start
  163.4 23.5 %collective-permute-start.2 = (bf16[128,1024]{1,0:T(8,128)(2,1)}, bf16[128,1024]{1,0:T(8,128)(2,1)}, u32[]{:S(2)}, u32[]{:S(2)}) collective-permute-start(bf16[128,1024]{1,0:T(8,128)(2,1)} %slice.35), channel_id=1, source_target_pairs={{0,1},{1,2},{2,3},{3,0},{4,5},{5,6},{6,7},{7,4},{8,9},{9,10},{10,1... | collective-permute-start | bytes 786440 | tf_op jit(solution)/shard_map/ppermute | solution.py:30
  163.4 0.8 copy-start.1
  164.9 21.9 %collective-permute-start.3 = (bf16[128,1024]{1,0:T(8,128)(2,1)}, bf16[128,1024]{1,0:T(8,128)(2,1)}, u32[]{:S(2)}, u32[]{:S(2)}) collective-permute-start(bf16[128,1024]{1,0:T(8,128)(2,1)} %slice.36), channel_id=1, source_target_pairs={{0,3},{1,0},{2,1},{3,2},{4,7},{5,4},{6,5},{7,6},{8,11},{9,8},{10,9... | collective-permute-start | bytes 786440 | tf_op jit(solution)/shard_map/ppermute | solution.py:30
  215.3 16.2 %copy-start.8 = (f32[32]{0:T(128)S(1)}, f32[32]{0:T(128)}, u32[]{:S(2)}) copy-start(f32[32]{0:T(128)} %param.17) | copy-start | bytes 388
  215.3 18.1 %copy-start.6 = (f32[2,128]{1,0:T(2,128)S(1)}, f32[2,128]{1,0:T(2,128)}, u32[]{:S(2)}) copy-start(f32[2,128]{1,0:T(2,128)} %copy-done.5) | copy-start | bytes 3076
  215.3 18.1 %copy-start.9 = (f32[32]{0:T(128)S(1)}, f32[32]{0:T(128)}, u32[]{:S(2)}) copy-start(f32[32]{0:T(128)} %exp.8) | copy-start | bytes 388
  226.4 8.6 %collective-permute-start.4 = (bf16[256,128]{1,0:T(8,128)(2,1)S(1)}, bf16[256,128]{1,0:T(8,128)(2,1)S(1)}, u32[]{:S(2)}, u32[]{:S(2)}) collective-permute-start(bf16[256,128]{1,0:T(8,128)(2,1)S(1)} %slice.40), channel_id=1, source_target_pairs={{0,3},{1,0},{2,1},{3,2},{4,7},{5,4},{6,5},{7,6},{8,11},{9,8},{10,9... | collective-permute-start | bytes 196616 | tf_op jit(solution)/shard_map/ppermute | solution.py:30
  229.7 5.3 %collective-permute-start.5 = (bf16[256,128]{1,0:T(8,128)(2,1)S(1)}, bf16[256,128]{1,0:T(8,128)(2,1)S(1)}, u32[]{:S(2)}, u32[]{:S(2)}) collective-permute-start(bf16[256,128]{1,0:T(8,128)(2,1)S(1)} %slice.40), channel_id=1, source_target_pairs={{0,2},{1,3},{2,0},{3,1},{4,6},{5,7},{6,4},{7,5},{8,10},{9,11},{10,... | collective-permute-start | bytes 196616 | tf_op jit(solution)/shard_map/ppermute | solution.py:30
  231.0 5.5 %collective-permute-start.6 = (bf16[256,128]{1,0:T(8,128)(2,1)S(1)}, bf16[256,128]{1,0:T(8,128)(2,1)S(1)}, u32[]{:S(2)}, u32[]{:S(2)}) collective-permute-start(bf16[256,128]{1,0:T(8,128)(2,1)S(1)} %slice.40), channel_id=1, source_target_pairs={{0,1},{1,2},{2,3},{3,0},{4,5},{5,6},{6,7},{7,4},{8,9},{9,10},{10,1... | collective-permute-start | bytes 196616 | tf_op jit(solution)/shard_map/ppermute | solution.py:30
  234.3 3.6 %copy-start.3 = (f32[2,128,32]{2,1,0:T(8,128)}, f32[2,128,32]{2,1,0:T(8,128)S(1)}, u32[]{:S(2)}) copy-start(f32[2,128,32]{2,1,0:T(8,128)S(1)} %reduce_window_sum.11.decay) | copy-start | bytes 98308
Sparse Core Ops, SparseCore 0:
  11.4 42.6 all-gather.4
  55.9 159.3 all-gather.6

commit v8 on v7

--- a/solution.py
+++ b/solution.py
@@ -298,7 +298,7 @@
 CHUNK = 8
 
 
-def attend_kernel(sources, prefix, queries, fresh, live, incoming, out, stacked, held, top, total, sems):
+def attend_kernel(sources, prefix, counts, queries, fresh, incoming, out, stacked, held, top, total, sems):
     members, slots = sources.shape
     heads = queries.shape[1] // HD
     factor = math.log2(math.e) / math.sqrt(HD)
@@ -383,20 +383,21 @@
             return carry
 
         lax.fori_loop(0, (prefix[member] + CHUNK - 1) // CHUNK, chunk, 0)
+        live = lax.broadcasted_iota(jnp.int32, (PAGE, HD), 0) < counts[member]
         for head in range(heads):
             at = slice(head * PAGE, (head + 1) * PAGE)
-            mixed = total[at, HD:] / total[at, :HD] * live[rows, :]
+            mixed = jnp.where(live, total[at, HD:] / total[at, :HD], 0.0)
             out[rows, head * HD : (head + 1) * HD] = mixed.astype(jnp.bfloat16)
 
 
-def attend(sources, prefix, queries, fresh, live, incoming):
+def attend(sources, prefix, counts, queries, fresh, incoming):
     rows, cols = queries.shape
     members, slots = sources.shape
     heads = cols // HD
     return pl.pallas_call(
         attend_kernel,
         out_shape=jax.ShapeDtypeStruct((rows, cols), jnp.bfloat16),
-        in_specs=[SCALARS, SCALARS] + [WHOLE] * 3 + [HBM],
+        in_specs=[SCALARS] * 3 + [WHOLE] * 2 + [HBM],
         out_specs=WHOLE,
         scratch_shapes=[
             pltpu.VMEM((heads * PAGE, HD), jnp.bfloat16),
@@ -407,12 +408,12 @@
         ],
         compiler_params=pltpu.CompilerParams(vmem_limit_bytes=VMEM),
         cost_estimate=pl.CostEstimate(
-            flops=272 * rows * cols * slots * PAGE,
+            flops=256 * rows * cols * slots * PAGE,
             bytes_accessed=members * slots * PAGE * 4 * HD,
             transcendentals=rows * heads * slots * PAGE,
         ),
         name="attend",
-    )(sources, prefix, queries, fresh, live, incoming)
+    )(sources, prefix, counts, queries, fresh, incoming)
 
 
 def gather_tokens(tokens):
@@ -472,7 +473,12 @@
     weights = pass_on(weights)
     weights = lax.all_gather(weights, ("y", "core"), axis=0)
     weights = weights.reshape((NY, 2) + weights.shape[1:])
-    tokens, _ = lax.optimization_barrier((tokens, kv_in))
+    attention_out = attend(
+        sources[:, SP:], prefix_pages, new_counts, queries, new_keyvals, kv_in
+    )
+    tokens, decay_log, skip_gain, new_counts, _ = lax.optimization_barrier(
+        (tokens, decay_log, skip_gain, new_counts, attention_out)
+    )
     inner, extras = project(
         x.reshape(1).astype(jnp.int32), weights, gather_tokens(tokens), rows, 2 * extra
     )
@@ -491,9 +497,6 @@
     live_column = live.reshape(rows, 1)
     local, factor = mix_locally(
         inner, b_values, c_values, decay, decay.transpose(0, 2, 1), step.transpose(0, 2, 1), gain, live_column
-    )
-    attention_out = attend(
-        sources[:, SP:], prefix_pages, queries, new_keyvals, live_column, kv_in
     )
     mamba_out = carry_state(sources[:, :SP], state_in, c_values, factor, local)
     return (mamba_out, attention_out)

time: 269 us -> 270 us (level)
  the two profiles are of different devices: /device:TPU:1 before, /device:TPU:96 now
where the time goes in v8:
time: 270 us; the launch traced here: 269 us
  waiting for transfers between devices  148 us (55%)
  Pallas kernels  49.2 us (18%)
  starting transfers between devices  29 us (11%)
  blocking collectives  17.6 us (7%)
  between operations  14.2 us (5%)
  other arithmetic  5.86 us (2%)
  local copies, waits for them, and re-layouts  5.71 us (2%)
    all_to_all x1, waiting for transfers between devices, body(): kv_in = lax.all_to_all(kv_out, DP, split_axis=0, concat_axis=0, tiled=True)  84.9 us
    all_gather x1, waiting for transfers between devices, body(): weights = lax.all_gather(weights, ('y', 'core'), axis=0)  35.5 us
    ppermute x7, waiting for transfers between devices, around_x(): lax.ppermute(array, 'tensor', [(i, (i + by) % NX) for i in range(NX)])  18.7 us
    all_to_all x1, blocking collectives, body(): picks = lax.all_to_all(asks, DP, split_axis=0, concat_axis=0, tiled=True)  17.6 us
    pallas_call x1, Pallas kernels, attend(): pl.pallas_call(attend_kernel, out_shape=jax.ShapeDtypeStruct((rows, cols)...  15.1 us
    pallas_call x2, Pallas kernels, pack_pages(): pl.pallas_call(functools.partial(pack_kernel, column), out_shape=jax.Shap...  11.4 us
    ppermute x7, starting transfers between devices, around_x(): lax.ppermute(array, 'tensor', [(i, (i + by) % NX) for i in range(NX)])  11 us
    pallas_call x1, Pallas kernels, project(): pl.pallas_call(project_kernel, out_shape=(jax.ShapeDtypeStruct((rows, mai...  10.2 us
  transfers between devices with their start and end apart: 11, of which 9 were waited for; matrix products, arithmetic and copies ran while one was open for 3% of the time, Pallas kernels for 16%

profile of v8, /device:TPU:96, one launch (start us, length us, event | category | flops | bytes accessed | tf_op | source)
XLA Modules:
  0.0 269.5 jit_solution(13491600984087202559)
XLA Ops:
  7.2 0.7 and_select_fusion
  7.9 0.1 slice.28.sources
  8.0 0.1 eq.37
  8.1 0.1 slice.29
  8.1 0.1 broadcast_in_dim.37
  8.2 0.1 eq.41
  8.3 0.1 broadcast_in_dim.40
  8.4 0.1 select_reduce_fusion
  8.5 0.1 select_reduce_fusion.1
  8.6 0.1 copy.36
  8.7 0.8 copy.45
  9.5 1.7 fusion.1
  11.2 17.6 %all_to_all.15.picks = s32[64,1,128]{2,1,0:T(1,128)} all-to-all(s32[64,1,128]{2,1,0:T(1,128)S(1)} %bitcast.29), channel_id=1, replica_groups=mesh['y'=4,'z'=8,'core'=2,'tensor'=4] {'y','z','core'}, dimensions={0} | all-to-all | bytes 65536 | tf_op jit(solution)/shard_map/all_to_all | solution.py:465
  28.8 4.8 %pack_pages.2 = bf16[64,128,256]{2,1,0:T(8,128)(2,1)} custom-call(s32[64,1,128]{2,1,0:T(1,128)} %all_to_all.15.picks, bf16[96,128,256]{2,1,0:T(8,128)(2,1)} %pool.3), custom_call_target="tpu_custom_call" | custom-call | bytes 8388608 | tf_op jit(solution)/shard_map/pack_pages/pallas_call | solution.py:59
  33.6 6.6 %pack_pages.3 = bf16[64,128,256]{2,1,0:T(8,128)(2,1)} custom-call(s32[64,1,128]{2,1,0:T(1,128)} %all_to_all.15.picks, bf16[96,128,256]{2,1,0:T(8,128)(2,1)} %pool.3), custom_call_target="tpu_custom_call" | custom-call | bytes 8388608 | tf_op jit(solution)/shard_map/pack_pages/pallas_call | solution.py:59
  40.3 8.1 %all-to-all-start.2 = ((bf16[64,128,256]{2,1,0:T(8,128)(2,1)}), bf16[64,128,256]{2,1,0:T(8,128)(2,1)}, u32[]{:S(2)}, u32[]{:S(2)}) async-start(bf16[64,128,256]{2,1,0:T(8,128)(2,1)} %pack_pages.2), calls=%async_computation.2 | async-start | bytes 8388608 | tf_op jit(solution)/shard_map/all_to_all | solution.py:469
  48.4 8.8 %all-gather.5.cloned.1.call-done = bf16[512,2304]{1,0:T(8,128)(2,1)} async-done(((bf16[64,2304]{1,0:T(8,128)(2,1)}), bf16[512,2304]{1,0:T(8,128)(2,1)}) %all-gather.5.cloned.1.call-update) | async-done | bytes 2359312 | tf_op jit(solution)/shard_map/all_gather | solution.py:464
  57.3 84.9 %all-to-all-done.2.incoming = bf16[64,128,256]{2,1,0:T(8,128)(2,1)} async-done(((bf16[64,128,256]{2,1,0:T(8,128)(2,1)}), bf16[64,128,256]{2,1,0:T(8,128)(2,1)}, u32[]{:S(2)}, u32[]{:S(2)}) %all-to-all-start.2) | async-done | bytes 4194336 | tf_op jit(solution)/shard_map/all_to_all | solution.py:469
  142.1 9.8 %all-to-all-start.1 = ((bf16[64,128,256]{2,1,0:T(8,128)(2,1)}), bf16[64,128,256]{2,1,0:T(8,128)(2,1)}, u32[]{:S(2)}, u32[]{:S(2)}) async-start(bf16[64,128,256]{2,1,0:T(8,128)(2,1)} %pack_pages.3), calls=%async_computation.1 | async-start | bytes 8388608 | tf_op jit(solution)/shard_map/all_to_all | solution.py:470
  152.0 15.1 %attend.1 = bf16[256,1024]{1,0:T(8,128)(2,1)} custom-call(s32[2,32]{1,0:T(2,128)} %copy-done.7, s32[2]{0:T(128)} %prefix.1, s32[2]{0:T(128)} %counts.1, bf16[256,1024]{1,0:T(8,128)(2,1)} %queries.1, bf16[256,256]{1,0:T(8,128)(2,1)} %fresh.1, bf16[64,128,256]{2,1,0:T(8,128)(2,1)} %all-to-all-done.2.incoming), custom_call_target="tpu_custom_call" | custom-call | flops 274877906944 | bytes 4194304 | tf_op jit(solution)/shard_map/attend/pallas_call | solution.py:397
  167.1 1.5 collective-permute-start
  168.6 1.8 collective-permute-start.1
  170.4 11.6 %collective-permute-done.refs_1_ = bf16[256,1024]{1,0:T(8,128)(2,1)S(1)} collective-permute-done((bf16[256,1024]{1,0:T(8,128)(2,1)S(1)}, bf16[256,1024]{1,0:T(8,128)(2,1)S(1)}, u32[]{:S(2)}, u32[]{:S(2)}) %collective-permute-start) | collective-permute-done | bytes 524320 | tf_op jit(solution)/shard_map/ppermute | solution.py:30
  182.0 0.3 collective-permute-start.2
  182.3 0.2 collective-permute-done.1.refs_2_
  182.6 3.3 %collective-permute-start.3 = (bf16[128,1024]{1,0:T(8,128)(2,1)S(1)}, bf16[128,1024]{1,0:T(8,128)(2,1)S(1)}, u32[]{:S(2)}, u32[]{:S(2)}) collective-permute-start(bf16[128,1024]{1,0:T(8,128)(2,1)S(1)} %slice.36), channel_id=1, source_target_pairs={{0,3},{1,0},{2,1},{3,2},{4,7},{5,4},{6,5},{7,6},{8,11},{9,8},{10,9... | collective-permute-start | bytes 786440 | tf_op jit(solution)/shard_map/ppermute | solution.py:30
  185.9 0.8 copy.42.live
  186.8 0.7 broadcast_in_dim_reshape.3.gain
  187.5 4.7 %collective-permute-done.2.refs_3_ = bf16[128,1024]{1,0:T(8,128)(2,1)S(1)} collective-permute-done((bf16[128,1024]{1,0:T(8,128)(2,1)S(1)}, bf16[128,1024]{1,0:T(8,128)(2,1)S(1)}, u32[]{:S(2)}, u32[]{:S(2)}) %collective-permute-start.2) | collective-permute-done | bytes 262176 | tf_op jit(solution)/shard_map/ppermute | solution.py:30
  192.2 0.3 collective-permute-done.3.refs_4_
  192.5 35.5 %all-gather.7.cloned.1.call-done = bf16[64,64,2304]{2,1,0:T(8,128)(2,1)} async-done(((bf16[8,64,2304]{2,1,0:T(8,128)(2,1)}), bf16[64,64,2304]{2,1,0:T(8,128)(2,1)}) %all-gather.7.cloned.1.call-update) | async-done | bytes 18874384 | tf_op jit(solution)/shard_map/all_gather | solution.py:474
  228.0 10.2 %project.1 = (bf16[256,2048]{1,0:T(8,128)(2,1)}, f32[256,256]{1,0:T(8,128)}) custom-call(s32[1]{0:T(128)} %bitcast.3.x, bf16[4,2,8,64,2304]{4,3,2,1,0:T(8,128)(2,1)} %bitcast.26, bf16[256,1024]{1,0:T(8,128)(2,1)} %refs_0_, bf16[256,1024]{1,0:T(8,128)(2,1)} %copy-done, bf16[256,1024]{1,0:T(8,128)(2,1)} %copy-done.1, bf16[128,1024]{1,0:T(8,128)(2,1)} %copy-done.4, ...), custom_call_target="tpu_custom_call" | custom-call | flops 4831838208 | bytes 20971520 | tf_op jit(solution)/shard_map/project/pallas_call | solution.py:152
  238.3 0.9 slice.40
  239.2 2.6 collective-permute-start.4
  241.8 0.9 collective-permute-start.5
  242.7 0.6 collective-permute-start.6
  243.3 1.0 compare_select_fusion
  244.3 0.9 slice_bitcast_fusion
  245.2 0.6 multiply_bitcast_fusion
  245.8 0.1 copy.40
  245.9 0.2 reduce_window_sum.11.decay
  246.1 0.7 copy.41
  246.8 1.2 collective-permute-done.5
  248.0 0.7 collective-permute-done.6
  248.8 0.7 pad_maximum_fusion.2.b_values
  249.5 0.7 pad_maximum_fusion.1.c_values
  250.1 7.3 %mix_locally.1 = (f32[256,2048]{1,0:T(8,128)}, f32[256,2048]{1,0:T(8,128)}) custom-call(bf16[256,2048]{1,0:T(8,128)(2,1)} %get-tuple-element.26.inner, bf16[256,256]{1,0:T(8,128)(2,1)} %pad_maximum_fusion.2.b_values, bf16[256,256]{1,0:T(8,128)(2,1)} %pad_maximum_fusion.1.c_values, f32[2,128,32]{2,1,0:T(8,128)} %copy-done.3, f32[2,32,128]{2,1,0:T(8,128)} %bitcast.33, ...), custom_call_target="tpu_custom_call" | custom-call | flops 536870912 | bytes 3145728 | tf_op jit(solution)/shard_map/mix_locally/pallas_call | solution.py:215
  257.5 5.2 %carry_state.1 = bf16[256,2048]{1,0:T(8,128)(2,1)} custom-call(s32[2,16]{1,0:T(2,128)} %bitcast.35, bf16[64,128,256]{2,1,0:T(8,128)(2,1)} %all-to-all-done.1.incoming, bf16[256,256]{1,0:T(8,128)(2,1)} %pad_maximum_fusion.1.c_values, f32[256,2048]{1,0:T(8,128)} %get-tuple-element.30.factor, f32[256,2048]{1,0:T(8,128)} %get-tuple-element.31.local), custom_call_target="tpu_custom_call" | custom-call | flops 268435456 | bytes 4194304 | tf_op jit(solution)/shard_map/carry_state/pallas_call | solution.py:277
  (41 shorter events, 0.5 us)
Async XLA Ops:
  7.2 50.1 %all-gather.5.cloned.1.call-start = ((), (), s32[]{:S(2)}) async-start(), calls=%async_computation.3 | async-start | bytes 2654208 | tf_op jit(solution)/shard_map/all_gather | solution.py:464
  7.9 0.7 copy-start.6
  8.0 25.7 %copy-start.7 = (s32[2,32]{1,0:T(2,128)}, s32[2,32]{1,0:T(2,128)S(1)}, u32[]{:S(2)}) copy-start(s32[2,32]{1,0:T(2,128)S(1)} %slice.28.sources) | copy-start | bytes 772
  40.3 101.9 %all-to-all-start.2 = ((bf16[64,128,256]{2,1,0:T(8,128)(2,1)}), bf16[64,128,256]{2,1,0:T(8,128)(2,1)}, u32[]{:S(2)}, u32[]{:S(2)}) async-start(bf16[64,128,256]{2,1,0:T(8,128)(2,1)} %pack_pages.2), calls=%async_computation.2 | async-start | bytes 8388608 | tf_op jit(solution)/shard_map/all_to_all | solution.py:469
  48.4 179.6 %all-gather.7.cloned.1.call-start = ((), (), s32[]{:S(2)}) async-start(), calls=%async_computation.4 | async-start | bytes 21233664 | tf_op jit(solution)/shard_map/all_gather | solution.py:474
  142.1 115.3 %all-to-all-start.1 = ((bf16[64,128,256]{2,1,0:T(8,128)(2,1)}), bf16[64,128,256]{2,1,0:T(8,128)(2,1)}, u32[]{:S(2)}, u32[]{:S(2)}) async-start(bf16[64,128,256]{2,1,0:T(8,128)(2,1)} %pack_pages.3), calls=%async_computation.1 | async-start | bytes 8388608 | tf_op jit(solution)/shard_map/all_to_all | solution.py:470
  152.0 15.1 %copy-start.2 = (bf16[256,1024]{1,0:T(8,128)(2,1)S(1)}, bf16[256,1024]{1,0:T(8,128)(2,1)}, u32[]{:S(2)}) copy-start(bf16[256,1024]{1,0:T(8,128)(2,1)} %refs_0_) | copy-start | bytes 1572868
  152.0 33.9 %copy-start.10 = (f32[32]{0:T(128)S(1)}, f32[32]{0:T(128)}, u32[]{:S(2)}) copy-start(f32[32]{0:T(128)} %param.18) | copy-start | bytes 388
  152.0 33.9 %copy-start.11 = (s32[2]{0:T(128)S(1)}, s32[2]{0:T(128)}, u32[]{:S(2)}) copy-start(s32[2]{0:T(128)} %counts.1) | copy-start | bytes 28
  152.0 34.7 %copy-start.9 = (f32[32]{0:T(128)S(1)}, f32[32]{0:T(128)}, u32[]{:S(2)}) copy-start(f32[32]{0:T(128)} %param.19) | copy-start | bytes 388
  167.1 14.9 %collective-permute-start = (bf16[256,1024]{1,0:T(8,128)(2,1)S(1)}, bf16[256,1024]{1,0:T(8,128)(2,1)S(1)}, u32[]{:S(2)}, u32[]{:S(2)}) collective-permute-start(bf16[256,1024]{1,0:T(8,128)(2,1)S(1)} %copy-done.2), channel_id=1, source_target_pairs={{0,1},{1,2},{2,3},{3,0},{4,5},{5,6},{6,7},{7,4},{8,9},{9,10},{10,1... | collective-permute-start | bytes 1572872 | tf_op jit(solution)/shard_map/ppermute | solution.py:30
  168.6 14.0 %collective-permute-start.1 = (bf16[256,1024]{1,0:T(8,128)(2,1)S(1)}, bf16[256,1024]{1,0:T(8,128)(2,1)S(1)}, u32[]{:S(2)}, u32[]{:S(2)}) collective-permute-start(bf16[256,1024]{1,0:T(8,128)(2,1)S(1)} %copy-done.2), channel_id=1, source_target_pairs={{0,3},{1,0},{2,1},{3,2},{4,7},{5,4},{6,5},{7,6},{8,11},{9,8},{10,9... | collective-permute-start | bytes 1572872 | tf_op jit(solution)/shard_map/ppermute | solution.py:30
  182.0 46.0 %copy-start = (bf16[256,1024]{1,0:T(8,128)(2,1)}, bf16[256,1024]{1,0:T(8,128)(2,1)S(1)}, u32[]{:S(2)}) copy-start(bf16[256,1024]{1,0:T(8,128)(2,1)S(1)} %collective-permute-done.refs_1_) | copy-start | bytes 1572868
  182.0 10.1 %collective-permute-start.2 = (bf16[128,1024]{1,0:T(8,128)(2,1)S(1)}, bf16[128,1024]{1,0:T(8,128)(2,1)S(1)}, u32[]{:S(2)}, u32[]{:S(2)}) collective-permute-start(bf16[128,1024]{1,0:T(8,128)(2,1)S(1)} %slice.35), channel_id=1, source_target_pairs={{0,1},{1,2},{2,3},{3,0},{4,5},{5,6},{6,7},{7,4},{8,9},{9,10},{10,1... | collective-permute-start | bytes 786440 | tf_op jit(solution)/shard_map/ppermute | solution.py:30
  182.5 45.4 %copy-start.1 = (bf16[256,1024]{1,0:T(8,128)(2,1)}, bf16[256,1024]{1,0:T(8,128)(2,1)S(1)}, u32[]{:S(2)}) copy-start(bf16[256,1024]{1,0:T(8,128)(2,1)S(1)} %collective-permute-done.1.refs_2_) | copy-start | bytes 1572868
  182.6 9.9 %collective-permute-start.3 = (bf16[128,1024]{1,0:T(8,128)(2,1)S(1)}, bf16[128,1024]{1,0:T(8,128)(2,1)S(1)}, u32[]{:S(2)}, u32[]{:S(2)}) collective-permute-start(bf16[128,1024]{1,0:T(8,128)(2,1)S(1)} %slice.36), channel_id=1, source_target_pairs={{0,3},{1,0},{2,1},{3,2},{4,7},{5,4},{6,5},{7,6},{8,11},{9,8},{10,9... | collective-permute-start | bytes 786440 | tf_op jit(solution)/shard_map/ppermute | solution.py:30
  192.2 35.8 %copy-start.4 = (bf16[128,1024]{1,0:T(8,128)(2,1)}, bf16[128,1024]{1,0:T(8,128)(2,1)S(1)}, u32[]{:S(2)}) copy-start(bf16[128,1024]{1,0:T(8,128)(2,1)S(1)} %collective-permute-done.2.refs_3_) | copy-start | bytes 786436
  192.5 35.5 %copy-start.5 = (bf16[128,1024]{1,0:T(8,128)(2,1)}, bf16[128,1024]{1,0:T(8,128)(2,1)S(1)}, u32[]{:S(2)}) copy-start(bf16[128,1024]{1,0:T(8,128)(2,1)S(1)} %collective-permute-done.3.refs_4_) | copy-start | bytes 786436
  228.0 15.3 %copy-start.8 = (f32[32]{0:T(128)S(1)}, f32[32]{0:T(128)}, u32[]{:S(2)}) copy-start(f32[32]{0:T(128)} %param.17) | copy-start | bytes 388
  239.2 7.7 %collective-permute-start.4 = (bf16[256,128]{1,0:T(8,128)(2,1)S(1)}, bf16[256,128]{1,0:T(8,128)(2,1)S(1)}, u32[]{:S(2)}, u32[]{:S(2)}) collective-permute-start(bf16[256,128]{1,0:T(8,128)(2,1)S(1)} %slice.40), channel_id=1, source_target_pairs={{0,3},{1,0},{2,1},{3,2},{4,7},{5,4},{6,5},{7,6},{8,11},{9,8},{10,9... | collective-permute-start | bytes 196616 | tf_op jit(solution)/shard_map/ppermute | solution.py:30
  241.8 6.2 %collective-permute-start.5 = (bf16[256,128]{1,0:T(8,128)(2,1)S(1)}, bf16[256,128]{1,0:T(8,128)(2,1)S(1)}, u32[]{:S(2)}, u32[]{:S(2)}) collective-permute-start(bf16[256,128]{1,0:T(8,128)(2,1)S(1)} %slice.40), channel_id=1, source_target_pairs={{0,2},{1,3},{2,0},{3,1},{4,6},{5,7},{6,4},{7,5},{8,10},{9,11},{10,... | collective-permute-start | bytes 196616 | tf_op jit(solution)/shard_map/ppermute | solution.py:30
  242.7 6.0 %collective-permute-start.6 = (bf16[256,128]{1,0:T(8,128)(2,1)S(1)}, bf16[256,128]{1,0:T(8,128)(2,1)S(1)}, u32[]{:S(2)}, u32[]{:S(2)}) collective-permute-start(bf16[256,128]{1,0:T(8,128)(2,1)S(1)} %slice.40), channel_id=1, source_target_pairs={{0,1},{1,2},{2,3},{3,0},{4,5},{5,6},{6,7},{7,4},{8,9},{9,10},{10,1... | collective-permute-start | bytes 196616 | tf_op jit(solution)/shard_map/ppermute | solution.py:30
  246.1 4.0 %copy-start.3 = (f32[2,128,32]{2,1,0:T(8,128)}, f32[2,128,32]{2,1,0:T(8,128)S(1)}, u32[]{:S(2)}) copy-start(f32[2,128,32]{2,1,0:T(8,128)S(1)} %reduce_window_sum.11.decay) | copy-start | bytes 98308
Sparse Core Ops, SparseCore 0:
  11.4 45.8 all-gather.4
  59.1 168.8 all-gather.6
